TPU v7x, 32 devices: a whole 2x2x4 slice. The times are simulated.
32 devices in a mesh: depth: 4 (over x, core), plane: 8 (over z, y).
Axes of the slice: x: 2, y: 2, z: 4, core: 2. Of those that a mesh axis runs over, the one named last changes fastest.
Arguments:
- magnet: float32 [3, 32, 32, 1024], P(None, 'depth', 'plane'), may hold values from -1 to 1, as said below
- mask: int32 [32, 1024], P('plane'), may hold values 0 or 1
- materials: int32 [32], P('depth'), may hold values from 0 to 3
- exchange_strength: float32 [4], replicated, may hold values from 0.5 to 2
- anisotropy: float32 [4], replicated, may hold values from 0.5 to 3
- damping: float32 [4], replicated, may hold values from 0.05 to 0.6
- source_strength: float32 [4], replicated, may hold values from 0.3 to 1.5
- thermal_strength: float32 [4], replicated, may hold values from 0.5 to 2
- pivots: float32 [32, 3, 3], replicated, may hold values from -1 to 1, as said below
- lower: float32 [32, 3, 3], replicated, may hold values from -1 to 1, as said below
- upper: float32 [32, 3, 3], replicated, may hold values from -1 to 1, as said below
- noise_stream: int32 [1], replicated, may hold values from 0 to 999999
- counter: int32 [1], replicated, may hold values from 0 to 99999
Outputs:
- magnet_next: float32 [3, 32, 32, 1024], P(None, 'depth', 'plane')
- accumulation: float32 [3, 32, 32, 1024], P(None, 'depth', 'plane')
Inputs may be any that keep to these rules, and one draw needn't show every extreme that they name: `magnet`: unit vectors. `pivots`: each block has spectral norm below 0.98. `lower`: each block has spectral norm below 1. `upper`: each block has spectral norm below 1.
All inputs are finite; a program needn't handle non-finite values. No bound on the sum of `mask` on one device may be relied on, other than what follows from the above.
Results may differ from a plain program's by a relative error of at most 0.000073.
Values sent between devices are 32-bit elements; how exact they have to be, the bound alone decides.
No kernel may reach another device: no remote copies, remote signals or barrier semaphores. Data moves between devices by JAX's collectives and lax.ppermute only.
A program may use at most 128 MiB of HBM per device.

v0:
```python
import jax
import jax.numpy as jnp
from jax import lax
from jax.sharding import PartitionSpec as P


def padded(block, sides, width, periodic):
    for axis, dim in sides:
        count = lax.axis_size(axis)
        forward = [(i, i + 1) for i in range(count - 1)]
        if periodic:
            forward.append((count - 1, 0))
        backward = [(target, source) for source, target in forward]
        low = lax.ppermute(
            lax.slice_in_dim(block, block.shape[dim] - width, None, axis=dim), axis, forward
        )
        high = lax.ppermute(lax.slice_in_dim(block, 0, width, axis=dim), axis, backward)
        block = jnp.concatenate([low, block, high], axis=dim)
    return block


def cross(a, b):
    return jnp.stack(
        [a[1] * b[2] - a[2] * b[1], a[2] * b[0] - a[0] * b[2], a[0] * b[1] - a[1] * b[0]]
    )


def apply_block(block, vec):
    return jnp.stack(
        [
            block[row, 0] * vec[0] + block[row, 1] * vec[1] + block[row, 2] * vec[2]
            for row in range(3)
        ]
    )


def forward_sweep(source, pivots, lower, initial):
    previous = initial
    values = []
    for layer_pos in range(source.shape[1]):
        previous = apply_block(
            pivots[layer_pos], source[:, layer_pos] - apply_block(lower[layer_pos], previous)
        )
        values.append(previous)
    return values


def backward_sweep(values, upper, initial):
    after = initial
    solved = [None] * len(values)
    for layer_pos in range(len(values) - 1, -1, -1):
        after = values[layer_pos] - apply_block(upper[layer_pos], after)
        solved[layer_pos] = after
    return solved


def solve_columns(source, pivots, lower, upper):
    zero_state = jnp.zeros_like(source[:, 0])
    values = forward_sweep(source, pivots, lower, zero_state)
    return jnp.stack(backward_sweep(values, upper, zero_state), axis=1)


def hash_uniform(index, stream, counter):
    mixed = index * 739982445 + stream * 695872825 + counter * 1597334677
    mixed = mixed ^ lax.shift_right_logical(mixed, jnp.int32(16))
    mixed = mixed * 739982445
    mixed = mixed ^ lax.shift_right_logical(mixed, jnp.int32(15))
    mixed = mixed * 695872825
    mixed = mixed ^ lax.shift_right_logical(mixed, jnp.int32(16))
    return (mixed & 65535).astype(jnp.float32) / 32767.5 - 1.0


def layer_values(materials, table):
    onehot = (materials[:, None] == jnp.arange(table.shape[0], dtype=jnp.int32)[None, :]).astype(
        jnp.float32
    )
    return jnp.sum(onehot * table[None, :], axis=1)[None, :, None, None]


def normalize(vec):
    return vec / jnp.sqrt(jnp.sum(vec * vec, axis=0, keepdims=True))


def spin_solve(source, pivots, lower, upper):
    columns = lax.all_to_all(source, "depth", split_axis=3, concat_axis=1, tiled=True)
    solved = solve_columns(columns, pivots, lower, upper)
    return lax.all_to_all(solved, "depth", split_axis=1, concat_axis=3, tiled=True)


def local(
    magnet,
    mask,
    materials,
    exchange_strength,
    anisotropy,
    damping,
    source_strength,
    thermal_strength,
    pivots,
    lower,
    upper,
    noise_stream,
    counter,
):
    depth_local = magnet.shape[1]
    row_local = magnet.shape[2]
    width_y = magnet.shape[3]
    total_layers = depth_local * lax.axis_size("depth")
    total_rows = row_local * lax.axis_size("plane")
    maskf = mask.astype(jnp.float32)[None, None]
    stiff = layer_values(materials, exchange_strength)
    aniso = layer_values(materials, anisotropy)
    alpha = layer_values(materials, damping)
    beta = layer_values(materials, source_strength)
    theta = layer_values(materials, thermal_strength)
    comp = jnp.arange(3, dtype=jnp.int32)[:, None, None, None]
    layer = (lax.axis_index("depth") * depth_local + jnp.arange(depth_local, dtype=jnp.int32))[
        None, :, None, None
    ]
    xrow = (lax.axis_index("plane") * row_local + jnp.arange(row_local, dtype=jnp.int32))[
        None, None, :, None
    ]
    ycol = jnp.arange(width_y, dtype=jnp.int32)[None, None, None, :]
    index = ((comp * total_layers + layer) * total_rows + xrow) * width_y + ycol
    noise = theta * hash_uniform(index, noise_stream[0], counter[0])
    axis_z = jnp.array([0.0, 0.0, 1.0], dtype=jnp.float32)[:, None, None, None]

    def rate(field):
        masked = field * maskf
        wide = padded(masked, (("plane", 2),), 2, True)
        near = (
            wide[:, :, 3 : row_local + 3]
            + wide[:, :, 1 : row_local + 1]
            + jnp.roll(masked, 1, 3)
            + jnp.roll(masked, -1, 3)
        )
        far = (
            wide[:, :, 4 : row_local + 4]
            + wide[:, :, 0:row_local]
            + jnp.roll(masked, 2, 3)
            + jnp.roll(masked, -2, 3)
        )
        planar = 4.0 / 3.0 * near - 1.0 / 12.0 * far
        stacked = padded(masked, (("depth", 1),), 1, False)
        vertical = stacked[:, 2:] + stacked[:, :-2]
        accum = spin_solve(beta * field, pivots, lower, upper)
        heff = stiff * (planar + 0.5 * vertical) + aniso * field * axis_z + noise + 0.5 * accum
        torque = cross(field, heff)
        change = -(torque + alpha * cross(field, torque)) / (1.0 + alpha * alpha) * maskf
        return (change, accum)

    first, _ = rate(magnet)
    middle = normalize(magnet + 0.03 * first)
    second, accum = rate(middle)
    magnet_next = normalize(magnet + 0.015 * (first + second))
    return (magnet_next, accum)


def solution(mesh):
    placed = (
        P(None, "depth", "plane", None),
        P("plane", None),
        P("depth"),
        P(),
        P(),
        P(),
        P(),
        P(),
        P(),
        P(),
        P(),
        P(),
        P(),
    )
    return jax.shard_map(
        local,
        mesh=mesh,
        in_specs=placed,
        out_specs=(P(None, "depth", "plane", None), P(None, "depth", "plane", None)),
        check_vma=False,
    )
```

profile of v0, /device:TPU:0, one launch (start us, length us, event | category | flops | bytes accessed | tf_op | source)
XLA Modules:
  0.0 1246.1 jit_solution(5173523018922406698)
XLA Ops:
  8.7 9.2 reshape.5395
  86.8 10.3 reshape.5396
  102.6 7.6 multiply_add_fusion.555
  114.1 7.7 multiply_add_fusion.549
  136.6 7.5 multiply_add_fusion.537
  147.8 7.8 multiply_add_fusion.531
  171.0 7.8 multiply_add_fusion.519
  182.5 7.5 multiply_add_fusion.513
  193.7 7.7 multiply_add_fusion.507
  227.3 7.6 multiply_add_fusion.489
  238.6 7.6 multiply_add_fusion.483
  249.9 7.6 multiply_add_fusion.477
  261.3 7.6 multiply_add_fusion.471
  306.1 7.6 multiply_add_fusion.447
  340.0 7.6 multiply_add_fusion.429
  395.8 7.5 multiply_add_fusion.399
  652.2 9.2 reshape.5397
  675.9 10.3 reshape.5398
  692.5 7.6 multiply_add_fusion.276
  703.9 7.7 multiply_add_fusion.270
  726.5 7.5 multiply_add_fusion.258
  737.7 7.8 multiply_add_fusion.252
  760.8 7.8 multiply_add_fusion.240
  772.4 7.5 multiply_add_fusion.234
  783.6 7.7 multiply_add_fusion.228
  817.1 7.6 multiply_add_fusion.210
  828.4 7.6 multiply_add_fusion.204
  839.7 7.6 multiply_add_fusion.198
  851.1 7.6 multiply_add_fusion.192
  895.9 7.6 multiply_add_fusion.168
  929.8 7.6 multiply_add_fusion.150
  985.6 7.5 multiply_add_fusion.120
  (514 shorter events, 977.4 us)
Async XLA Ops:
  2.7 1.3 copy-start.6
  2.8 633.7 %copy-start.9 = (f32[8]{0:T(128)}, f32[8]{0:T(128)S(1)}, u32[]{:S(2)}) copy-start(f32[8]{0:T(128)S(1)} %get-tuple-element.104) | copy-start | bytes 100
  4.0 30.3 %copy-start.1 = (f32[32,3,3]{0,2,1:T(4,128)S(1)}, f32[32,3,3]{0,2,1:T(4,128)}, u32[]{:S(2)}) copy-start(f32[32,3,3]{0,2,1:T(4,128)} %param.23) | copy-start | bytes 3460
  4.0 30.8 %copy-start.2 = (f32[32,3,3]{0,2,1:T(4,128)S(1)}, f32[32,3,3]{0,2,1:T(4,128)}, u32[]{:S(2)}) copy-start(f32[32,3,3]{0,2,1:T(4,128)} %param.22) | copy-start | bytes 3460
  4.0 31.2 %copy-start.3 = (f32[32,3,3]{0,2,1:T(4,128)S(1)}, f32[32,3,3]{0,2,1:T(4,128)}, u32[]{:S(2)}) copy-start(f32[32,3,3]{0,2,1:T(4,128)} %param.24) | copy-start | bytes 3460
  17.9 66.6 %all-to-all-start = ((f32[4,1,24576]{2,1,0:T(1,128)}), f32[4,1,24576]{2,1,0:T(1,128)S(1)}, u32[]{:S(2)}, u32[]{:S(2)}) async-start(f32[4,1,24576]{2,1,0:T(1,128)} %reshape.5395), calls=%async_computation | async-start | bytes 786432 | tf_op jit(solution)/shard_map/all_to_all | solution.py:85
  22.9 621.1 %collective-permute-start = (f32[3,8,2,1024]{3,1,2,0:T(8,128)}, f32[3,8,2,1024]{3,1,2,0:T(8,128)S(1)}, u32[]{:S(2)}, u32[]{:S(2)}) collective-permute-start(f32[3,8,2,1024]{3,1,2,0:T(8,128)} %get-tuple-element.427), channel_id=1, source_target_pairs={{1,0},{2,1},{3,2},{4,3},{5,4},{6,5},{7,6},{0,7},{9,8},{10,9},{11,1... | collective-permute-start | bytes 589832 | tf_op jit(solution)/shard_map/ppermute | solution.py:17
  28.1 615.8 %collective-permute-start.1 = (f32[3,8,2,1024]{3,1,2,0:T(8,128)}, f32[3,8,2,1024]{3,1,2,0:T(8,128)}, u32[]{:S(2)}, u32[]{:S(2)}) collective-permute-start(f32[3,8,2,1024]{3,1,2,0:T(8,128)} %get-tuple-element.428), channel_id=1, source_target_pairs={{0,1},{1,2},{2,3},{3,4},{4,5},{5,6},{6,7},{7,0},{8,9},{9,10},{10,1... | collective-permute-start | bytes 589832 | tf_op jit(solution)/shard_map/ppermute | solution.py:14
  28.8 615.1 %collective-permute-start.2 = (f32[3,1,4,1024]{3,1,2,0:T(1,128)}, f32[3,1,4,1024]{3,1,2,0:T(1,128)}, u32[]{:S(2)}, u32[]{:S(2)}) collective-permute-start(f32[3,1,4,1024]{3,1,2,0:T(1,128)} %get-tuple-element.425), channel_id=1, source_target_pairs={{8,0},{16,8},{24,16},{9,1},{17,9},{25,17},{10,2},{18,10},{26,18},{... | collective-permute-start | bytes 147464 | tf_op jit(solution)/shard_map/ppermute | solution.py:17
  30.1 613.8 %collective-permute-start.3 = (f32[3,1,4,1024]{3,1,2,0:T(1,128)}, f32[3,1,4,1024]{3,1,2,0:T(1,128)}, u32[]{:S(2)}, u32[]{:S(2)}) collective-permute-start(f32[3,1,4,1024]{3,1,2,0:T(1,128)} %get-tuple-element.426), channel_id=1, source_target_pairs={{0,8},{8,16},{16,24},{1,9},{9,17},{17,25},{2,10},{10,18},{18,26},{... | collective-permute-start | bytes 147464 | tf_op jit(solution)/shard_map/ppermute | solution.py:14
  84.2 18.3 %copy-start.8 = (f32[3]{0:T(128)}, f32[3]{0:T(128)S(1)}, u32[]{:S(2)}) copy-start(f32[3]{0:T(128)S(1)} %maximum_maximum_fusion.1) | copy-start | bytes 40
  84.3 547.8 %copy-start.4 = (f32[3]{0:T(128)}, f32[3]{0:T(128)S(1)}, u32[]{:S(2)}) copy-start(f32[3]{0:T(128)S(1)} %maximum_maximum_fusion) | copy-start | bytes 40
  216.2 427.8 %copy-start = (f32[3,8,4,1024]{3,2,1,0:T(4,128)S(1)}, f32[3,8,4,1024]{3,2,1,0:T(4,128)}, u32[]{:S(2)}) copy-start(f32[3,8,4,1024]{3,2,1,0:T(4,128)} %param.14) | copy-start | bytes 1179652
  633.0 10.9 all-to-all-start.1
  643.9 2.1 copy-start.10
  643.9 2.1 copy-start.12
  643.9 2.5 copy-start.7
  661.4 11.8 all-to-all-start.2
  691.5 531.1 %copy-start.5 = (f32[3]{0:T(128)S(1)}, f32[3]{0:T(128)}, u32[]{:S(2)}) copy-start(f32[3]{0:T(128)} %copy-done.4) | copy-start | bytes 40
  1223.5 14.5 %all-to-all-start.3 = ((f32[3,32,4,256]{3,2,0,1:T(4,128)}), f32[3,32,4,256]{3,2,0,1:T(4,128)S(1)}, u32[]{:S(2)}, u32[]{:S(2)}) async-start(f32[3,32,4,256]{3,2,0,1:T(4,128)} %copy.319), calls=%async_computation.3 | async-start | bytes 786432 | tf_op jit(solution)/shard_map/all_to_all | solution.py:87
  1227.6 11.5 collective-permute-start.4
  1232.3 10.0 collective-permute-start.5
  1232.3 6.7 collective-permute-start.6
  1233.6 5.4 collective-permute-start.7
  1238.0 6.4 copy-start.11
  1238.0 6.4 copy-start.13
where the time goes:
time: 1260 us; the launch traced here: 1250 us
  other arithmetic  1070 us (85%)
  local copies, waits for them, and re-layouts  106 us (8%)
  starting transfers between devices  35.8 us (3%)
  between operations  16.4 us (1%)
  waiting for transfers between devices  15.3 us (1%)
    add x186, other arithmetic, apply_block(): block[row, 0] * vec[0] + block[row, 1] * vec[1] + block[row, 2] * vec[2]  1040 us
    unnamed x34, local copies, waits for them, and re-layouts  41 us
    slice x49, local copies, waits for them, and re-layouts, apply_block(): block[row, 0] * vec[0] + block[row, 1] * vec[1] + block[row, 2] * vec[2]  34.8 us
  transfers between devices with their start and end apart: 12, of which 3 were waited for; matrix products, arithmetic and copies ran while one was open for 47% of the time, Pallas kernels for 0%

commit v1 on v0

v1 whole, which is shorter than its diff:
```python
import functools

import jax
import jax.numpy as jnp
from jax import lax
from jax.experimental import pallas as pl
from jax.experimental.pallas import tpu as pltpu
from jax.sharding import PartitionSpec as P

LANES = 128
NEAR = 4.0 / 3.0
FAR = -1.0 / 12.0
HALO = 2
F32 = jnp.float32


def wrapped(value):
    value &= 0xFFFFFFFF
    return value - (1 << 32) if value >= (1 << 31) else value


HASH_A = wrapped(739982445)
HASH_B = wrapped(695872825)
HASH_C = wrapped(1597334677)


class Dims:
    def __init__(self, layers, rows, width, depth, plane):
        self.layers = layers
        self.rows = rows
        self.width = width
        self.chunks = width // LANES
        self.depth = depth
        self.plane = plane
        self.tile = (self.chunks, LANES)

    def field(self):
        return (3, self.layers, self.rows) + self.tile


def shape(*dims):
    return jax.ShapeDtypeStruct(dims, F32)


def vmem():
    return pl.BlockSpec(memory_space=pltpu.VMEM)


def smem():
    return pl.BlockSpec(memory_space=pltpu.SMEM)


def cells(dims, comp, layer, row):
    base = (comp * dims.layers + layer) * (dims.chunks * dims.rows) + row
    return pl.ds(base, dims.chunks, stride=dims.rows)


def mask_tile(dims, mask_ref, row):
    return mask_ref[pl.ds(row, dims.chunks, stride=dims.rows), :].astype(F32)


def matvec(get, vec):
    return [get(i, 0) * vec[0] + get(i, 1) * vec[1] + get(i, 2) * vec[2] for i in range(3)]


def add(a, b):
    return [x + y for x, y in zip(a, b)]


def cross(a, b):
    return [
        a[1] * b[2] - a[2] * b[1],
        a[2] * b[0] - a[0] * b[2],
        a[0] * b[1] - a[1] * b[0],
    ]


def unit(vec):
    scale = lax.rsqrt(vec[0] * vec[0] + vec[1] * vec[1] + vec[2] * vec[2])
    return [v * scale for v in vec]


def edges_kernel(dims, magnet, mask, low, high):
    for r in range(HALO):
        top = dims.rows - HALO + r
        mask_low = mask_tile(dims, mask, r)
        mask_high = mask_tile(dims, mask, top)
        for c in range(3):
            for l in range(dims.layers):
                low[c, l, r] = magnet[cells(dims, c, l, r), :] * mask_low
                high[c, l, r] = magnet[cells(dims, c, l, top), :] * mask_high


def sweep_kernel(dims, natural, field, mask, materials, source, pivots, lower, upper, *refs):
    messages, local = refs[: dims.depth - 1], refs[dims.depth - 1]
    group = lax.axis_index("depth")

    def load(c, l, r):
        if natural:
            return field[cells(dims, c, l, r), :]
        return field[c, l, r]

    def block(ref, layer):
        at = group * dims.layers + layer
        return lambda i, j: ref[at, i, j]

    rows = range(dims.rows)

    def forward(l, prev):
        beta = source[materials[l]]
        out = []
        for r in rows:
            f = [beta * load(c, l, r) for c in range(3)]
            low = matvec(block(lower, l), prev[r])
            y = matvec(block(pivots, l), [a - b for a, b in zip(f, low)])
            for c in range(3):
                local[c, l, r] = y[c]
            out.append(y)
        return out

    def backward(k, after):
        l = dims.layers - 1 - k
        out = []
        for r in rows:
            up = matvec(block(upper, l), after[r])
            s = [local[c, l, r] - up[c] for c in range(3)]
            for c in range(3):
                local[c, l, r] = s[c]
            out.append(s)
        return out

    zero = [[jnp.zeros(dims.tile, F32)] * 3 for _ in rows]
    last = lax.fori_loop(0, dims.layers, forward, zero)
    first = lax.fori_loop(0, dims.layers, backward, zero)
    for k, message in enumerate(messages, 1):
        for r in rows:
            for c in range(3):
                message[c, r] = last[r][c]
                message[3 + c, r] = first[r][c]
        at = 6
        for take, l in ((k == 1, dims.layers - 1), (k == dims.depth - 1, 0)):
            if take:
                for r in rows:
                    mask_row = mask_tile(dims, mask, r)
                    for c in range(3):
                        message[at + c, r] = load(c, l, r) * mask_row
                at += 3


def response_kernel(dims, pivots, lower, upper, out):
    total = dims.layers * dims.depth
    lane = lax.broadcasted_iota(jnp.int32, (1, LANES), 1)
    for g in range(dims.depth):
        y = [(lane == c).astype(F32) for c in range(3)]
        s = [(lane == 3 + c).astype(F32) for c in range(3)]

        def forward(k, y):
            l = g * dims.layers + k
            low = matvec(lambda i, j: lower[l, i, j], y)
            y = matvec(lambda i, j: pivots[l, i, j], [-a for a in low])
            for c in range(3):
                out[l, pl.ds(c, 1)] = y[c]
            return y

        def backward(k, s):
            l = (g + 1) * dims.layers - 1 - k
            up = matvec(lambda i, j: upper[l, i, j], s)
            s = [out[l, pl.ds(c, 1)] - up[c] for c in range(3)]
            for c in range(3):
                out[l, pl.ds(c, 1)] = s[c]
            return s

        y = lax.fori_loop(0, dims.layers, forward, y)
        for c in range(3):
            out[total + g, pl.ds(c, 1)] = y[c]
        lax.fori_loop(0, dims.layers, backward, s)


def shifted_sum(dims, w, lane):
    after = pltpu.roll(w, dims.chunks - 1, 0)
    before = pltpu.roll(w, 1, 0)
    near = pltpu.roll(jnp.where(lane < 1, after, w), LANES - 1, 1)
    near += pltpu.roll(jnp.where(lane >= LANES - 1, before, w), 1, 1)
    far = pltpu.roll(jnp.where(lane < 2, after, w), LANES - 2, 1)
    far += pltpu.roll(jnp.where(lane >= LANES - 2, before, w), 2, 1)
    return NEAR * near + FAR * far


def hash_uniform(mixed):
    mixed = mixed ^ lax.shift_right_logical(mixed, jnp.int32(16))
    mixed = mixed * HASH_A
    mixed = mixed ^ lax.shift_right_logical(mixed, jnp.int32(15))
    mixed = mixed * HASH_B
    mixed = mixed ^ lax.shift_right_logical(mixed, jnp.int32(16))
    return (mixed & 65535).astype(F32) * (1.0 / 32767.5) - 1.0


def local_kernel(dims, first, field, mask, local, materials, stiffness, anisotropy, *refs):
    if first:
        thermal, stream, counter, heff, noise, masked = refs
        group = lax.axis_index("depth")
        block = lax.axis_index("plane")
        within = (
            lax.broadcasted_iota(jnp.int32, dims.tile, 0) * LANES
            + lax.broadcasted_iota(jnp.int32, dims.tile, 1)
        ) * HASH_A
        seed = stream[0] * HASH_B + counter[0] * HASH_C
    else:
        noise, heff, masked = refs
    lane = lax.broadcasted_iota(jnp.int32, dims.tile, 1)
    rows = range(dims.rows)

    def load(c, l, r):
        if first:
            return field[cells(dims, c, l, r), :]
        return field[c, l, r]

    for c in range(3):
        for r in rows:
            masked[c, 0, r] = jnp.zeros(dims.tile, F32)
            masked[c, dims.layers + 1, r] = jnp.zeros(dims.tile, F32)

    def fill(l, carry):
        for r in rows:
            mask_row = mask_tile(dims, mask, r)
            for c in range(3):
                masked[c, l + 1, r] = load(c, l, r) * mask_row
        return carry

    lax.fori_loop(0, dims.layers, fill, 0)

    def body(l, carry):
        material = materials[l]
        stiff = stiffness[material]
        aniso = anisotropy[material]
        for c in range(3):
            w = [masked[c, l + 1, r] for r in rows]
            for r in rows:
                total = shifted_sum(dims, w[r], lane)
                for step, weight in ((1, NEAR), (2, FAR)):
                    inside = [w[q] for q in (r - step, r + step) if 0 <= q < dims.rows]
                    if inside:
                        total += weight * functools.reduce(jnp.add, inside)
                total += 0.5 * (masked[c, l, r] + masked[c, l + 2, r])
                h = stiff * total + 0.5 * local[c, l, r]
                if c == 2:
                    h += aniso * load(c, l, r)
                if first:
                    layer = group * dims.layers + l
                    line = (c * (dims.depth * dims.layers) + layer) * (
                        dims.plane * dims.rows
                    ) + (block * dims.rows + r)
                    start = line * dims.width * HASH_A + seed
                    value = thermal[material] * hash_uniform(within + start)
                    noise[c, l, r] = value
                    h += value
                else:
                    h += noise[c, l, r]
                heff[c, l, r] = h
        return carry

    lax.fori_loop(0, dims.layers, body, 0)


def finish_kernel(
    dims,
    first,
    field,
    mask,
    heff,
    own,
    response,
    materials,
    stiffness,
    damping,
    before,
    after,
    *refs,
):
    others, refs = refs[: dims.depth - 1], refs[dims.depth - 1 :]
    if first:
        middle, base, low, high, bound, edge = refs
    else:
        base, local, result, accum, bound, edge = refs
    group = lax.axis_index("depth")
    total = dims.layers * dims.depth
    rows = range(dims.rows)

    def load(c, l, r):
        if first:
            return field[cells(dims, c, l, r), :]
        return field[c, l, r]

    def carry_y(g):
        return lambda i, j: response[total + g, i, j]

    def first_y(g):
        return lambda i, j: response[g * dims.layers, i, j]

    def first_s(g):
        return lambda i, j: response[g * dims.layers, i, 3 + j]

    for g in range(dims.depth):

        @pl.when(group == g)
        def _():
            def message(h):
                return own if h == g else others[(g - h) % dims.depth - 1]

            for r in rows:
                end = [
                    [message(h)[c, r] for c in range(3)] for h in range(dims.depth - 1)
                ]
                ys = {0: None}
                for h in range(1, dims.depth):
                    ys[h] = end[h - 1]
                    if ys[h - 1] is not None:
                        ys[h] = add(ys[h], matvec(carry_y(h - 1), ys[h - 1]))
                s = None
                for h in range(dims.depth - 1, g, -1):
                    value = [message(h)[3 + c, r] for c in range(3)]
                    value = add(value, matvec(first_y(h), ys[h]))
                    if s is not None:
                        value = add(value, matvec(first_s(h), s))
                    s = value
                for c in range(3):
                    zero = jnp.zeros(dims.tile, F32)
                    bound[c, r] = zero if ys[g] is None else ys[g][c]
                    bound[3 + c, r] = zero if s is None else s[c]
                    edge[c, r] = zero if g == 0 else others[0][6 + c, r]
                    at = 9 if dims.depth == 2 else 6
                    top = others[dims.depth - 2]
                    edge[3 + c, r] = zero if g == dims.depth - 1 else top[at + c, r]

    def body(l, carry):
        material = materials[l]
        stiff = stiffness[material]
        alpha = damping[material]
        layer = group * dims.layers + l
        scale = 1.0 / (1.0 + jnp.full(dims.tile, alpha, F32) * alpha)
        down = jnp.where(l == 0, 0.5 * stiff, 0.0)
        up = jnp.where(l == dims.layers - 1, 0.5 * stiff, 0.0)
        for r in rows:
            v = [load(c, l, r) for c in range(3)]
            h = [heff[c, l, r] for c in range(3)]
            y = [bound[c, r] for c in range(3)]
            s = [bound[3 + c, r] for c in range(3)]
            fix = add(
                matvec(lambda i, j: response[layer, i, j], y),
                matvec(lambda i, j: response[layer, i, 3 + j], s),
            )
            for c in range(3):
                for step, weight in ((1, NEAR), (2, FAR)):
                    if r - step < 0:
                        h[c] += (stiff * weight) * before[c, l, r - step + HALO]
                    if r + step >= dims.rows:
                        h[c] += (stiff * weight) * after[c, l, r + step - dims.rows]
                h[c] += down * edge[c, r] + up * edge[3 + c, r] + 0.5 * fix[c]
            torque = cross(v, h)
            twice = cross(v, torque)
            mask_row = mask_tile(dims, mask, r)
            gain = scale * mask_row
            rate = [(torque[c] + alpha * twice[c]) * gain for c in range(3)]
            if first:
                m1 = unit([v[c] - 0.03 * rate[c] for c in range(3)])
                for c in range(3):
                    middle[c, l, r] = m1[c]
                    base[c, l, r] = v[c] - 0.015 * rate[c]
                    if r < HALO:
                        low[c, l, r] = m1[c] * mask_row
                    if r >= dims.rows - HALO:
                        high[c, l, r - dims.rows + HALO] = m1[c] * mask_row
            else:
                new = unit([base[c, l, r] - 0.015 * rate[c] for c in range(3)])
                for c in range(3):
                    result[cells(dims, c, l, r), :] = new[c]
                    accum[cells(dims, c, l, r), :] = local[c, l, r] + fix[c]
        return carry

    lax.fori_loop(0, dims.layers, body, 0)


def call(kernel, outs, ins, args, scratch=(), flops=1000000):
    return pl.pallas_call(
        kernel,
        out_shape=outs,
        in_specs=[smem() if i else vmem() for i in ins],
        out_specs=[vmem()] * len(outs),
        scratch_shapes=scratch,
        cost_estimate=pl.CostEstimate(flops=flops, bytes_accessed=1000000, transcendentals=0),
    )(*args)


def ring(count, step):
    return [(i, (i + step) % count) for i in range(count)]


def local(
    magnet,
    mask,
    materials,
    exchange_strength,
    anisotropy,
    damping,
    source_strength,
    thermal_strength,
    pivots,
    lower,
    upper,
    noise_stream,
    counter,
):
    dims = Dims(
        magnet.shape[1],
        magnet.shape[2],
        magnet.shape[3],
        lax.axis_size("depth"),
        lax.axis_size("plane"),
    )
    lines = (3, dims.layers, dims.rows, dims.chunks, LANES)
    view = magnet.reshape(lines).transpose(0, 1, 3, 2, 4).reshape(-1, LANES)
    mask_view = mask.reshape(lines[2:]).transpose(1, 0, 2).reshape(-1, LANES)
    halo = shape(3, dims.layers, HALO, *dims.tile)
    field = shape(*dims.field())
    planes = 3 * dims.rows

    def bind(kernel, *static):
        return functools.partial(kernel, dims, *static)

    def swap_plane(low, high):
        after = lax.ppermute(low, "plane", ring(dims.plane, -1))
        before = lax.ppermute(high, "plane", ring(dims.plane, 1))
        return before, after

    messages = []
    for k in range(1, dims.depth):
        parts = 6 + 3 * (k == 1) + 3 * (k == dims.depth - 1)
        messages.append(shape(parts, dims.rows, *dims.tile))

    def swap_depth(sent):
        return [
            lax.ppermute(message, "depth", ring(dims.depth, k)) for k, message in enumerate(sent, 1)
        ]

    def sweep(natural, values):
        out = call(
            bind(sweep_kernel, natural),
            messages + [field],
            [0, 0, 1, 1, 1, 1, 1],
            (values, mask_view, materials, source_strength, pivots, lower, upper),
        )
        return out[:-1], out[-1]

    padded = pltpu.VMEM((3, dims.layers + 2, dims.rows) + dims.tile, F32)
    bounds = [pltpu.VMEM((6, dims.rows) + dims.tile, F32)] * 2

    low, high = call(bind(edges_kernel), [halo, halo], [0, 0], (view, mask_view))
    before, after = swap_plane(low, high)
    sent, solved = sweep(True, view)
    others = swap_depth(sent)
    (response,) = call(
        bind(response_kernel),
        [shape(dims.depth * (dims.layers + 1), 3, LANES)],
        [1, 1, 1],
        (pivots, lower, upper),
    )
    heff, noise = call(
        bind(local_kernel, True),
        [field, field],
        [0, 0, 0, 1, 1, 1, 1, 1, 1],
        (
            view,
            mask_view,
            solved,
            materials,
            exchange_strength,
            anisotropy,
            thermal_strength,
            noise_stream,
            counter,
        ),
        [padded],
    )
    kinds = [0, 0, 0, 0, 1, 1, 1, 1] + [0] * (1 + dims.depth)
    middle, base, low, high = call(
        bind(finish_kernel, True),
        [field, field, halo, halo],
        kinds,
        (
            view,
            mask_view,
            heff,
            sent[0],
            response,
            materials,
            exchange_strength,
            damping,
            before,
            after,
            *others,
        ),
        bounds,
    )
    before, after = swap_plane(low, high)
    sent, solved = sweep(False, middle)
    others = swap_depth(sent)
    (heff,) = call(
        bind(local_kernel, False),
        [field],
        [0, 0, 0, 1, 1, 1, 0],
        (middle, mask_view, solved, materials, exchange_strength, anisotropy, noise),
        [padded],
    )
    lined = shape(*view.shape)
    result, accum = call(
        bind(finish_kernel, False),
        [lined, lined],
        kinds + [0, 0],
        (
            middle,
            mask_view,
            heff,
            sent[0],
            response,
            materials,
            exchange_strength,
            damping,
            before,
            after,
            *others,
            base,
            solved,
        ),
        bounds,
    )

    def whole(lines_view):
        cut = lines_view.reshape(3, dims.layers, dims.chunks, dims.rows, LANES)
        return cut.transpose(0, 1, 3, 2, 4).reshape(magnet.shape)

    return whole(result), whole(accum)


def solution(mesh):
    placed = (
        P(None, "depth", "plane", None),
        P("plane", None),
        P("depth"),
    ) + (P(),) * 10
    return jax.shard_map(
        local,
        mesh=mesh,
        in_specs=placed,
        out_specs=(P(None, "depth", "plane", None), P(None, "depth", "plane", None)),
        check_vma=False,
    )
```

time: 1260 us -> 56.6 us (0.04); the launches traced: 1250 us -> 56 us
  other arithmetic: 1070 us -> 0 us
  local copies, waits for them, and re-layouts: 106 us -> 3.79 us
  Pallas kernels: 0 us -> 32.3 us
  starting transfers between devices: 35.8 us -> 14.3 us
  between operations: 16.4 us -> 2.07 us
    add x191 -> x0, other arithmetic: 1050 us -> none  [the longest x186 1040 us: apply_block(): block[row, 0] * vec[0] + block[row, 1] * vec[1] + block[row, 2] * vec[2]]
    slice x73 -> x0, local copies, waits for them, and re-layouts: 43.4 us -> none  [the longest x49 34.8 us: apply_block(): block[row, 0] * vec[0] + block[row, 1] * vec[1] + block[row, 2] * vec[2]]
    unnamed x34 -> x29, local copies, waits for them, and re-layouts: 41 us -> 3.79 us
    pallas_call x0 -> x8, Pallas kernels: none -> 32.3 us  [call(): pl.pallas_call(kernel, out_shape=outs, in_specs=[smem() if i else vmem()...]
    all_to_all x4 -> x0, starting transfers between devices: 15.4 us -> none  [the longest x2 8.52 us: spin_solve(): lax.all_to_all(source, 'depth', split_axis=3, concat_axis=1, tiled=True)]
  transfers between devices with their start and end apart: 12 -> 10, of which waited for: 3 -> 1; matrix products, arithmetic and copies ran while one was open for 47% -> 4% of each run, Pallas kernels for 0% -> 41%
where the time goes in v1:
time: 56.6 us; the launch traced here: 56 us
  Pallas kernels  32.3 us (57%)
  starting transfers between devices  14.3 us (25%)
  local copies, waits for them, and re-layouts  3.79 us (7%)
  waiting for transfers between devices  3.52 us (6%)
  between operations  2.07 us (4%)
    pallas_call x8, Pallas kernels, call(): pl.pallas_call(kernel, out_shape=outs, in_specs=[smem() if i else vmem()...  32.3 us
    ppermute x2, starting transfers between devices, swap_plane(): after = lax.ppermute(low, 'plane', ring(dims.plane, -1))  7.76 us
    unnamed x29, local copies, waits for them, and re-layouts  3.79 us
    ppermute x6, starting transfers between devices, swap_depth(): lax.ppermute(message, 'depth', ring(dims.depth, k))  3.59 us
    ppermute x6, waiting for transfers between devices, swap_depth(): lax.ppermute(message, 'depth', ring(dims.depth, k))  3.51 us
    ppermute x2, starting transfers between devices, swap_plane(): before = lax.ppermute(high, 'plane', ring(dims.plane, 1))  2.97 us
  transfers between devices with their start and end apart: 10, of which 1 were waited for; matrix products, arithmetic and copies ran while one was open for 4% of the time, Pallas kernels for 41%

profile of v1, /device:TPU:0, one launch (start us, length us, event | category | flops | bytes accessed | tf_op | source)
XLA Modules:
  0.0 56.0 jit_solution(6525159802439563074)
XLA Ops:
  0.6 1.8 %shard_map.143 = (f32[3,8,2,8,128]{4,3,2,1,0:T(8,128)}, f32[3,8,2,8,128]{4,3,2,1,0:T(8,128)}) custom-call(f32[768,128]{1,0:T(8,128)} %bitcast.20, s32[32,128]{1,0:T(8,128)} %bitcast.24), custom_call_target="tpu_custom_call" | custom-call | flops 1000000 | bytes 1000000 | tf_op jit(solution)/shard_map/pallas_call | solution.py:384
  2.4 3.0 %collective-permute-start = (f32[3,8,2,8,128]{4,3,2,1,0:T(8,128)}, f32[3,8,2,8,128]{4,3,2,1,0:T(8,128)S(1)}, u32[]{:S(2)}, u32[]{:S(2)}) collective-permute-start(f32[3,8,2,8,128]{4,3,2,1,0:T(8,128)} %get-tuple-element.23), channel_id=1, source_target_pairs={{0,1},{1,2},{2,3},{3,4},{4,5},{5,6},{6,7},{7,0},{8,9},{9,10},{10,1... | collective-permute-start | bytes 589832 | tf_op jit(solution)/shard_map/ppermute | solution.py:432
  5.4 3.0 %collective-permute-start.1 = (f32[3,8,2,8,128]{4,3,2,1,0:T(8,128)}, f32[3,8,2,8,128]{4,3,2,1,0:T(8,128)S(1)}, u32[]{:S(2)}, u32[]{:S(2)}) collective-permute-start(f32[3,8,2,8,128]{4,3,2,1,0:T(8,128)} %get-tuple-element.24), channel_id=1, source_target_pairs={{0,7},{1,0},{2,1},{3,2},{4,3},{5,4},{6,5},{7,6},{8,15},{9,8},{10,9... | collective-permute-start | bytes 589832 | tf_op jit(solution)/shard_map/ppermute | solution.py:431
  8.5 0.7 %copy.17.pivots = f32[32,3,3]{2,1,0:T(4,128)} copy(f32[32,3,3]{0,2,1:T(4,128)S(1)} %copy-done.10) | data formatting | bytes 2304 | tf_op args[8]
  9.2 0.7 %copy.18.lower = f32[32,3,3]{2,1,0:T(4,128)} copy(f32[32,3,3]{0,2,1:T(4,128)S(1)} %copy-done.11) | data formatting | bytes 2304 | tf_op args[9]
  9.9 0.7 %copy.19.upper = f32[32,3,3]{2,1,0:T(4,128)} copy(f32[32,3,3]{0,2,1:T(4,128)S(1)} %copy-done.12) | data formatting | bytes 2304 | tf_op args[10]
  10.6 5.5 %shard_map.140 = (f32[9,4,8,128]{3,2,1,0:T(8,128)}, f32[6,4,8,128]{3,2,1,0:T(8,128)}, f32[9,4,8,128]{3,2,1,0:T(8,128)}, f32[3,8,4,8,128]{4,3,2,1,0:T(8,128)}) custom-call(f32[768,128]{1,0:T(8,128)} %bitcast.21, s32[32,128]{1,0:T(8,128)} %bitcast.25, s32[8]{0:T(128)} %materials.11, f32[4]{0:T(128)} %source.3, f32[32,3,3]{2,1,0:T(4,128)} %copy.17.pivots, ...), custom_call_target="tpu_custom_call" | custom-call | flops 1000000 | bytes 1000000 | tf_op jit(solution)/shard_map/pallas_call | solution.py:384
  16.2 0.7 %collective-permute-start.4 = (f32[9,4,8,128]{3,2,1,0:T(8,128)}, f32[9,4,8,128]{3,2,1,0:T(8,128)S(1)}, u32[]{:S(2)}, u32[]{:S(2)}) collective-permute-start(f32[9,4,8,128]{3,2,1,0:T(8,128)} %get-tuple-element.26), channel_id=1, source_target_pairs={{0,24},{8,0},{16,8},{24,16},{1,25},{9,1},{17,9},{25,17},{2,26},{10... | collective-permute-start | bytes 442376 | tf_op jit(solution)/shard_map/ppermute | solution.py:442
  16.8 0.0 collective-permute-start.2
  16.8 1.5 %collective-permute-start.3 = (f32[6,4,8,128]{3,2,1,0:T(8,128)}, f32[6,4,8,128]{3,2,1,0:T(8,128)S(1)}, u32[]{:S(2)}, u32[]{:S(2)}) collective-permute-start(f32[6,4,8,128]{3,2,1,0:T(8,128)} %get-tuple-element.25), channel_id=1, source_target_pairs={{0,16},{8,24},{16,0},{24,8},{1,17},{9,25},{17,1},{25,9},{2,18},{10... | collective-permute-start | bytes 294920 | tf_op jit(solution)/shard_map/ppermute | solution.py:442
  19.6 5.5 %shard_map.142.response = f32[36,3,128]{2,1,0:T(4,128)} custom-call(f32[32,3,3]{2,1,0:T(4,128)} %copy.17.pivots, f32[32,3,3]{2,1,0:T(4,128)} %copy.18.lower, f32[32,3,3]{2,1,0:T(4,128)} %copy.19.upper), custom_call_target="tpu_custom_call" | custom-call | flops 1000000 | bytes 1000000 | tf_op jit(solution)/shard_map/pallas_call | solution.py:384
  25.2 3.1 %shard_map.141 = (f32[3,8,4,8,128]{4,3,2,1,0:T(8,128)}, f32[3,8,4,8,128]{4,3,2,1,0:T(8,128)}) custom-call(f32[768,128]{1,0:T(8,128)} %bitcast.22, s32[32,128]{1,0:T(8,128)} %bitcast.26, f32[3,8,4,8,128]{4,3,2,1,0:T(8,128)} %get-tuple-element.20.local, s32[8]{0:T(128)} %materials.11, f32[4]{0:T(128)} %stiffness.7, f32[4]{0:T(128)} %anisotropy.3, f32[4]{0:T(128)} %refs_0_.1, ...), custom_call_target="tpu_custom_call" | custom-call | flops 1000000 | bytes 1000000 | tf_op jit(solution)/shard_map/pallas_call | solution.py:384
  28.3 0.0 copy-start
  28.3 0.5 copy-done.8
  28.8 0.1 copy-done.4
  28.9 0.0 copy-done.5
  29.0 0.1 copy-done
  29.0 0.1 copy-done.1
  29.1 4.0 %shard_map.144 = (f32[3,8,4,8,128]{4,3,2,1,0:T(8,128)}, f32[3,8,4,8,128]{4,3,2,1,0:T(8,128)}, f32[3,8,2,8,128]{4,3,2,1,0:T(8,128)}, f32[3,8,2,8,128]{4,3,2,1,0:T(8,128)}) custom-call(f32[768,128]{1,0:T(8,128)} %bitcast.23, s32[32,128]{1,0:T(8,128)} %bitcast.27, f32[3,8,4,8,128]{4,3,2,1,0:T(8,128)} %get-tuple-element.21.heff, ...), custom_call_target="tpu_custom_call" | custom-call | flops 1000000 | bytes 1000000 | tf_op jit(solution)/shard_map/pallas_call | solution.py:384
  33.1 4.7 %collective-permute-start.6 = (f32[3,8,2,8,128]{4,3,2,1,0:T(8,128)}, f32[3,8,2,8,128]{4,3,2,1,0:T(8,128)S(1)}, u32[]{:S(2)}, u32[]{:S(2)}) collective-permute-start(f32[3,8,2,8,128]{4,3,2,1,0:T(8,128)} %get-tuple-element.32), channel_id=1, source_target_pairs={{0,7},{1,0},{2,1},{3,2},{4,3},{5,4},{6,5},{7,6},{8,15},{9,8},{10,9... | collective-permute-start | bytes 589832 | tf_op jit(solution)/shard_map/ppermute | solution.py:431
  37.8 5.5 %shard_map.145 = (f32[9,4,8,128]{3,2,1,0:T(8,128)}, f32[6,4,8,128]{3,2,1,0:T(8,128)}, f32[9,4,8,128]{3,2,1,0:T(8,128)}, f32[3,8,4,8,128]{4,3,2,1,0:T(8,128)}) custom-call(f32[3,8,4,8,128]{4,3,2,1,0:T(8,128)} %get-tuple-element.27.field, s32[32,128]{1,0:T(8,128)} %bitcast.28, s32[8]{0:T(128)} %materials.11, f32[4]{0:T(128)} %source.3, ...), custom_call_target="tpu_custom_call" | custom-call | flops 1000000 | bytes 1000000 | tf_op jit(solution)/shard_map/pallas_call | solution.py:384
  43.3 0.4 collective-permute-start.9
  43.7 0.1 collective-permute-start.7
  43.8 0.9 %collective-permute-start.8 = (f32[6,4,8,128]{3,2,1,0:T(8,128)}, f32[6,4,8,128]{3,2,1,0:T(8,128)S(1)}, u32[]{:S(2)}, u32[]{:S(2)}) collective-permute-start(f32[6,4,8,128]{3,2,1,0:T(8,128)} %get-tuple-element.33), channel_id=1, source_target_pairs={{0,16},{8,24},{16,0},{24,8},{1,17},{9,25},{17,1},{25,9},{2,18},{10... | collective-permute-start | bytes 294920 | tf_op jit(solution)/shard_map/ppermute | solution.py:442
  44.8 3.1 %shard_map.146.heff = f32[3,8,4,8,128]{4,3,2,1,0:T(8,128)} custom-call(f32[3,8,4,8,128]{4,3,2,1,0:T(8,128)} %get-tuple-element.27.field, s32[32,128]{1,0:T(8,128)} %bitcast.29, f32[3,8,4,8,128]{4,3,2,1,0:T(8,128)} %get-tuple-element.28.local.refs_4_, s32[8]{0:T(128)} %materials.11, f32[4]{0:T(128)} %stiffness.7, f32[4]{0:T(128)} %anisotropy.3, ...), custom_call_target="tpu_custom_call" | custom-call | flops 1000000 | bytes 1000000 | tf_op jit(solution)/shard_map/pallas_call | solution.py:384
  47.9 3.5 %collective-permute-done.8.refs_1_ = f32[6,4,8,128]{3,2,1,0:T(8,128)S(1)} collective-permute-done((f32[6,4,8,128]{3,2,1,0:T(8,128)}, f32[6,4,8,128]{3,2,1,0:T(8,128)S(1)}, u32[]{:S(2)}, u32[]{:S(2)}) %collective-permute-start.8) | collective-permute-done | bytes 98336 | tf_op jit(solution)/shard_map/ppermute | solution.py:442
  51.4 0.6 %copy-done.9 = f32[6,4,8,128]{3,2,1,0:T(8,128)} copy-done((f32[6,4,8,128]{3,2,1,0:T(8,128)}, f32[6,4,8,128]{3,2,1,0:T(8,128)S(1)}, u32[]{:S(2)}) %copy-start.9) | copy-done | bytes 98328
  52.0 0.1 copy-done.6
  52.1 0.1 copy-done.7
  52.1 0.1 copy-done.2
  52.2 0.0 copy-done.3
  52.3 3.8 %shard_map.147 = (f32[768,128]{1,0:T(8,128)}, f32[768,128]{1,0:T(8,128)}) custom-call(f32[3,8,4,8,128]{4,3,2,1,0:T(8,128)} %get-tuple-element.27.field, s32[32,128]{1,0:T(8,128)} %bitcast.30, f32[3,8,4,8,128]{4,3,2,1,0:T(8,128)} %shard_map.146.heff, f32[9,4,8,128]{3,2,1,0:T(8,128)} %get-tuple-element.30.own, f32[36,3,128]{2,1,0:T(4,128)} %shard_map.142.response, ...), custom_call_target="tpu_custom_call" | custom-call | flops 1000000 | bytes 1000000 | tf_op jit(solution)/shard_map/pallas_call | solution.py:384
  (25 shorter events, 0.1 us)
Async XLA Ops:
  0.6 7.8 %copy-start.10 = (f32[32,3,3]{0,2,1:T(4,128)S(1)}, f32[32,3,3]{0,2,1:T(4,128)}, u32[]{:S(2)}) copy-start(f32[32,3,3]{0,2,1:T(4,128)} %param.21) | copy-start | bytes 3460
  2.4 25.8 %collective-permute-start = (f32[3,8,2,8,128]{4,3,2,1,0:T(8,128)}, f32[3,8,2,8,128]{4,3,2,1,0:T(8,128)S(1)}, u32[]{:S(2)}, u32[]{:S(2)}) collective-permute-start(f32[3,8,2,8,128]{4,3,2,1,0:T(8,128)} %get-tuple-element.23), channel_id=1, source_target_pairs={{0,1},{1,2},{2,3},{3,4},{4,5},{5,6},{6,7},{7,0},{8,9},{9,10},{10,1... | collective-permute-start | bytes 589832 | tf_op jit(solution)/shard_map/ppermute | solution.py:432
  5.4 3.8 %copy-start.11 = (f32[32,3,3]{0,2,1:T(4,128)S(1)}, f32[32,3,3]{0,2,1:T(4,128)}, u32[]{:S(2)}) copy-start(f32[32,3,3]{0,2,1:T(4,128)} %param.22) | copy-start | bytes 3460
  5.4 22.9 %collective-permute-start.1 = (f32[3,8,2,8,128]{4,3,2,1,0:T(8,128)}, f32[3,8,2,8,128]{4,3,2,1,0:T(8,128)S(1)}, u32[]{:S(2)}, u32[]{:S(2)}) collective-permute-start(f32[3,8,2,8,128]{4,3,2,1,0:T(8,128)} %get-tuple-element.24), channel_id=1, source_target_pairs={{0,7},{1,0},{2,1},{3,2},{4,3},{5,4},{6,5},{7,6},{8,15},{9,8},{10,9... | collective-permute-start | bytes 589832 | tf_op jit(solution)/shard_map/ppermute | solution.py:431
  9.2 0.7 %copy-start.12 = (f32[32,3,3]{0,2,1:T(4,128)S(1)}, f32[32,3,3]{0,2,1:T(4,128)}, u32[]{:S(2)}) copy-start(f32[32,3,3]{0,2,1:T(4,128)} %param.23) | copy-start | bytes 3460
  16.2 12.1 %collective-permute-start.4 = (f32[9,4,8,128]{3,2,1,0:T(8,128)}, f32[9,4,8,128]{3,2,1,0:T(8,128)S(1)}, u32[]{:S(2)}, u32[]{:S(2)}) collective-permute-start(f32[9,4,8,128]{3,2,1,0:T(8,128)} %get-tuple-element.26), channel_id=1, source_target_pairs={{0,24},{8,0},{16,8},{24,16},{1,25},{9,1},{17,9},{25,17},{2,26},{10... | collective-permute-start | bytes 442376 | tf_op jit(solution)/shard_map/ppermute | solution.py:442
  16.8 11.4 %collective-permute-start.2 = (f32[9,4,8,128]{3,2,1,0:T(8,128)}, f32[9,4,8,128]{3,2,1,0:T(8,128)S(1)}, u32[]{:S(2)}, u32[]{:S(2)}) collective-permute-start(f32[9,4,8,128]{3,2,1,0:T(8,128)} %get-tuple-element.22.own), channel_id=1, source_target_pairs={{0,8},{8,16},{16,24},{24,0},{1,9},{9,17},{17,25},{25,1},{2,10},{10... | collective-permute-start | bytes 442376 | tf_op jit(solution)/shard_map/ppermute | solution.py:442
  16.8 11.4 %collective-permute-start.3 = (f32[6,4,8,128]{3,2,1,0:T(8,128)}, f32[6,4,8,128]{3,2,1,0:T(8,128)S(1)}, u32[]{:S(2)}, u32[]{:S(2)}) collective-permute-start(f32[6,4,8,128]{3,2,1,0:T(8,128)} %get-tuple-element.25), channel_id=1, source_target_pairs={{0,16},{8,24},{16,0},{24,8},{1,17},{9,25},{17,1},{25,9},{2,18},{10... | collective-permute-start | bytes 294920 | tf_op jit(solution)/shard_map/ppermute | solution.py:442
  28.2 0.6 %copy-start.8 = (f32[6,4,8,128]{3,2,1,0:T(8,128)}, f32[6,4,8,128]{3,2,1,0:T(8,128)S(1)}, u32[]{:S(2)}) copy-start(f32[6,4,8,128]{3,2,1,0:T(8,128)S(1)} %collective-permute-done.3.refs_1_) | copy-start | bytes 294916
  28.2 0.7 %copy-start.4 = (f32[9,4,8,128]{3,2,1,0:T(8,128)}, f32[9,4,8,128]{3,2,1,0:T(8,128)S(1)}, u32[]{:S(2)}) copy-start(f32[9,4,8,128]{3,2,1,0:T(8,128)S(1)} %collective-permute-done.4.refs_2_) | copy-start | bytes 442372
  28.2 0.7 %copy-start.5 = (f32[9,4,8,128]{3,2,1,0:T(8,128)}, f32[9,4,8,128]{3,2,1,0:T(8,128)S(1)}, u32[]{:S(2)}) copy-start(f32[9,4,8,128]{3,2,1,0:T(8,128)S(1)} %collective-permute-done.2.refs_0_) | copy-start | bytes 442372
  28.3 0.7 %copy-start = (f32[3,8,2,8,128]{4,3,2,1,0:T(8,128)}, f32[3,8,2,8,128]{4,3,2,1,0:T(8,128)S(1)}, u32[]{:S(2)}) copy-start(f32[3,8,2,8,128]{4,3,2,1,0:T(8,128)S(1)} %collective-permute-done.before) | copy-start | bytes 589828
  28.3 0.8 %copy-start.1 = (f32[3,8,2,8,128]{4,3,2,1,0:T(8,128)}, f32[3,8,2,8,128]{4,3,2,1,0:T(8,128)S(1)}, u32[]{:S(2)}) copy-start(f32[3,8,2,8,128]{4,3,2,1,0:T(8,128)S(1)} %collective-permute-done.1.after) | copy-start | bytes 589828
  33.1 18.3 %collective-permute-start.5 = (f32[3,8,2,8,128]{4,3,2,1,0:T(8,128)}, f32[3,8,2,8,128]{4,3,2,1,0:T(8,128)S(1)}, u32[]{:S(2)}, u32[]{:S(2)}) collective-permute-start(f32[3,8,2,8,128]{4,3,2,1,0:T(8,128)} %get-tuple-element.31), channel_id=1, source_target_pairs={{0,1},{1,2},{2,3},{3,4},{4,5},{5,6},{6,7},{7,0},{8,9},{9,10},{10,1... | collective-permute-start | bytes 589832 | tf_op jit(solution)/shard_map/ppermute | solution.py:432
  33.1 18.3 %collective-permute-start.6 = (f32[3,8,2,8,128]{4,3,2,1,0:T(8,128)}, f32[3,8,2,8,128]{4,3,2,1,0:T(8,128)S(1)}, u32[]{:S(2)}, u32[]{:S(2)}) collective-permute-start(f32[3,8,2,8,128]{4,3,2,1,0:T(8,128)} %get-tuple-element.32), channel_id=1, source_target_pairs={{0,7},{1,0},{2,1},{3,2},{4,3},{5,4},{6,5},{7,6},{8,15},{9,8},{10,9... | collective-permute-start | bytes 589832 | tf_op jit(solution)/shard_map/ppermute | solution.py:431
  43.3 8.1 %collective-permute-start.9 = (f32[9,4,8,128]{3,2,1,0:T(8,128)}, f32[9,4,8,128]{3,2,1,0:T(8,128)S(1)}, u32[]{:S(2)}, u32[]{:S(2)}) collective-permute-start(f32[9,4,8,128]{3,2,1,0:T(8,128)} %get-tuple-element.34), channel_id=1, source_target_pairs={{0,24},{8,0},{16,8},{24,16},{1,25},{9,1},{17,9},{25,17},{2,26},{10... | collective-permute-start | bytes 442376 | tf_op jit(solution)/shard_map/ppermute | solution.py:442
  43.7 7.7 %collective-permute-start.7 = (f32[9,4,8,128]{3,2,1,0:T(8,128)}, f32[9,4,8,128]{3,2,1,0:T(8,128)S(1)}, u32[]{:S(2)}, u32[]{:S(2)}) collective-permute-start(f32[9,4,8,128]{3,2,1,0:T(8,128)} %get-tuple-element.30.own), channel_id=1, source_target_pairs={{0,8},{8,16},{16,24},{24,0},{1,9},{9,17},{17,25},{25,1},{2,10},{10... | collective-permute-start | bytes 442376 | tf_op jit(solution)/shard_map/ppermute | solution.py:442
  43.8 7.5 %collective-permute-start.8 = (f32[6,4,8,128]{3,2,1,0:T(8,128)}, f32[6,4,8,128]{3,2,1,0:T(8,128)S(1)}, u32[]{:S(2)}, u32[]{:S(2)}) collective-permute-start(f32[6,4,8,128]{3,2,1,0:T(8,128)} %get-tuple-element.33), channel_id=1, source_target_pairs={{0,16},{8,24},{16,0},{24,8},{1,17},{9,25},{17,1},{25,9},{2,18},{10... | collective-permute-start | bytes 294920 | tf_op jit(solution)/shard_map/ppermute | solution.py:442
  51.4 0.6 %copy-start.9 = (f32[6,4,8,128]{3,2,1,0:T(8,128)}, f32[6,4,8,128]{3,2,1,0:T(8,128)S(1)}, u32[]{:S(2)}) copy-start(f32[6,4,8,128]{3,2,1,0:T(8,128)S(1)} %collective-permute-done.8.refs_1_) | copy-start | bytes 294916
  51.4 0.7 %copy-start.6 = (f32[9,4,8,128]{3,2,1,0:T(8,128)}, f32[9,4,8,128]{3,2,1,0:T(8,128)S(1)}, u32[]{:S(2)}) copy-start(f32[9,4,8,128]{3,2,1,0:T(8,128)S(1)} %collective-permute-done.9.refs_2_) | copy-start | bytes 442372
  51.4 0.7 %copy-start.7 = (f32[9,4,8,128]{3,2,1,0:T(8,128)}, f32[9,4,8,128]{3,2,1,0:T(8,128)S(1)}, u32[]{:S(2)}) copy-start(f32[9,4,8,128]{3,2,1,0:T(8,128)S(1)} %collective-permute-done.7.refs_0_) | copy-start | bytes 442372
  51.4 0.8 %copy-start.2 = (f32[3,8,2,8,128]{4,3,2,1,0:T(8,128)}, f32[3,8,2,8,128]{4,3,2,1,0:T(8,128)S(1)}, u32[]{:S(2)}) copy-start(f32[3,8,2,8,128]{4,3,2,1,0:T(8,128)S(1)} %collective-permute-done.5.before) | copy-start | bytes 589828
  51.4 0.8 %copy-start.3 = (f32[3,8,2,8,128]{4,3,2,1,0:T(8,128)}, f32[3,8,2,8,128]{4,3,2,1,0:T(8,128)S(1)}, u32[]{:S(2)}) copy-start(f32[3,8,2,8,128]{4,3,2,1,0:T(8,128)S(1)} %collective-permute-done.6.after) | copy-start | bytes 589828

commit v2 on v1

--- a/solution.py
+++ b/solution.py
@@ -11,6 +11,7 @@
 NEAR = 4.0 / 3.0
 FAR = -1.0 / 12.0
 HALO = 2
+VMEM_LIMIT = 16 * 1024 * 1024
 F32 = jnp.float32
 
 
@@ -102,7 +103,7 @@
 
     def block(ref, layer):
         at = group * dims.layers + layer
-        return lambda i, j: ref[at, i, j]
+        return lambda i, j: ref[i, j, at]
 
     rows = range(dims.rows)
 
@@ -147,33 +148,42 @@
                 at += 3
 
 
-def response_kernel(dims, pivots, lower, upper, out):
+def response_kernel(dims, pivots, lower, upper, out, table):
     total = dims.layers * dims.depth
+    groups = range(dims.depth)
     lane = lax.broadcasted_iota(jnp.int32, (1, LANES), 1)
-    for g in range(dims.depth):
-        y = [(lane == c).astype(F32) for c in range(3)]
-        s = [(lane == 3 + c).astype(F32) for c in range(3)]
-
-        def forward(k, y):
+    table[...] = jnp.zeros_like(table)
+
+    def forward(k, ys):
+        done = []
+        for g in groups:
             l = g * dims.layers + k
-            low = matvec(lambda i, j: lower[l, i, j], y)
-            y = matvec(lambda i, j: pivots[l, i, j], [-a for a in low])
-            for c in range(3):
-                out[l, pl.ds(c, 1)] = y[c]
-            return y
-
-        def backward(k, s):
+            low = matvec(lambda i, j: lower[i, j, l], ys[g])
+            y = matvec(lambda i, j: pivots[i, j, l], [-a for a in low])
+            for c in range(3):
+                table[pl.ds(3 * l + c, 1), :] = y[c]
+            done.append(y)
+        return done
+
+    def backward(k, after):
+        done = []
+        for g in groups:
             l = (g + 1) * dims.layers - 1 - k
-            up = matvec(lambda i, j: upper[l, i, j], s)
-            s = [out[l, pl.ds(c, 1)] - up[c] for c in range(3)]
-            for c in range(3):
-                out[l, pl.ds(c, 1)] = s[c]
-            return s
-
-        y = lax.fori_loop(0, dims.layers, forward, y)
+            up = matvec(lambda i, j: upper[i, j, l], after[g])
+            s = [table[pl.ds(3 * l + c, 1), :] - up[c] for c in range(3)]
+            for c in range(3):
+                table[pl.ds(3 * l + c, 1), :] = s[c]
+            done.append(s)
+        return done
+
+    start = [[(lane == c).astype(F32) for c in range(3)] for _ in groups]
+    ends = lax.fori_loop(0, dims.layers, forward, start)
+    for g in groups:
         for c in range(3):
-            out[total + g, pl.ds(c, 1)] = y[c]
-        lax.fori_loop(0, dims.layers, backward, s)
+            table[pl.ds(3 * (total + g) + c, 1), :] = ends[g][c]
+    start = [[(lane == 3 + c).astype(F32) for c in range(3)] for _ in groups]
+    lax.fori_loop(0, dims.layers, backward, start)
+    out[...] = table[...].T[:8]
 
 
 def shifted_sum(dims, w, lane):
@@ -292,13 +302,13 @@
         return field[c, l, r]
 
     def carry_y(g):
-        return lambda i, j: response[total + g, i, j]
+        return lambda i, j: response[j, 3 * (total + g) + i]
 
     def first_y(g):
-        return lambda i, j: response[g * dims.layers, i, j]
+        return lambda i, j: response[j, 3 * g * dims.layers + i]
 
     def first_s(g):
-        return lambda i, j: response[g * dims.layers, i, 3 + j]
+        return lambda i, j: response[3 + j, 3 * g * dims.layers + i]
 
     for g in range(dims.depth):
 
@@ -346,8 +356,8 @@
             y = [bound[c, r] for c in range(3)]
             s = [bound[3 + c, r] for c in range(3)]
             fix = add(
-                matvec(lambda i, j: response[layer, i, j], y),
-                matvec(lambda i, j: response[layer, i, 3 + j], s),
+                matvec(lambda i, j: response[j, 3 * layer + i], y),
+                matvec(lambda i, j: response[3 + j, 3 * layer + i], s),
             )
             for c in range(3):
                 for step, weight in ((1, NEAR), (2, FAR)):
@@ -387,6 +397,7 @@
         in_specs=[smem() if i else vmem() for i in ins],
         out_specs=[vmem()] * len(outs),
         scratch_shapes=scratch,
+        compiler_params=pltpu.CompilerParams(vmem_limit_bytes=VMEM_LIMIT),
         cost_estimate=pl.CostEstimate(flops=flops, bytes_accessed=1000000, transcendentals=0),
     )(*args)
 
@@ -422,7 +433,8 @@
     mask_view = mask.reshape(lines[2:]).transpose(1, 0, 2).reshape(-1, LANES)
     halo = shape(3, dims.layers, HALO, *dims.tile)
     field = shape(*dims.field())
-    planes = 3 * dims.rows
+    table = -(-3 * dims.depth * (dims.layers + 1) // LANES) * LANES
+    pivots, lower, upper = (block.transpose(1, 2, 0) for block in (pivots, lower, upper))
 
     def bind(kernel, *static):
         return functools.partial(kernel, dims, *static)
@@ -460,9 +472,10 @@
     others = swap_depth(sent)
     (response,) = call(
         bind(response_kernel),
-        [shape(dims.depth * (dims.layers + 1), 3, LANES)],
+        [shape(8, table)],
         [1, 1, 1],
         (pivots, lower, upper),
+        [pltpu.VMEM((table, LANES), F32)],
     )
     heff, noise = call(
         bind(local_kernel, True),

time: 56.6 us -> 37.4 us (0.66)
  Pallas kernels: 32.3 us -> 12 us
  waiting for transfers between devices: 3.52 us -> 5.3 us
  local copies, waits for them, and re-layouts: 3.79 us -> 3.16 us
    pallas_call x8, Pallas kernels: 32.3 us -> 12 us  [call(): pl.pallas_call(kernel, out_shape=outs, in_specs=[smem() if i else vmem()...]
    ppermute x6, waiting for transfers between devices: 3.51 us -> 5.29 us  [swap_depth(): lax.ppermute(message, 'depth', ring(dims.depth, k))]
    unnamed x29 -> x26, local copies, waits for them, and re-layouts: 3.79 us -> 3.16 us
  transfers between devices with their start and end apart: 10 -> 10, of which waited for: 1 -> 2; matrix products, arithmetic and copies ran while one was open for 4% -> 0% of each run, Pallas kernels for 41% -> 22%
where the time goes in v2:
time: 37.4 us; the launch traced here: 37.1 us
  starting transfers between devices  14.7 us (39%)
  Pallas kernels  12 us (32%)
  waiting for transfers between devices  5.3 us (14%)
  local copies, waits for them, and re-layouts  3.16 us (8%)
  between operations  2.05 us (5%)
    pallas_call x8, Pallas kernels, call(): pl.pallas_call(kernel, out_shape=outs, in_specs=[smem() if i else vmem()...  12 us
    ppermute x2, starting transfers between devices, swap_plane(): after = lax.ppermute(low, 'plane', ring(dims.plane, -1))  7.83 us
    ppermute x6, waiting for transfers between devices, swap_depth(): lax.ppermute(message, 'depth', ring(dims.depth, k))  5.29 us
    ppermute x6, starting transfers between devices, swap_depth(): lax.ppermute(message, 'depth', ring(dims.depth, k))  3.75 us
    unnamed x26, local copies, waits for them, and re-layouts  3.16 us
    ppermute x2, starting transfers between devices, swap_plane(): before = lax.ppermute(high, 'plane', ring(dims.plane, 1))  3.08 us
  transfers between devices with their start and end apart: 10, of which 2 were waited for; matrix products, arithmetic and copies ran while one was open for 0% of the time, Pallas kernels for 22%

profile of v2, /device:TPU:0, one launch (start us, length us, event | category | flops | bytes accessed | tf_op | source)
XLA Modules:
  0.0 37.1 jit_solution(6560989651899162160)
XLA Ops:
  0.6 1.0 %copy-done = f32[3,8,4,1024]{3,2,1,0:T(4,128)S(1)} copy-done((f32[3,8,4,1024]{3,2,1,0:T(4,128)S(1)}, f32[3,8,4,1024]{3,2,1,0:T(4,128)}, u32[]{:S(2)}) %copy-start) | copy-done | bytes 393240
  1.6 0.7 %copy-done.2 = s32[4,1024]{1,0:T(4,128)S(1)} copy-done((s32[4,1024]{1,0:T(4,128)S(1)}, s32[4,1024]{1,0:T(4,128)}, u32[]{:S(2)}) %copy-start.2) | copy-done | bytes 16408
  2.4 0.0 copy-start.4
  2.4 3.0 %collective-permute-start = (f32[3,8,2,8,128]{4,3,2,1,0:T(8,128)S(1)}, f32[3,8,2,8,128]{4,3,2,1,0:T(8,128)S(1)}, u32[]{:S(2)}, u32[]{:S(2)}) collective-permute-start(f32[3,8,2,8,128]{4,3,2,1,0:T(8,128)S(1)} %get-tuple-element.23), channel_id=1, source_target_pairs={{0,1},{1,2},{2,3},{3,4},{4,5},{5,6},{6,7},{7,0},{8,9},{9,10},{10,1... | collective-permute-start | bytes 589832 | tf_op jit(solution)/shard_map/ppermute | solution.py:444
  5.4 3.1 %collective-permute-start.1 = (f32[3,8,2,8,128]{4,3,2,1,0:T(8,128)S(1)}, f32[3,8,2,8,128]{4,3,2,1,0:T(8,128)S(1)}, u32[]{:S(2)}, u32[]{:S(2)}) collective-permute-start(f32[3,8,2,8,128]{4,3,2,1,0:T(8,128)S(1)} %get-tuple-element.24), channel_id=1, source_target_pairs={{0,7},{1,0},{2,1},{3,2},{4,3},{5,4},{6,5},{7,6},{8,15},{9,8},{10,9... | collective-permute-start | bytes 589832 | tf_op jit(solution)/shard_map/ppermute | solution.py:443
  8.5 0.6 %copy-done.7 = s32[8]{0:T(128)S(1)} copy-done((s32[8]{0:T(128)S(1)}, s32[8]{0:T(128)}, u32[]{:S(2)}) %copy-start.7) | copy-done | bytes 56
  9.2 0.0 copy-done.10
  9.2 1.6 %shard_map.140 = (f32[9,4,8,128]{3,2,1,0:T(8,128)S(1)}, f32[6,4,8,128]{3,2,1,0:T(8,128)S(1)}, f32[9,4,8,128]{3,2,1,0:T(8,128)S(1)}, f32[3,8,4,8,128]{4,3,2,1,0:T(8,128)S(1)}) custom-call(f32[768,128]{1,0:T(8,128)S(1)} %bitcast.24, s32[32,128]{1,0:T(8,128)S(1)} %bitcast.28, s32[8]{0:T(128)S(1)} %copy-done.7, f32[4]{0:T(128)S(1)} %copy-done.10, ...), custom_call_target="tpu_custom_call" | custom-call | flops 1000000 | bytes 1000000 | tf_op jit(solution)/shard_map/pallas_call | solution.py:394
  10.8 0.7 %collective-permute-start.4 = (f32[9,4,8,128]{3,2,1,0:T(8,128)S(1)}, f32[9,4,8,128]{3,2,1,0:T(8,128)S(1)}, u32[]{:S(2)}, u32[]{:S(2)}) collective-permute-start(f32[9,4,8,128]{3,2,1,0:T(8,128)S(1)} %get-tuple-element.26), channel_id=1, source_target_pairs={{0,24},{8,0},{16,8},{24,16},{1,25},{9,1},{17,9},{25,17},{2,26},{10... | collective-permute-start | bytes 442376 | tf_op jit(solution)/shard_map/ppermute | solution.py:454
  11.5 0.0 collective-permute-start.2
  11.5 1.4 %collective-permute-start.3 = (f32[6,4,8,128]{3,2,1,0:T(8,128)S(1)}, f32[6,4,8,128]{3,2,1,0:T(8,128)S(1)}, u32[]{:S(2)}, u32[]{:S(2)}) collective-permute-start(f32[6,4,8,128]{3,2,1,0:T(8,128)S(1)} %get-tuple-element.25), channel_id=1, source_target_pairs={{0,16},{8,24},{16,0},{24,8},{1,17},{9,25},{17,1},{25,9},{2,18},{10... | collective-permute-start | bytes 294920 | tf_op jit(solution)/shard_map/ppermute | solution.py:454
  14.2 1.6 %shard_map.142.response = f32[8,128]{1,0:T(8,128)S(1)} custom-call(f32[3,3,32]{2,1,0:T(4,128)S(1)} %bitcast.35, f32[3,3,32]{2,1,0:T(4,128)S(1)} %bitcast.38, f32[3,3,32]{2,1,0:T(4,128)S(1)} %bitcast.41), custom_call_target="tpu_custom_call" | custom-call | flops 1000000 | bytes 1000000 | tf_op jit(solution)/shard_map/pallas_call | solution.py:394
  15.8 0.0 copy-done.1
  15.9 0.6 %copy-done.8 = f32[4]{0:T(128)S(1)} copy-done((f32[4]{0:T(128)S(1)}, f32[4]{0:T(128)}, u32[]{:S(2)}) %copy-start.8) | copy-done | bytes 40
  16.5 0.0 copy-done.9
  16.5 0.0 copy-done.12
  16.6 1.7 %shard_map.141 = (f32[3,8,4,8,128]{4,3,2,1,0:T(8,128)S(1)}, f32[3,8,4,8,128]{4,3,2,1,0:T(8,128)S(1)}) custom-call(f32[768,128]{1,0:T(8,128)S(1)} %bitcast.25, s32[32,128]{1,0:T(8,128)S(1)} %bitcast.29, f32[3,8,4,8,128]{4,3,2,1,0:T(8,128)S(1)} %get-tuple-element.20.local, s32[8]{0:T(128)S(1)} %copy-done.7, f32[4]{0:T(128)S(1)} %copy-done.8, f32[4]{0:T(128)S(1)} %copy-done.9, ...), custom_call_target="tpu_custom_call" | custom-call | flops 1000000 | bytes 1000000 | tf_op jit(solution)/shard_map/pallas_call | solution.py:394
  18.2 0.0 copy-start.11
  18.2 0.5 %collective-permute-done.3.refs_1_ = f32[6,4,8,128]{3,2,1,0:T(8,128)S(1)} collective-permute-done((f32[6,4,8,128]{3,2,1,0:T(8,128)S(1)}, f32[6,4,8,128]{3,2,1,0:T(8,128)S(1)}, u32[]{:S(2)}, u32[]{:S(2)}) %collective-permute-start.3) | collective-permute-done | bytes 98336 | tf_op jit(solution)/shard_map/ppermute | solution.py:454
  18.8 0.0 collective-permute-done.2.refs_0_
  18.8 0.0 collective-permute-done.before
  18.8 0.1 copy-done.11
  18.9 1.5 %shard_map.144 = (f32[3,8,4,8,128]{4,3,2,1,0:T(8,128)S(1)}, f32[3,8,4,8,128]{4,3,2,1,0:T(8,128)S(1)}, f32[3,8,2,8,128]{4,3,2,1,0:T(8,128)S(1)}, f32[3,8,2,8,128]{4,3,2,1,0:T(8,128)S(1)}) custom-call(f32[768,128]{1,0:T(8,128)S(1)} %bitcast.26, s32[32,128]{1,0:T(8,128)S(1)} %bitcast.30, f32[3,8,4,8,128]{4,3,2,1,0:T(8,128)S(1)} %get-tuple-element.21.heff, ...), custom_call_target="tpu_custom_call" | custom-call | flops 1000000 | bytes 1000000 | tf_op jit(solution)/shard_map/pallas_call | solution.py:394
  20.4 0.1 collective-permute-start.5
  20.5 4.7 %collective-permute-start.6 = (f32[3,8,2,8,128]{4,3,2,1,0:T(8,128)S(1)}, f32[3,8,2,8,128]{4,3,2,1,0:T(8,128)S(1)}, u32[]{:S(2)}, u32[]{:S(2)}) collective-permute-start(f32[3,8,2,8,128]{4,3,2,1,0:T(8,128)S(1)} %get-tuple-element.32), channel_id=1, source_target_pairs={{0,7},{1,0},{2,1},{3,2},{4,3},{5,4},{6,5},{7,6},{8,15},{9,8},{10,9... | collective-permute-start | bytes 589832 | tf_op jit(solution)/shard_map/ppermute | solution.py:443
  25.2 1.5 %shard_map.145 = (f32[9,4,8,128]{3,2,1,0:T(8,128)S(1)}, f32[6,4,8,128]{3,2,1,0:T(8,128)S(1)}, f32[9,4,8,128]{3,2,1,0:T(8,128)S(1)}, f32[3,8,4,8,128]{4,3,2,1,0:T(8,128)S(1)}) custom-call(f32[3,8,4,8,128]{4,3,2,1,0:T(8,128)S(1)} %get-tuple-element.27.field, s32[32,128]{1,0:T(8,128)S(1)} %bitcast.31, s32[8]{0:T(128)S(1)} %copy-done.7, f32[4]{0:T(128)S(1)} %copy-done.10, ...), custom_call_target="tpu_custom_call" | custom-call | flops 1000000 | bytes 1000000 | tf_op jit(solution)/shard_map/pallas_call | solution.py:394
  26.7 0.4 %collective-permute-start.9 = (f32[9,4,8,128]{3,2,1,0:T(8,128)S(1)}, f32[9,4,8,128]{3,2,1,0:T(8,128)S(1)}, u32[]{:S(2)}, u32[]{:S(2)}) collective-permute-start(f32[9,4,8,128]{3,2,1,0:T(8,128)S(1)} %get-tuple-element.34), channel_id=1, source_target_pairs={{0,24},{8,0},{16,8},{24,16},{1,25},{9,1},{17,9},{25,17},{2,26},{10... | collective-permute-start | bytes 442376 | tf_op jit(solution)/shard_map/ppermute | solution.py:454
  27.2 0.1 collective-permute-start.7
  27.3 1.0 %collective-permute-start.8 = (f32[6,4,8,128]{3,2,1,0:T(8,128)S(1)}, f32[6,4,8,128]{3,2,1,0:T(8,128)S(1)}, u32[]{:S(2)}, u32[]{:S(2)}) collective-permute-start(f32[6,4,8,128]{3,2,1,0:T(8,128)S(1)} %get-tuple-element.33), channel_id=1, source_target_pairs={{0,16},{8,24},{16,0},{24,8},{1,17},{9,25},{17,1},{25,9},{2,18},{10... | collective-permute-start | bytes 294920 | tf_op jit(solution)/shard_map/ppermute | solution.py:454
  28.3 1.6 %shard_map.146.heff = f32[3,8,4,8,128]{4,3,2,1,0:T(8,128)S(1)} custom-call(f32[3,8,4,8,128]{4,3,2,1,0:T(8,128)S(1)} %get-tuple-element.27.field, s32[32,128]{1,0:T(8,128)S(1)} %bitcast.32, f32[3,8,4,8,128]{4,3,2,1,0:T(8,128)S(1)} %get-tuple-element.28.local.refs_4_, s32[8]{0:T(128)S(1)} %copy-done.7, f32[4]{0:T(128)S(1)} %copy-done.8, f32[4]{0:T(128)S(1)} %copy-done.9, ...), custom_call_target="tpu_custom_call" | custom-call | flops 1000000 | bytes 1000000 | tf_op jit(solution)/shard_map/pallas_call | solution.py:394
  30.0 4.7 %collective-permute-done.8.refs_1_ = f32[6,4,8,128]{3,2,1,0:T(8,128)S(1)} collective-permute-done((f32[6,4,8,128]{3,2,1,0:T(8,128)S(1)}, f32[6,4,8,128]{3,2,1,0:T(8,128)S(1)}, u32[]{:S(2)}, u32[]{:S(2)}) %collective-permute-start.8) | collective-permute-done | bytes 98336 | tf_op jit(solution)/shard_map/ppermute | solution.py:454
  34.8 2.4 %shard_map.147 = (f32[768,128]{1,0:T(8,128)}, f32[768,128]{1,0:T(8,128)}) custom-call(f32[3,8,4,8,128]{4,3,2,1,0:T(8,128)S(1)} %get-tuple-element.27.field, s32[32,128]{1,0:T(8,128)S(1)} %bitcast.33, f32[3,8,4,8,128]{4,3,2,1,0:T(8,128)S(1)} %shard_map.146.heff, f32[9,4,8,128]{3,2,1,0:T(8,128)S(1)} %get-tuple-element.30.own, ...), custom_call_target="tpu_custom_call" | custom-call | flops 1000000 | bytes 1000000 | tf_op jit(solution)/shard_map/pallas_call | solution.py:394
  (22 shorter events, 0.1 us)
Async XLA Ops:
  0.6 1.0 %copy-start = (f32[3,8,4,1024]{3,2,1,0:T(4,128)S(1)}, f32[3,8,4,1024]{3,2,1,0:T(4,128)}, u32[]{:S(2)}) copy-start(f32[3,8,4,1024]{3,2,1,0:T(4,128)} %param.13) | copy-start | bytes 1179652
  1.6 0.7 %copy-start.2 = (s32[4,1024]{1,0:T(4,128)S(1)}, s32[4,1024]{1,0:T(4,128)}, u32[]{:S(2)}) copy-start(s32[4,1024]{1,0:T(4,128)} %param.14) | copy-start | bytes 49156
  2.3 6.2 %copy-start.5 = (f32[32,3,3]{0,2,1:T(4,128)S(1)}, f32[32,3,3]{0,2,1:T(4,128)}, u32[]{:S(2)}) copy-start(f32[32,3,3]{0,2,1:T(4,128)} %param.22) | copy-start | bytes 3460
  2.3 6.2 %copy-start.6 = (f32[32,3,3]{0,2,1:T(4,128)S(1)}, f32[32,3,3]{0,2,1:T(4,128)}, u32[]{:S(2)}) copy-start(f32[32,3,3]{0,2,1:T(4,128)} %param.23) | copy-start | bytes 3460
  2.3 13.5 %copy-start.1 = (f32[3,8,4,1024]{3,2,1,0:T(4,128)S(1)}, f32[3,8,4,1024]{3,2,1,0:T(4,128)}, u32[]{:S(2)}) copy-start(f32[3,8,4,1024]{3,2,1,0:T(4,128)} %param.13) | copy-start | bytes 1179652
  2.4 6.2 %copy-start.4 = (f32[32,3,3]{0,2,1:T(4,128)S(1)}, f32[32,3,3]{0,2,1:T(4,128)}, u32[]{:S(2)}) copy-start(f32[32,3,3]{0,2,1:T(4,128)} %param.21) | copy-start | bytes 3460
  2.4 16.4 %collective-permute-start = (f32[3,8,2,8,128]{4,3,2,1,0:T(8,128)S(1)}, f32[3,8,2,8,128]{4,3,2,1,0:T(8,128)S(1)}, u32[]{:S(2)}, u32[]{:S(2)}) collective-permute-start(f32[3,8,2,8,128]{4,3,2,1,0:T(8,128)S(1)} %get-tuple-element.23), channel_id=1, source_target_pairs={{0,1},{1,2},{2,3},{3,4},{4,5},{5,6},{6,7},{7,0},{8,9},{9,10},{10,1... | collective-permute-start | bytes 589832 | tf_op jit(solution)/shard_map/ppermute | solution.py:444
  5.4 13.4 %collective-permute-start.1 = (f32[3,8,2,8,128]{4,3,2,1,0:T(8,128)S(1)}, f32[3,8,2,8,128]{4,3,2,1,0:T(8,128)S(1)}, u32[]{:S(2)}, u32[]{:S(2)}) collective-permute-start(f32[3,8,2,8,128]{4,3,2,1,0:T(8,128)S(1)} %get-tuple-element.24), channel_id=1, source_target_pairs={{0,7},{1,0},{2,1},{3,2},{4,3},{5,4},{6,5},{7,6},{8,15},{9,8},{10,9... | collective-permute-start | bytes 589832 | tf_op jit(solution)/shard_map/ppermute | solution.py:443
  8.5 0.7 %copy-start.7 = (s32[8]{0:T(128)S(1)}, s32[8]{0:T(128)}, u32[]{:S(2)}) copy-start(s32[8]{0:T(128)} %materials.11) | copy-start | bytes 100
  8.5 0.7 %copy-start.10 = (f32[4]{0:T(128)S(1)}, f32[4]{0:T(128)}, u32[]{:S(2)}) copy-start(f32[4]{0:T(128)} %source.3) | copy-start | bytes 52
  10.8 8.0 %collective-permute-start.4 = (f32[9,4,8,128]{3,2,1,0:T(8,128)S(1)}, f32[9,4,8,128]{3,2,1,0:T(8,128)S(1)}, u32[]{:S(2)}, u32[]{:S(2)}) collective-permute-start(f32[9,4,8,128]{3,2,1,0:T(8,128)S(1)} %get-tuple-element.26), channel_id=1, source_target_pairs={{0,24},{8,0},{16,8},{24,16},{1,25},{9,1},{17,9},{25,17},{2,26},{10... | collective-permute-start | bytes 442376 | tf_op jit(solution)/shard_map/ppermute | solution.py:454
  11.5 7.3 %collective-permute-start.2 = (f32[9,4,8,128]{3,2,1,0:T(8,128)S(1)}, f32[9,4,8,128]{3,2,1,0:T(8,128)S(1)}, u32[]{:S(2)}, u32[]{:S(2)}) collective-permute-start(f32[9,4,8,128]{3,2,1,0:T(8,128)S(1)} %get-tuple-element.22.own), channel_id=1, source_target_pairs={{0,8},{8,16},{16,24},{24,0},{1,9},{9,17},{17,25},{25,1},{2,10},{10... | collective-permute-start | bytes 442376 | tf_op jit(solution)/shard_map/ppermute | solution.py:454
  11.5 7.3 %collective-permute-start.3 = (f32[6,4,8,128]{3,2,1,0:T(8,128)S(1)}, f32[6,4,8,128]{3,2,1,0:T(8,128)S(1)}, u32[]{:S(2)}, u32[]{:S(2)}) collective-permute-start(f32[6,4,8,128]{3,2,1,0:T(8,128)S(1)} %get-tuple-element.25), channel_id=1, source_target_pairs={{0,16},{8,24},{16,0},{24,8},{1,17},{9,25},{17,1},{25,9},{2,18},{10... | collective-permute-start | bytes 294920 | tf_op jit(solution)/shard_map/ppermute | solution.py:454
  15.8 0.7 %copy-start.8 = (f32[4]{0:T(128)S(1)}, f32[4]{0:T(128)}, u32[]{:S(2)}) copy-start(f32[4]{0:T(128)} %stiffness.7) | copy-start | bytes 52
  15.8 0.7 %copy-start.9 = (f32[4]{0:T(128)S(1)}, f32[4]{0:T(128)}, u32[]{:S(2)}) copy-start(f32[4]{0:T(128)} %anisotropy.3) | copy-start | bytes 52
  15.8 0.7 %copy-start.12 = (f32[4]{0:T(128)S(1)}, f32[4]{0:T(128)}, u32[]{:S(2)}) copy-start(f32[4]{0:T(128)} %refs_0_.1) | copy-start | bytes 52
  18.2 0.7 %copy-start.11 = (f32[4]{0:T(128)S(1)}, f32[4]{0:T(128)}, u32[]{:S(2)}) copy-start(f32[4]{0:T(128)} %damping.3) | copy-start | bytes 52
  20.4 14.3 %collective-permute-start.5 = (f32[3,8,2,8,128]{4,3,2,1,0:T(8,128)S(1)}, f32[3,8,2,8,128]{4,3,2,1,0:T(8,128)S(1)}, u32[]{:S(2)}, u32[]{:S(2)}) collective-permute-start(f32[3,8,2,8,128]{4,3,2,1,0:T(8,128)S(1)} %get-tuple-element.31), channel_id=1, source_target_pairs={{0,1},{1,2},{2,3},{3,4},{4,5},{5,6},{6,7},{7,0},{8,9},{9,10},{10,1... | collective-permute-start | bytes 589832 | tf_op jit(solution)/shard_map/ppermute | solution.py:444
  20.5 14.3 %collective-permute-start.6 = (f32[3,8,2,8,128]{4,3,2,1,0:T(8,128)S(1)}, f32[3,8,2,8,128]{4,3,2,1,0:T(8,128)S(1)}, u32[]{:S(2)}, u32[]{:S(2)}) collective-permute-start(f32[3,8,2,8,128]{4,3,2,1,0:T(8,128)S(1)} %get-tuple-element.32), channel_id=1, source_target_pairs={{0,7},{1,0},{2,1},{3,2},{4,3},{5,4},{6,5},{7,6},{8,15},{9,8},{10,9... | collective-permute-start | bytes 589832 | tf_op jit(solution)/shard_map/ppermute | solution.py:443
  25.2 3.1 %copy-start.3 = (s32[4,1024]{1,0:T(4,128)S(1)}, s32[4,1024]{1,0:T(4,128)}, u32[]{:S(2)}) copy-start(s32[4,1024]{1,0:T(4,128)} %param.14) | copy-start | bytes 49156
  26.7 8.0 %collective-permute-start.9 = (f32[9,4,8,128]{3,2,1,0:T(8,128)S(1)}, f32[9,4,8,128]{3,2,1,0:T(8,128)S(1)}, u32[]{:S(2)}, u32[]{:S(2)}) collective-permute-start(f32[9,4,8,128]{3,2,1,0:T(8,128)S(1)} %get-tuple-element.34), channel_id=1, source_target_pairs={{0,24},{8,0},{16,8},{24,16},{1,25},{9,1},{17,9},{25,17},{2,26},{10... | collective-permute-start | bytes 442376 | tf_op jit(solution)/shard_map/ppermute | solution.py:454
  27.2 7.6 %collective-permute-start.7 = (f32[9,4,8,128]{3,2,1,0:T(8,128)S(1)}, f32[9,4,8,128]{3,2,1,0:T(8,128)S(1)}, u32[]{:S(2)}, u32[]{:S(2)}) collective-permute-start(f32[9,4,8,128]{3,2,1,0:T(8,128)S(1)} %get-tuple-element.30.own), channel_id=1, source_target_pairs={{0,8},{8,16},{16,24},{24,0},{1,9},{9,17},{17,25},{25,1},{2,10},{10... | collective-permute-start | bytes 442376 | tf_op jit(solution)/shard_map/ppermute | solution.py:454
  27.3 7.4 %collective-permute-start.8 = (f32[6,4,8,128]{3,2,1,0:T(8,128)S(1)}, f32[6,4,8,128]{3,2,1,0:T(8,128)S(1)}, u32[]{:S(2)}, u32[]{:S(2)}) collective-permute-start(f32[6,4,8,128]{3,2,1,0:T(8,128)S(1)} %get-tuple-element.33), channel_id=1, source_target_pairs={{0,16},{8,24},{16,0},{24,8},{1,17},{9,25},{17,1},{25,9},{2,18},{10... | collective-permute-start | bytes 294920 | tf_op jit(solution)/shard_map/ppermute | solution.py:454

commit v3 on v2

v3 whole, which is shorter than its diff:
```python
import functools

import jax
import jax.numpy as jnp
from jax import lax
from jax.experimental import pallas as pl
from jax.experimental.pallas import tpu as pltpu
from jax.sharding import PartitionSpec as P

LANES = 128
NEAR = 4.0 / 3.0
FAR = -1.0 / 12.0
HALO = 2
VMEM_LIMIT = 16 * 1024 * 1024
UNROLL = 4
F32 = jnp.float32


def wrapped(value):
    value &= 0xFFFFFFFF
    return value - (1 << 32) if value >= (1 << 31) else value


HASH_A = wrapped(739982445)
HASH_B = wrapped(695872825)
HASH_C = wrapped(1597334677)


class Dims:
    def __init__(self, layers, rows, width, depth, plane):
        self.layers = layers
        self.rows = rows
        self.width = width
        self.chunks = width // LANES
        self.depth = depth
        self.plane = plane
        self.tile = (self.chunks, LANES)

    def field(self):
        return (3, self.layers, self.rows) + self.tile


def shape(*dims):
    return jax.ShapeDtypeStruct(dims, F32)


def vmem():
    return pl.BlockSpec(memory_space=pltpu.VMEM)


def hbm():
    return pl.BlockSpec(memory_space=pltpu.HBM)


def pick(parts, comp, layer, row):
    rows = parts[0].shape[2]
    return parts[row // rows][comp, layer, row % rows]


def cells(dims, comp, layer, row):
    base = (comp * dims.layers + layer) * (dims.chunks * dims.rows) + row
    return pl.ds(base, dims.chunks, stride=dims.rows)


def matvec(get, vec):
    return [get(i, 0) * vec[0] + get(i, 1) * vec[1] + get(i, 2) * vec[2] for i in range(3)]


def add(a, b):
    return [x + y for x, y in zip(a, b)]


def cross(a, b):
    return [
        a[1] * b[2] - a[2] * b[1],
        a[2] * b[0] - a[0] * b[2],
        a[0] * b[1] - a[1] * b[0],
    ]


def unit(vec):
    scale = lax.rsqrt(vec[0] * vec[0] + vec[1] * vec[1] + vec[2] * vec[2])
    return [v * scale for v in vec]


PIVOT_SOURCE, PIVOT_LOWER, UPPER, FROM_Y, FROM_S, LAYER_COEFS = 0, 9, 18, 27, 36, 45
LAST_Y, FIRST_Y, FIRST_S, GROUP_COEFS = 0, 9, 18, 27
STIFF, ANISO, DAMP, THERMAL, SCALE, LAYER_VALUES = 0, 1, 2, 3, 4, 5


def table(ref, at, first):
    return lambda i, j: ref[at, first + 3 * i + j]


def sweep_back(dims, local, upper, rows):
    def backward(l, after):
        done = []
        for r in rows:
            up = matvec(upper(l), after[r])
            s = [local[c, l, r] - up[c] for c in range(3)]
            for c in range(3):
                local[c, l, r] = s[c]
            done.append(s)
        return done

    zero = [[jnp.zeros(dims.tile, F32)] * 3 for _ in rows]
    return loop(dims.layers, lambda k, after: backward(dims.layers - 1 - k, after), zero)


def loop(count, body, start):
    step = max(k for k in range(1, UNROLL + 1) if count % k == 0)

    def steps(k, carry):
        for i in range(step):
            carry = body(k * step + i, carry)
        return carry

    if step == count:
        return steps(0, start)
    return lax.fori_loop(0, count // step, steps, start)


def message_parts(dims, k):
    last, first = (k == 1) * 3, (k == dims.depth - 1) * 3
    return [range(0, 6)] + [range(6, 9)] * (last > 0) + [range(9, 12)] * (first > 0)


def fetch(inputs, held, sems):
    copies = [
        pltpu.make_async_copy(src, dst, sems.at[k])
        for k, (src, dst) in enumerate(zip(inputs, held))
    ]
    for copy in copies:
        copy.start()
    for copy in copies:
        copy.wait()


def enter_kernel(dims, *refs):
    inputs, refs = refs[:7], refs[7:]
    field, maskf, low, high, local, *messages = refs[: 4 + dims.depth]
    *held, sems = refs[4 + dims.depth :]
    magnet, mask, materials, source, pivots, lower, upper = held
    fetch(inputs, held, sems)
    group = lax.axis_index("depth")
    rows = range(dims.rows)
    for r in rows:
        maskf[r] = mask[pl.ds(r, dims.chunks, stride=dims.rows), :].astype(F32)

    def block(ref, l):
        at = group * dims.layers + l
        return lambda i, j: ref[i, j, at]

    def forward(l, prev):
        beta = source[materials[l]]
        done = []
        for r in rows:
            v = [magnet[cells(dims, c, l, r), :] for c in range(3)]
            mask_row = maskf[r]
            for c in range(3):
                field[c, l, r] = v[c]
                if r < HALO:
                    low[c, l, r] = v[c] * mask_row
                if r >= dims.rows - HALO:
                    high[c, l, r - dims.rows + HALO] = v[c] * mask_row
            drop = matvec(block(lower, l), prev[r])
            y = matvec(block(pivots, l), [beta * v[c] - drop[c] for c in range(3)])
            for c in range(3):
                local[c, l, r] = y[c]
            done.append(y)
        return done

    zero = [[jnp.zeros(dims.tile, F32)] * 3 for _ in rows]
    last = loop(dims.layers, forward, zero)
    first = sweep_back(dims, local, lambda l: block(upper, l), rows)
    for r in rows:
        values = [last[r][c] for c in range(3)] + [first[r][c] for c in range(3)]
        for l in (dims.layers - 1, 0):
            values += [field[c, l, r] * maskf[r] for c in range(3)]
        for k, message in enumerate(messages, 1):
            at = 0
            for part in message_parts(dims, k):
                for p in part:
                    message[at, r] = values[p]
                    at += 1


def coefficient_kernel(dims, *refs):
    inputs, refs = refs[:9], refs[9:]
    coefs, groups, values, trail = refs[:4]
    fetch(inputs, refs[4:13], refs[13])
    materials, stiffness, anisotropy, damping, source, thermal, pivots, lower, upper = refs[4:13]
    group = lax.axis_index("depth")
    lane = lax.broadcasted_iota(jnp.int32, dims.tile, 1)
    every = range(dims.depth)

    def splat(value):
        return jnp.full(dims.tile, value, F32)

    def column(value, j):
        return jnp.broadcast_to(value[:, j : j + 1], dims.tile)

    def forward(k, ys):
        done = []
        for g in every:
            l = g * dims.layers + k
            low = matvec(lambda i, j: lower[i, j, l], ys[g])
            y = matvec(lambda i, j: pivots[i, j, l], [-a for a in low])
            for c in range(3):
                trail[g, k, c] = y[c]
            done.append(y)
        return done

    def backward(k, after):
        done = []
        for g in every:
            at = dims.layers - 1 - k
            l = g * dims.layers + at
            up = matvec(lambda i, j: upper[i, j, l], after[g])
            s = [trail[g, at, c] - up[c] for c in range(3)]
            for c in range(3):
                trail[g, at, c] = s[c]
            done.append(s)
        return done

    start = [[(lane == c).astype(F32) for c in range(3)] for _ in every]
    last = lax.fori_loop(0, dims.layers, forward, start)
    start = [[(lane == 3 + c).astype(F32) for c in range(3)] for _ in every]
    first = lax.fori_loop(0, dims.layers, backward, start)
    for g in every:
        for i in range(3):
            for j in range(3):
                groups[g, LAST_Y + 3 * i + j] = column(last[g][i], j)
                groups[g, FIRST_Y + 3 * i + j] = column(first[g][i], j)
                groups[g, FIRST_S + 3 * i + j] = column(first[g][i], 3 + j)

    def layer(l, carry):
        at = group * dims.layers + l
        material = materials[l]
        alpha = splat(damping[material])
        values[l, STIFF] = splat(stiffness[material])
        values[l, ANISO] = splat(anisotropy[material])
        values[l, DAMP] = alpha
        values[l, THERMAL] = splat(thermal[material])
        values[l, SCALE] = 1.0 / (1.0 + alpha * alpha)
        beta = splat(source[material])
        pivot = [[splat(pivots[i, j, at]) for j in range(3)] for i in range(3)]
        low = [[splat(lower[i, j, at]) for j in range(3)] for i in range(3)]
        for i in range(3):
            for j in range(3):
                coefs[l, PIVOT_SOURCE + 3 * i + j] = pivot[i][j] * beta
                coefs[l, PIVOT_LOWER + 3 * i + j] = (
                    pivot[i][0] * low[0][j] + pivot[i][1] * low[1][j] + pivot[i][2] * low[2][j]
                )
                coefs[l, UPPER + 3 * i + j] = splat(upper[i, j, at])
                coefs[l, FROM_Y + 3 * i + j] = column(trail[group, l, i], j)
                coefs[l, FROM_S + 3 * i + j] = column(trail[group, l, i], 3 + j)
        return carry

    lax.fori_loop(0, dims.layers, layer, 0)


def shifted_sum(dims, w, lane):
    after = pltpu.roll(w, dims.chunks - 1, 0)
    before = pltpu.roll(w, 1, 0)
    near = pltpu.roll(jnp.where(lane < 1, after, w), LANES - 1, 1)
    near += pltpu.roll(jnp.where(lane >= LANES - 1, before, w), 1, 1)
    far = pltpu.roll(jnp.where(lane < 2, after, w), LANES - 2, 1)
    far += pltpu.roll(jnp.where(lane >= LANES - 2, before, w), 2, 1)
    return NEAR * near + FAR * far


def hash_uniform(mixed):
    mixed = mixed ^ lax.shift_right_logical(mixed, jnp.int32(16))
    mixed = mixed * HASH_A
    mixed = mixed ^ lax.shift_right_logical(mixed, jnp.int32(15))
    mixed = mixed * HASH_B
    mixed = mixed ^ lax.shift_right_logical(mixed, jnp.int32(16))
    return (mixed & 65535).astype(F32) * (1.0 / 32767.5) - 1.0


def local_kernel(dims, first, parts, *refs):
    fields, refs = refs[:parts], refs[parts:]
    solved, refs = refs[:parts], refs[parts:]
    maskf, values = refs[:2]
    if first:
        seed, heff, noise, masked = refs[2:]
        group = lax.axis_index("depth")
        place = lax.axis_index("plane")
        within = (
            lax.broadcasted_iota(jnp.int32, dims.tile, 0) * LANES
            + lax.broadcasted_iota(jnp.int32, dims.tile, 1)
        ) * HASH_A + seed[...]
    else:
        noise, heff, masked = refs[2:]
    lane = lax.broadcasted_iota(jnp.int32, dims.tile, 1)
    rows = range(dims.rows)

    for c in range(3):
        for r in rows:
            masked[c, 0, r] = jnp.zeros(dims.tile, F32)
            masked[c, dims.layers + 1, r] = jnp.zeros(dims.tile, F32)

    def fill(l, carry):
        for r in rows:
            mask_row = maskf[r]
            for c in range(3):
                masked[c, l + 1, r] = pick(fields, c, l, r) * mask_row
        return carry

    lax.fori_loop(0, dims.layers, fill, 0)

    def body(l, carry):
        stiff = values[l, STIFF]
        aniso = values[l, ANISO]
        for c in range(3):
            w = [masked[c, l + 1, r] for r in rows]
            for r in rows:
                total = shifted_sum(dims, w[r], lane)
                for step, weight in ((1, NEAR), (2, FAR)):
                    inside = [w[q] for q in (r - step, r + step) if 0 <= q < dims.rows]
                    if inside:
                        total += weight * functools.reduce(jnp.add, inside)
                total += 0.5 * (masked[c, l, r] + masked[c, l + 2, r])
                h = stiff * total + 0.5 * pick(solved, c, l, r)
                if c == 2:
                    h += aniso * pick(fields, c, l, r)
                if first:
                    layer = group * dims.layers + l
                    line = (c * (dims.depth * dims.layers) + layer) * (
                        dims.plane * dims.rows
                    ) + (place * dims.rows + r)
                    value = values[l, THERMAL] * hash_uniform(within + line * dims.width * HASH_A)
                    noise[c, l, r] = value
                    h += value
                else:
                    h += noise[c, l, r]
                heff[c, l, r] = h
        return carry

    lax.fori_loop(0, dims.layers, body, 0)


def true_bounds(dims, groups, own, others, rows, start, bound, edge):
    group = lax.axis_index("depth")
    for g in range(dims.depth):

        @pl.when(group == g)
        def _():
            def message(h):
                return own if h == g else others[(g - h) % dims.depth - 1]

            for r in rows:
                at = start + r
                ys = {}
                for h in range(1, dims.depth):
                    ys[h] = [message(h - 1)[c, at] for c in range(3)]
                    if h > 1:
                        ys[h] = add(ys[h], matvec(table(groups, h - 1, LAST_Y), ys[h - 1]))
                s = None
                for h in range(dims.depth - 1, g, -1):
                    value = [message(h)[3 + c, at] for c in range(3)]
                    value = add(value, matvec(table(groups, h, FIRST_Y), ys[h]))
                    if s is not None:
                        value = add(value, matvec(table(groups, h, FIRST_S), s))
                    s = value
                zero = jnp.zeros(dims.tile, F32)
                above = 9 if dims.depth == 2 else 6
                for c in range(3):
                    bound[c, r] = zero if g == 0 else ys[g][c]
                    bound[3 + c, r] = zero if s is None else s[c]
                    edge[c, r] = zero if g == 0 else others[0][6 + c, at]
                    edge[3 + c, r] = (
                        zero if g == dims.depth - 1 else others[dims.depth - 2][above + c, at]
                    )


def finish_kernel(dims, first, upper_half, parts, *refs):
    field, refs = refs[:parts], refs[parts:]
    maskf, heff, halo, own, *refs = refs
    others, refs = refs[: dims.depth - 1], refs[dims.depth - 1 :]
    coefs, groups, values, *refs = refs
    count = dims.rows // 2
    start = count if upper_half else 0
    rows = range(count)
    if first and upper_half:
        mate, middle, base, local, out_halo, *messages, bound, edge = refs
    elif first:
        middle, base, local, out_halo, ends, bound, edge = refs
    elif upper_half:
        base, local, result, accum, bound, edge = refs
    else:
        base, local, *mates, result_out, accum_out, bound, edge, result, accum, sems = refs
        pairs = ((result, result_out), (accum, accum_out))
    true_bounds(dims, groups, own, others, rows, start, bound, edge)

    def body(l, prev):
        stiff = values[l, STIFF]
        near, far = stiff * NEAR, stiff * FAR
        alpha = values[l, DAMP]
        scale = values[l, SCALE]
        down = jnp.where(l == 0, 0.5, 0.0) * stiff
        up = jnp.where(l == dims.layers - 1, 0.5, 0.0) * stiff
        done = []
        for r in rows:
            at = start + r
            v = [pick(field, c, l, at) for c in range(3)]
            h = [heff[c, l, at] for c in range(3)]
            y = [bound[c, r] for c in range(3)]
            s = [bound[3 + c, r] for c in range(3)]
            fix = add(matvec(table(coefs, l, FROM_Y), y), matvec(table(coefs, l, FROM_S), s))
            for c in range(3):
                for step, weight in ((1, near), (2, far)):
                    if at - step < 0:
                        h[c] += weight * halo[c, l, at - step + HALO]
                    if at + step >= dims.rows:
                        h[c] += weight * halo[c, l, at + step - dims.rows]
                h[c] += down * edge[c, r] + up * edge[3 + c, r] + 0.5 * fix[c]
            torque = cross(v, h)
            twice = cross(v, torque)
            mask_row = maskf[at]
            gain = scale * mask_row
            rate = [(torque[c] + alpha * twice[c]) * gain for c in range(3)]
            if first:
                m1 = unit([v[c] - 0.03 * rate[c] for c in range(3)])
                edge_row = at - (dims.rows - HALO) if upper_half else at
                for c in range(3):
                    middle[c, l, r] = m1[c]
                    base[c, l, r] = v[c] - 0.015 * rate[c]
                    if 0 <= edge_row < HALO:
                        out_halo[c, l, edge_row] = m1[c] * mask_row
                y = matvec(table(coefs, l, PIVOT_SOURCE), m1)
                drop = matvec(table(coefs, l, PIVOT_LOWER), prev[r])
                y = [a - b for a, b in zip(y, drop)]
                for c in range(3):
                    local[c, l, r] = y[c]
                done.append(y)
            else:
                new = unit([base[c, l, r] - 0.015 * rate[c] for c in range(3)])
                for c in range(3):
                    spin = local[c, l, r] + fix[c]
                    if upper_half:
                        result[c, l, r] = new[c]
                        accum[c, l, r] = spin
                    else:
                        result[cells(dims, c, l, r), :] = new[c]
                        accum[cells(dims, c, l, r), :] = spin
                        result[cells(dims, c, l, r + count), :] = mates[0][c, l, r]
                        accum[cells(dims, c, l, r + count), :] = mates[1][c, l, r]
        if not first and not upper_half:
            for k, (src, dst) in enumerate(pairs):
                for c in range(3):
                    lines = dims.chunks * dims.rows
                    where = pl.ds((c * dims.layers + l) * lines, lines)
                    pltpu.make_async_copy(src.at[where], dst.at[where], sems.at[k]).start()
        return done

    if not first:
        loop(dims.layers, lambda l, carry: (body(l, None), carry)[1], 0)
        if not upper_half:
            for k, (src, dst) in enumerate(pairs):
                pltpu.make_async_copy(src, dst, sems.at[k]).wait()
        return
    zero = [[jnp.zeros(dims.tile, F32)] * 3 for _ in rows]
    last = loop(dims.layers, body, zero)
    head = sweep_back(dims, local, lambda l: table(coefs, l, UPPER), rows)
    for r in rows:
        sent = [last[r][c] for c in range(3)] + [head[r][c] for c in range(3)]
        for l in (dims.layers - 1, 0):
            sent += [middle[c, l, r] * maskf[start + r] for c in range(3)]
        if not upper_half:
            for p in range(12):
                ends[p, r] = sent[p]
            continue
        for k, message in enumerate(messages, 1):
            at = 0
            for part in message_parts(dims, k):
                for p in part:
                    message[at, r] = mate[p, r]
                    message[at, start + r] = sent[p]
                    at += 1


def call(kernel, outs, args, scratch=(), ins=vmem, results=vmem):
    return pl.pallas_call(
        kernel,
        out_shape=outs,
        in_specs=[ins()] * len(args),
        out_specs=[results()] * len(outs),
        scratch_shapes=list(scratch),
        compiler_params=pltpu.CompilerParams(vmem_limit_bytes=VMEM_LIMIT),
        cost_estimate=pl.CostEstimate(flops=1000000, bytes_accessed=1000000, transcendentals=0),
    )(*args)


def ring(count, step):
    return [(i, (i + step) % count) for i in range(count)]


def local(
    magnet,
    mask,
    materials,
    exchange_strength,
    anisotropy,
    damping,
    source_strength,
    thermal_strength,
    pivots,
    lower,
    upper,
    noise_stream,
    counter,
):
    dims = Dims(
        magnet.shape[1],
        magnet.shape[2],
        magnet.shape[3],
        lax.axis_size("depth"),
        lax.axis_size("plane"),
    )
    lines = (3, dims.layers, dims.rows, dims.chunks, LANES)
    view = magnet.reshape(lines).transpose(0, 1, 3, 2, 4).reshape(-1, LANES)
    mask_view = mask.reshape(lines[2:]).transpose(1, 0, 2).reshape(-1, LANES)
    halo = shape(3, dims.layers, HALO, *dims.tile)
    field = shape(*dims.field())
    half = shape(3, dims.layers, dims.rows // 2, *dims.tile)
    blocks = [values.transpose(1, 2, 0) for values in (pivots, lower, upper)]
    bounds = [pltpu.VMEM((6, dims.rows // 2) + dims.tile, F32)] * 2
    padded = [pltpu.VMEM((3, dims.layers + 2, dims.rows) + dims.tile, F32)]
    messages = [
        shape(sum(len(part) for part in message_parts(dims, k)), dims.rows, *dims.tile)
        for k in range(1, dims.depth)
    ]

    def forward(values):
        return lax.ppermute(values, "plane", ring(dims.plane, 1))

    def backward(values):
        return lax.ppermute(values, "plane", ring(dims.plane, -1))

    def swap_depth(sent):
        return [
            lax.ppermute(message, "depth", ring(dims.depth, k)) for k, message in enumerate(sent, 1)
        ]

    def local_field(first, fields, solved, extra, outs):
        kernel = functools.partial(local_kernel, dims, first, len(fields))
        return call(kernel, outs, (*fields, *solved, maskf, values, *extra), padded)

    def finish(first, upper_half, fields, heff, rows, own, others, extra, outs, *rest):
        kernel = functools.partial(finish_kernel, dims, first, upper_half, len(fields))
        args = (*fields, maskf, heff, rows, own, *others, coefs, groups, values, *extra)
        return call(kernel, outs, args, bounds + list(rest[:1] and rest[0]), *rest[1:])

    inputs = (view, mask_view, materials, source_strength, *blocks)
    seed = jnp.full(dims.tile, noise_stream[0] * HASH_B + counter[0] * HASH_C, jnp.int32)
    constants = (
        materials,
        exchange_strength,
        anisotropy,
        damping,
        source_strength,
        thermal_strength,
        *blocks,
    )
    inputs = [pltpu.with_memory_space_constraint(x, pltpu.HBM) for x in inputs]
    constants = [pltpu.with_memory_space_constraint(x, pltpu.HBM) for x in constants]
    spaces = [pltpu.VMEM] * 2 + [pltpu.SMEM] * 5
    held = [space(x.shape, x.dtype) for space, x in zip(spaces, inputs)]
    tiles, maskf, low, high, solved, *sent = call(
        functools.partial(enter_kernel, dims),
        [
            field,
            shape(dims.rows, *dims.tile),
            halo,
            halo,
            field,
        ]
        + messages,
        inputs,
        held + [pltpu.SemaphoreType.DMA((len(inputs),))],
        hbm,
    )
    before = forward(high)
    others = swap_depth(sent)
    after = backward(low)
    coefs, groups, values = call(
        functools.partial(coefficient_kernel, dims),
        [
            shape(dims.layers, LAYER_COEFS, *dims.tile),
            shape(dims.depth, GROUP_COEFS, *dims.tile),
            shape(dims.layers, LAYER_VALUES, *dims.tile),
        ],
        constants,
        [pltpu.VMEM((dims.depth, dims.layers, 3) + dims.tile, F32)]
        + [pltpu.SMEM(x.shape, x.dtype) for x in constants]
        + [pltpu.SemaphoreType.DMA((len(constants),))],
        hbm,
    )
    heff, noise = local_field(True, [tiles], [solved], (seed,), [field, field])
    middle_low, base_low, solved_low, low, ends = finish(
        True,
        False,
        [tiles],
        heff,
        before,
        sent[0],
        others,
        (),
        [half, half, half, halo, shape(12, dims.rows // 2, *dims.tile)],
    )
    next_after = backward(low)
    middle_high, base_high, solved_high, high, *sent2 = finish(
        True,
        True,
        [tiles],
        heff,
        after,
        sent[0],
        others,
        (ends,),
        [half, half, half, halo] + messages,
    )
    next_before = forward(high)
    others2 = swap_depth(sent2)
    middle = [middle_low, middle_high]
    (heff2,) = local_field(False, middle, [solved_low, solved_high], (noise,), [field])
    new_high = finish(
        False,
        True,
        middle,
        heff2,
        next_after,
        sent2[0],
        others2,
        (base_high, solved_high),
        [half, half],
    )
    lined = shape(*view.shape)
    result, accum = finish(
        False,
        False,
        middle,
        heff2,
        next_before,
        sent2[0],
        others2,
        (base_low, solved_low, *new_high),
        [lined, lined],
        [pltpu.VMEM(view.shape, F32)] * 2 + [pltpu.SemaphoreType.DMA((2,))],
        vmem,
        hbm,
    )

    def whole(lines_view):
        cut = lines_view.reshape(3, dims.layers, dims.chunks, dims.rows, LANES)
        return cut.transpose(0, 1, 3, 2, 4).reshape(magnet.shape)

    return whole(result), whole(accum)


def solution(mesh):
    placed = (
        P(None, "depth", "plane", None),
        P("plane", None),
        P("depth"),
    ) + (P(),) * 10
    return jax.shard_map(
        local,
        mesh=mesh,
        in_specs=placed,
        out_specs=(P(None, "depth", "plane", None), P(None, "depth", "plane", None)),
        check_vma=False,
    )
```

time: 37.4 us -> 30.4 us (0.81)
  local copies, waits for them, and re-layouts: 3.16 us -> 0.01 us
  Pallas kernels: 12 us -> 9.06 us
  starting transfers between devices: 14.7 us -> 13.1 us
  waiting for transfers between devices: 5.3 us -> 6.04 us
    unnamed x26 -> x0, local copies, waits for them, and re-layouts: 3.16 us -> none
    pallas_call x8, Pallas kernels: 12 us -> 9.06 us  [call(): pl.pallas_call(kernel, out_shape=outs, in_specs=[ins()] * len(args), out_...]
    ppermute x4, starting transfers between devices: 10.9 us -> 9.03 us  [the longest x2 5.95 us: backward(): return lax.ppermute(values, 'plane', ring(dims.plane, -1))]
    ppermute x6, waiting for transfers between devices: 5.29 us -> 5.8 us  [swap_depth(): lax.ppermute(message, 'depth', ring(dims.depth, k))]
  transfers between devices with their start and end apart: 10 -> 10, of which waited for: 2 -> 3; matrix products, arithmetic and copies ran while one was open for 0% -> 0% of each run, Pallas kernels for 22% -> 21%
where the time goes in v3:
time: 30.4 us; the launch traced here: 30.2 us
  starting transfers between devices  13.1 us (43%)
  Pallas kernels  9.06 us (30%)
  waiting for transfers between devices  6.04 us (20%)
  between operations  2.02 us (7%)
    pallas_call x8, Pallas kernels, call(): pl.pallas_call(kernel, out_shape=outs, in_specs=[ins()] * len(args), out_...  9.06 us
    ppermute x2, starting transfers between devices, backward(): return lax.ppermute(values, 'plane', ring(dims.plane, -1))  5.95 us
    ppermute x6, waiting for transfers between devices, swap_depth(): lax.ppermute(message, 'depth', ring(dims.depth, k))  5.8 us
    ppermute x6, starting transfers between devices, swap_depth(): lax.ppermute(message, 'depth', ring(dims.depth, k))  4.09 us
    ppermute x2, starting transfers between devices, forward(): return lax.ppermute(values, 'plane', ring(dims.plane, 1))  3.08 us
  transfers between devices with their start and end apart: 10, of which 3 were waited for; matrix products, arithmetic and copies ran while one was open for 0% of the time, Pallas kernels for 21%

profile of v3, /device:TPU:0, one launch (start us, length us, event | category | flops | bytes accessed | tf_op | source)
XLA Modules:
  0.0 30.2 jit_solution(1259958286290823268)
XLA Ops:
  0.6 1.7 %shard_map.140 = (f32[3,8,4,8,128]{4,3,2,1,0:T(8,128)S(1)}, f32[4,8,128]{2,1,0:T(8,128)S(1)}, f32[3,8,2,8,128]{4,3,2,1,0:T(8,128)S(1)}, f32[3,8,2,8,128]{4,3,2,1...) custom-call(f32[768,128]{1,0:T(8,128)} %bitcast.24, ...), custom_call_target="tpu_custom_call" | custom-call | flops 1000000 | bytes 1000000 | tf_op jit(solution)/shard_map/pallas_call | solution.py:485
  2.4 3.0 %collective-permute-start = (f32[3,8,2,8,128]{4,3,2,1,0:T(8,128)S(1)}, f32[3,8,2,8,128]{4,3,2,1,0:T(8,128)S(1)}, u32[]{:S(2)}, u32[]{:S(2)}) collective-permute-start(f32[3,8,2,8,128]{4,3,2,1,0:T(8,128)S(1)} %get-tuple-element.36), channel_id=1, source_target_pairs={{0,1},{1,2},{2,3},{3,4},{4,5},{5,6},{6,7},{7,0},{8,9},{9,10},{10,1... | collective-permute-start | bytes 589832 | tf_op jit(solution)/shard_map/ppermute | solution.py:537
  5.4 3.1 %collective-permute-start.4 = (f32[3,8,2,8,128]{4,3,2,1,0:T(8,128)S(1)}, f32[3,8,2,8,128]{4,3,2,1,0:T(8,128)S(1)}, u32[]{:S(2)}, u32[]{:S(2)}) collective-permute-start(f32[3,8,2,8,128]{4,3,2,1,0:T(8,128)S(1)} %get-tuple-element.43), channel_id=1, source_target_pairs={{0,7},{1,0},{2,1},{3,2},{4,3},{5,4},{6,5},{7,6},{8,15},{9,8},{10,9... | collective-permute-start | bytes 589832 | tf_op jit(solution)/shard_map/ppermute | solution.py:540
  8.5 0.7 %collective-permute-start.3 = (f32[9,4,8,128]{3,2,1,0:T(8,128)S(1)}, f32[9,4,8,128]{3,2,1,0:T(8,128)S(1)}, u32[]{:S(2)}, u32[]{:S(2)}) collective-permute-start(f32[9,4,8,128]{3,2,1,0:T(8,128)S(1)} %get-tuple-element.39), channel_id=1, source_target_pairs={{0,24},{8,0},{16,8},{24,16},{1,25},{9,1},{17,9},{25,17},{2,26},{10... | collective-permute-start | bytes 442376 | tf_op jit(solution)/shard_map/ppermute | solution.py:544
  9.1 0.0 collective-permute-start.1
  9.1 1.4 %collective-permute-start.2 = (f32[6,4,8,128]{3,2,1,0:T(8,128)S(1)}, f32[6,4,8,128]{3,2,1,0:T(8,128)S(1)}, u32[]{:S(2)}, u32[]{:S(2)}) collective-permute-start(f32[6,4,8,128]{3,2,1,0:T(8,128)S(1)} %get-tuple-element.38), channel_id=1, source_target_pairs={{0,16},{8,24},{16,0},{24,8},{1,17},{9,25},{17,1},{25,9},{2,18},{10... | collective-permute-start | bytes 294920 | tf_op jit(solution)/shard_map/ppermute | solution.py:544
  11.9 2.8 %shard_map.141 = (f32[8,45,8,128]{3,2,1,0:T(8,128)S(1)}, f32[4,27,8,128]{3,2,1,0:T(8,128)S(1)}, f32[8,5,8,128]{3,2,1,0:T(8,128)S(1)}) custom-call(s32[8]{0:T(128)} %refs_0_.1, f32[4]{0:T(128)} %refs_1_.1, f32[4]{0:T(128)} %refs_2_.3, f32[4]{0:T(128)} %refs_3_.3, f32[4]{0:T(128)} %refs_4_.1, f32[4]{0:T(128)} %refs_5_.1, f32[3,3,32]{2,1,0:T(4,128)} %bitcast.26, ...), custom_call_target="tpu_custom_call" | custom-call | flops 1000000 | bytes 1000000 | tf_op jit(solution)/shard_map/pallas_call | solution.py:485
  14.7 1.1 %shard_map.142 = (f32[3,8,4,8,128]{4,3,2,1,0:T(8,128)S(1)}, f32[3,8,4,8,128]{4,3,2,1,0:T(8,128)S(1)}) custom-call(f32[3,8,4,8,128]{4,3,2,1,0:T(8,128)S(1)} %get-tuple-element.31.refs_0_, f32[3,8,4,8,128]{4,3,2,1,0:T(8,128)S(1)} %get-tuple-element.33.refs_1_, f32[4,8,128]{2,1,0:T(8,128)S(1)} %get-tuple-element.32.refs_2_.refs_1_.refs_4_, ...), custom_call_target="tpu_custom_call" | custom-call | flops 1000000 | bytes 1000000 | tf_op jit(solution)/shard_map/pallas_call | solution.py:485
  15.8 0.7 %collective-permute-done.2.refs_6_ = f32[6,4,8,128]{3,2,1,0:T(8,128)S(1)} collective-permute-done((f32[6,4,8,128]{3,2,1,0:T(8,128)S(1)}, f32[6,4,8,128]{3,2,1,0:T(8,128)S(1)}, u32[]{:S(2)}, u32[]{:S(2)}) %collective-permute-start.2) | collective-permute-done | bytes 98336 | tf_op jit(solution)/shard_map/ppermute | solution.py:544
  16.4 0.0 collective-permute-done.3.refs_7_
  16.4 0.0 collective-permute-done.1.refs_5_
  16.5 0.0 collective-permute-done.refs_3_
  16.5 0.5 %shard_map.143 = (f32[3,8,2,8,128]{4,3,2,1,0:T(8,128)S(1)}, f32[3,8,2,8,128]{4,3,2,1,0:T(8,128)S(1)}, f32[3,8,2,8,128]{4,3,2,1,0:T(8,128)S(1)}, f32[3,8,2,8,128]{4,3,2,1,0:T(8,128)S(1)}, f32[12,2,8,128]{3,2,1,0:T(8,128)S(1)}) custom-call(f32[3,8,4,8,128]{4,3,2,1,0:T(8,128)S(1)} %get-tuple-element.31.refs_0_, ...), custom_call_target="tpu_custom_call" | custom-call | flops 1000000 | bytes 1000000 | tf_op jit(solution)/shard_map/pallas_call | solution.py:485
  17.0 2.9 %collective-permute-start.9 = (f32[3,8,2,8,128]{4,3,2,1,0:T(8,128)S(1)}, f32[3,8,2,8,128]{4,3,2,1,0:T(8,128)S(1)}, u32[]{:S(2)}, u32[]{:S(2)}) collective-permute-start(f32[3,8,2,8,128]{4,3,2,1,0:T(8,128)S(1)} %get-tuple-element.54), channel_id=1, source_target_pairs={{0,7},{1,0},{2,1},{3,2},{4,3},{5,4},{6,5},{7,6},{8,15},{9,8},{10,9... | collective-permute-start | bytes 589832 | tf_op jit(solution)/shard_map/ppermute | solution.py:540
  19.8 0.0 collective-permute-done.4.refs_3_
  19.8 0.5 %shard_map.144 = (f32[3,8,2,8,128]{4,3,2,1,0:T(8,128)S(1)}, f32[3,8,2,8,128]{4,3,2,1,0:T(8,128)S(1)}, f32[3,8,2,8,128]{4,3,2,1,0:T(8,128)S(1)}, f32[3,8,2,8,128]...) custom-call(f32[3,8,4,8,128]{4,3,2,1,0:T(8,128)S(1)} %get-tuple-elem, ...), custom_call_target="tpu_custom_call" | custom-call | flops 1000000 | bytes 1000000 | tf_op jit(solution)/shard_map/pallas_call | solution.py:485
  20.3 0.1 collective-permute-start.5
  20.4 0.1 collective-permute-start.8
  20.5 0.5 %collective-permute-start.6 = (f32[9,4,8,128]{3,2,1,0:T(8,128)S(1)}, f32[9,4,8,128]{3,2,1,0:T(8,128)S(1)}, u32[]{:S(2)}, u32[]{:S(2)}) collective-permute-start(f32[9,4,8,128]{3,2,1,0:T(8,128)S(1)} %get-tuple-element.50.refs_5_), channel_id=1, source_target_pairs={{0,8},{8,16},{16,24},{24,0},{1,9},{9,17},{17,25},{25,1},{2,10},{10... | collective-permute-start | bytes 442376 | tf_op jit(solution)/shard_map/ppermute | solution.py:544
  21.0 1.4 %collective-permute-start.7 = (f32[6,4,8,128]{3,2,1,0:T(8,128)S(1)}, f32[6,4,8,128]{3,2,1,0:T(8,128)S(1)}, u32[]{:S(2)}, u32[]{:S(2)}) collective-permute-start(f32[6,4,8,128]{3,2,1,0:T(8,128)S(1)} %get-tuple-element.51), channel_id=1, source_target_pairs={{0,16},{8,24},{16,0},{24,8},{1,17},{9,25},{17,1},{25,9},{2,18},{10... | collective-permute-start | bytes 294920 | tf_op jit(solution)/shard_map/ppermute | solution.py:544
  22.4 1.1 %shard_map.145.refs_3_ = f32[3,8,4,8,128]{4,3,2,1,0:T(8,128)S(1)} custom-call(f32[3,8,2,8,128]{4,3,2,1,0:T(8,128)S(1)} %get-tuple-element.42.refs_0_, f32[3,8,2,8,128]{4,3,2,1,0:T(8,128)S(1)} %get-tuple-element.45.refs_1_, f32[3,8,2,8,128]{4,3,2,1,0:T(8,128)S(1)} %get-tuple-element.46.refs_2_.refs_13_, ...), custom_call_target="tpu_custom_call" | custom-call | flops 1000000 | bytes 1000000 | tf_op jit(solution)/shard_map/pallas_call | solution.py:485
  23.5 5.1 %collective-permute-done.7.refs_7_ = f32[6,4,8,128]{3,2,1,0:T(8,128)S(1)} collective-permute-done((f32[6,4,8,128]{3,2,1,0:T(8,128)S(1)}, f32[6,4,8,128]{3,2,1,0:T(8,128)S(1)}, u32[]{:S(2)}, u32[]{:S(2)}) %collective-permute-start.7) | collective-permute-done | bytes 98336 | tf_op jit(solution)/shard_map/ppermute | solution.py:544
  28.6 0.0 collective-permute-done.8.refs_8_
  28.6 0.0 collective-permute-done.6.refs_6_
  28.6 0.0 collective-permute-done.9.refs_4_
  28.6 0.3 %shard_map.146 = (f32[3,8,2,8,128]{4,3,2,1,0:T(8,128)S(1)}, f32[3,8,2,8,128]{4,3,2,1,0:T(8,128)S(1)}) custom-call(f32[3,8,2,8,128]{4,3,2,1,0:T(8,128)S(1)} %get-tuple-element.42.refs_0_, f32[3,8,2,8,128]{4,3,2,1,0:T(8,128)S(1)} %get-tuple-element.45.refs_1_, f32[4,8,128]{2,1,0:T(8,128)S(1)} %get-tuple-element.32.refs_2_.refs_1_.refs_4_, ...), custom_call_target="tpu_custom_call" | custom-call | flops 1000000 | bytes 1000000 | tf_op jit(solution)/shard_map/pallas_call | solution.py:485
  29.0 0.2 collective-permute-done.5.refs_4_
  29.2 1.0 %shard_map.147 = (f32[768,128]{1,0:T(8,128)}, f32[768,128]{1,0:T(8,128)}) custom-call(f32[3,8,2,8,128]{4,3,2,1,0:T(8,128)S(1)} %get-tuple-element.42.refs_0_, f32[3,8,2,8,128]{4,3,2,1,0:T(8,128)S(1)} %get-tuple-element.45.refs_1_, f32[4,8,128]{2,1,0:T(8,128)S(1)} %get-tuple-element.32.refs_2_.refs_1_.refs_4_, f32[3,8,4,8,128]{4,3,2,1,0:T(8,128)S(1)} %shard_map.145.refs_3_, ...), custom_call_target="tpu_custom_call" | custom-call | flops 1000000 | bytes 1000000 | tf_op jit(solution)/shard_map/pallas_call | solution.py:485
  (1 shorter events, 0.0 us)
Async XLA Ops:
  2.4 14.1 %collective-permute-start = (f32[3,8,2,8,128]{4,3,2,1,0:T(8,128)S(1)}, f32[3,8,2,8,128]{4,3,2,1,0:T(8,128)S(1)}, u32[]{:S(2)}, u32[]{:S(2)}) collective-permute-start(f32[3,8,2,8,128]{4,3,2,1,0:T(8,128)S(1)} %get-tuple-element.36), channel_id=1, source_target_pairs={{0,1},{1,2},{2,3},{3,4},{4,5},{5,6},{6,7},{7,0},{8,9},{9,10},{10,1... | collective-permute-start | bytes 589832 | tf_op jit(solution)/shard_map/ppermute | solution.py:537
  5.4 14.4 %collective-permute-start.4 = (f32[3,8,2,8,128]{4,3,2,1,0:T(8,128)S(1)}, f32[3,8,2,8,128]{4,3,2,1,0:T(8,128)S(1)}, u32[]{:S(2)}, u32[]{:S(2)}) collective-permute-start(f32[3,8,2,8,128]{4,3,2,1,0:T(8,128)S(1)} %get-tuple-element.43), channel_id=1, source_target_pairs={{0,7},{1,0},{2,1},{3,2},{4,3},{5,4},{6,5},{7,6},{8,15},{9,8},{10,9... | collective-permute-start | bytes 589832 | tf_op jit(solution)/shard_map/ppermute | solution.py:540
  8.5 8.0 %collective-permute-start.3 = (f32[9,4,8,128]{3,2,1,0:T(8,128)S(1)}, f32[9,4,8,128]{3,2,1,0:T(8,128)S(1)}, u32[]{:S(2)}, u32[]{:S(2)}) collective-permute-start(f32[9,4,8,128]{3,2,1,0:T(8,128)S(1)} %get-tuple-element.39), channel_id=1, source_target_pairs={{0,24},{8,0},{16,8},{24,16},{1,25},{9,1},{17,9},{25,17},{2,26},{10... | collective-permute-start | bytes 442376 | tf_op jit(solution)/shard_map/ppermute | solution.py:544
  9.1 7.3 %collective-permute-start.1 = (f32[9,4,8,128]{3,2,1,0:T(8,128)S(1)}, f32[9,4,8,128]{3,2,1,0:T(8,128)S(1)}, u32[]{:S(2)}, u32[]{:S(2)}) collective-permute-start(f32[9,4,8,128]{3,2,1,0:T(8,128)S(1)} %get-tuple-element.37.refs_4_), channel_id=1, source_target_pairs={{0,8},{8,16},{16,24},{24,0},{1,9},{9,17},{17,25},{25,1},{2,10},{10... | collective-permute-start | bytes 442376 | tf_op jit(solution)/shard_map/ppermute | solution.py:544
  9.1 7.3 %collective-permute-start.2 = (f32[6,4,8,128]{3,2,1,0:T(8,128)S(1)}, f32[6,4,8,128]{3,2,1,0:T(8,128)S(1)}, u32[]{:S(2)}, u32[]{:S(2)}) collective-permute-start(f32[6,4,8,128]{3,2,1,0:T(8,128)S(1)} %get-tuple-element.38), channel_id=1, source_target_pairs={{0,16},{8,24},{16,0},{24,8},{1,17},{9,25},{17,1},{25,9},{2,18},{10... | collective-permute-start | bytes 294920 | tf_op jit(solution)/shard_map/ppermute | solution.py:544
  17.0 11.7 %collective-permute-start.9 = (f32[3,8,2,8,128]{4,3,2,1,0:T(8,128)S(1)}, f32[3,8,2,8,128]{4,3,2,1,0:T(8,128)S(1)}, u32[]{:S(2)}, u32[]{:S(2)}) collective-permute-start(f32[3,8,2,8,128]{4,3,2,1,0:T(8,128)S(1)} %get-tuple-element.54), channel_id=1, source_target_pairs={{0,7},{1,0},{2,1},{3,2},{4,3},{5,4},{6,5},{7,6},{8,15},{9,8},{10,9... | collective-permute-start | bytes 589832 | tf_op jit(solution)/shard_map/ppermute | solution.py:540
  20.3 8.9 %collective-permute-start.5 = (f32[3,8,2,8,128]{4,3,2,1,0:T(8,128)S(1)}, f32[3,8,2,8,128]{4,3,2,1,0:T(8,128)S(1)}, u32[]{:S(2)}, u32[]{:S(2)}) collective-permute-start(f32[3,8,2,8,128]{4,3,2,1,0:T(8,128)S(1)} %get-tuple-element.49), channel_id=1, source_target_pairs={{0,1},{1,2},{2,3},{3,4},{4,5},{5,6},{6,7},{7,0},{8,9},{9,10},{10,1... | collective-permute-start | bytes 589832 | tf_op jit(solution)/shard_map/ppermute | solution.py:537
  20.4 8.2 %collective-permute-start.8 = (f32[9,4,8,128]{3,2,1,0:T(8,128)S(1)}, f32[9,4,8,128]{3,2,1,0:T(8,128)S(1)}, u32[]{:S(2)}, u32[]{:S(2)}) collective-permute-start(f32[9,4,8,128]{3,2,1,0:T(8,128)S(1)} %get-tuple-element.52), channel_id=1, source_target_pairs={{0,24},{8,0},{16,8},{24,16},{1,25},{9,1},{17,9},{25,17},{2,26},{10... | collective-permute-start | bytes 442376 | tf_op jit(solution)/shard_map/ppermute | solution.py:544
  20.5 8.2 %collective-permute-start.6 = (f32[9,4,8,128]{3,2,1,0:T(8,128)S(1)}, f32[9,4,8,128]{3,2,1,0:T(8,128)S(1)}, u32[]{:S(2)}, u32[]{:S(2)}) collective-permute-start(f32[9,4,8,128]{3,2,1,0:T(8,128)S(1)} %get-tuple-element.50.refs_5_), channel_id=1, source_target_pairs={{0,8},{8,16},{16,24},{24,0},{1,9},{9,17},{17,25},{25,1},{2,10},{10... | collective-permute-start | bytes 442376 | tf_op jit(solution)/shard_map/ppermute | solution.py:544
  21.0 7.6 %collective-permute-start.7 = (f32[6,4,8,128]{3,2,1,0:T(8,128)S(1)}, f32[6,4,8,128]{3,2,1,0:T(8,128)S(1)}, u32[]{:S(2)}, u32[]{:S(2)}) collective-permute-start(f32[6,4,8,128]{3,2,1,0:T(8,128)S(1)} %get-tuple-element.51), channel_id=1, source_target_pairs={{0,16},{8,24},{16,0},{24,8},{1,17},{9,25},{17,1},{25,9},{2,18},{10... | collective-permute-start | bytes 294920 | tf_op jit(solution)/shard_map/ppermute | solution.py:544

commit v4 on v3

v4 whole, which is shorter than its diff:
```python
import functools

import jax
import jax.numpy as jnp
from jax import lax
from jax.experimental import pallas as pl
from jax.experimental.pallas import tpu as pltpu
from jax.sharding import PartitionSpec as P

LANES = 128
NEAR = 4.0 / 3.0
FAR = -1.0 / 12.0
HALO = 2
VMEM_LIMIT = 16 * 1024 * 1024
UNROLL = 4
F32 = jnp.float32


def wrapped(value):
    value &= 0xFFFFFFFF
    return value - (1 << 32) if value >= (1 << 31) else value


HASH_A = wrapped(739982445)
HASH_B = wrapped(695872825)
HASH_C = wrapped(1597334677)


class Dims:
    def __init__(self, layers, rows, width, depth, plane):
        self.layers = layers
        self.rows = rows
        self.width = width
        self.chunks = width // LANES
        self.depth = depth
        self.plane = plane
        self.tile = (self.chunks, LANES)

    def field(self):
        return (3, self.layers, self.rows) + self.tile


def shape(*dims):
    return jax.ShapeDtypeStruct(dims, F32)


def vmem():
    return pl.BlockSpec(memory_space=pltpu.VMEM)


def hbm():
    return pl.BlockSpec(memory_space=pltpu.HBM)


def turned(dims, position):
    odd = lax.axis_index("plane") % 2 == 1
    return jnp.where(odd, dims.rows - 1 - position, position)


def cells(dims, comp, layer, row):
    base = (comp * dims.layers + layer) * (dims.chunks * dims.rows) + row
    return pl.ds(base, dims.chunks, stride=dims.rows)


def matvec(get, vec):
    return [get(i, 0) * vec[0] + get(i, 1) * vec[1] + get(i, 2) * vec[2] for i in range(3)]


def add(a, b):
    return [x + y for x, y in zip(a, b)]


def cross(a, b):
    return [
        a[1] * b[2] - a[2] * b[1],
        a[2] * b[0] - a[0] * b[2],
        a[0] * b[1] - a[1] * b[0],
    ]


def unit(vec):
    scale = lax.rsqrt(vec[0] * vec[0] + vec[1] * vec[1] + vec[2] * vec[2])
    return [v * scale for v in vec]


PIVOT, LOWER, UPPER, BLOCK_COEFS = 0, 9, 18, 27
PIVOT_SOURCE, PIVOT_LOWER, FROM_Y, FROM_S, LAYER_COEFS = 0, 9, 18, 27, 36
STIFF, ANISO, DAMP, THERMAL, SCALE, SOURCE, LAYER_VALUES = 0, 1, 2, 3, 4, 5, 6
LAST, FIRST, TOP, BOTTOM, PARTS = 0, 3, 6, 9, 12
LAST_Y, FIRST_Y, FIRST_S, THROUGH, ECHO, LINKS = 0, 9, 18, 27, 36, 45
SECOND = 8
GROUPS = 4


def table(ref, at, first):
    return lambda i, j: ref[at, first + 3 * i + j]


def column(value, j):
    return jnp.broadcast_to(value[:, j : j + 1], value.shape)


def columns(values, first):
    return [[column(values[i], first + j) for j in range(3)] for i in range(3)]


def entries(matrix):
    return lambda i, j: matrix[i][j]


def entries_by_column(matrix):
    return lambda i, j: matrix[j][i]


def sweep_back(dims, lines, upper, start):
    def backward(k, after):
        l = dims.layers - 1 - k
        done = []
        for (ref, r), s in zip(lines, after):
            up = matvec(upper(l), s)
            s = [ref[c, l, r] - up[c] for c in range(3)]
            for c in range(3):
                ref[c, l, r] = s[c]
            done.append(s)
        return done

    return loop(dims.layers, backward, start)


def loop(count, body, start):
    step = max(k for k in range(1, UNROLL + 1) if count % k == 0)

    def steps(k, carry):
        for i in range(step):
            carry = body(k * step + i, carry)
        return carry

    if step == count:
        return steps(0, start)
    return lax.fori_loop(0, count // step, steps, start)


def fetch(inputs, held, sems):
    copies = [
        pltpu.make_async_copy(src, dst, sems.at[k])
        for k, (src, dst) in enumerate(zip(inputs, held))
    ]
    for copy in copies:
        copy.start()
    for copy in copies:
        copy.wait()


def enter_kernel(dims, *refs):
    inputs, refs = refs[:11], refs[11:]
    field, maskf, near, blocks, values, *held, sems = refs
    fetch(inputs, held, sems)
    magnet, mask, materials, stiffness, anisotropy, damping, source, thermal, *matrices = held
    group = lax.axis_index("depth")
    rows = range(dims.rows)
    lines = [turned(dims, r) for r in rows]
    for r in rows:
        maskf[r] = mask[pl.ds(lines[r], dims.chunks, stride=dims.rows), :].astype(F32)

    def layer(l, carry):
        for r in rows:
            mask_row = maskf[r]
            for c in range(3):
                v = magnet[cells(dims, c, l, lines[r]), :]
                field[c, l, r] = v
                if r >= dims.rows - HALO:
                    near[c, l, dims.rows - 1 - r] = v * mask_row
        at = group * dims.layers + l
        material = materials[l]
        for k, ref in enumerate(matrices):
            for i in range(3):
                for j in range(3):
                    blocks[l, 9 * k + 3 * i + j] = jnp.full(dims.tile, ref[i, j, at], F32)
        alpha = jnp.full(dims.tile, damping[material], F32)
        values[l, DAMP] = alpha
        values[l, SCALE] = 1.0 / (1.0 + alpha * alpha)
        rest = ((STIFF, stiffness), (ANISO, anisotropy), (THERMAL, thermal), (SOURCE, source))
        for k, ref in rest:
            values[l, k] = jnp.full(dims.tile, ref[material], F32)
        return carry

    loop(dims.layers, layer, 0)


def sweep_kernel(dims, field, maskf, blocks, values, local, trail, message, far):
    rows = range(dims.rows)

    def forward(l, prev):
        beta = values[l, SOURCE]
        done = []
        for r in [*rows, None]:
            drop = matvec(table(blocks, l, LOWER), prev[len(done)])
            f = [-a for a in drop] if r is None else [beta * field[c, l, r] - drop[c] for c in range(3)]
            y = matvec(table(blocks, l, PIVOT), f)
            for c in range(3):
                if r is None:
                    trail[c, l, 0] = y[c]
                else:
                    local[c, l, r] = y[c]
                    if r < HALO:
                        far[c, l, r] = field[c, l, r] * maskf[r]
            done.append(y)
        return done

    zero = [[jnp.zeros(dims.tile, F32)] * 3 for _ in rows]
    lane = lax.broadcasted_iota(jnp.int32, dims.tile, 1)
    before, after = [[(lane == first + c).astype(F32) for c in range(3)] for first in (0, 3)]
    last = loop(dims.layers, forward, zero + [before])
    lines = [(local, r) for r in rows] + [(trail, 0)]
    first = sweep_back(dims, lines, lambda l: table(blocks, l, UPPER), zero + [after])
    for c in range(3):
        message[PARTS * dims.rows + LAST + c] = last[-1][c]
        message[PARTS * dims.rows + FIRST + c] = first[-1][c]
    for r in rows:
        sent = [last[r][c] for c in range(3)] + [first[r][c] for c in range(3)]
        for l in (dims.layers - 1, 0):
            sent += [field[c, l, r] * maskf[r] for c in range(3)]
        for p in range(PARTS):
            message[p * dims.rows + r] = sent[p]


def coefficient_kernel(dims, trail, blocks, values, coefs):
    def layer(l, carry):
        pivot, low = table(blocks, l, PIVOT), table(blocks, l, LOWER)
        beta = values[l, SOURCE]
        for i in range(3):
            for j in range(3):
                coefs[l, PIVOT_SOURCE + 3 * i + j] = pivot(i, j) * beta
                coefs[l, PIVOT_LOWER + 3 * i + j] = (
                    pivot(i, 0) * low(0, j) + pivot(i, 1) * low(1, j) + pivot(i, 2) * low(2, j)
                )
                coefs[l, FROM_Y + 3 * i + j] = column(trail[i, l, 0], j)
                coefs[l, FROM_S + 3 * i + j] = column(trail[i, l, 0], 3 + j)
        return carry

    loop(dims.layers, layer, 0)


def for_each_group(body):
    group = lax.axis_index("depth")
    for g in range(GROUPS):

        @pl.when(group == g)
        def _():
            body(g)


def getter(dims, ref):
    return lambda part, r: [ref[(part + c) * dims.rows + r] for c in range(3)]


def getter(dims, ref):
    return lambda part, r: [ref[(part + c) * dims.rows + r] for c in range(3)]


def spread(dims, ref):
    base = PARTS * dims.rows
    return lambda part: [ref[base + part + c] for c in range(3)]


def cross_kernel(dims, own, mate, out):
    def body(g):
        even, odd = (own, mate) if g % 2 == 0 else (mate, own)
        get_even, get_odd = getter(dims, even), getter(dims, odd)
        if g < 2:
            odd_y = entries(columns(spread(dims, odd)(LAST), 0))
        else:
            odd_first = entries(columns(spread(dims, odd)(FIRST), 0))
            even_s = entries(columns(spread(dims, even)(FIRST), 3))
        for r in range(dims.rows):
            if g < 2:
                value = add(get_odd(LAST, r), matvec(odd_y, get_even(LAST, r)))
                side = get_odd(TOP, r)
            else:
                value = add(get_odd(FIRST, r), matvec(odd_first, get_even(LAST, r)))
                value = add(get_even(FIRST, r), matvec(even_s, value))
                side = get_even(BOTTOM, r)
            for c in range(3):
                out[c * dims.rows + r] = value[c]
                out[(3 + c) * dims.rows + r] = side[c]
        lane = lax.broadcasted_iota(jnp.int32, dims.tile, 1)
        for part in (LAST, FIRST):
            pair = zip(spread(dims, even)(part), spread(dims, odd)(part))
            for c, (a, b) in enumerate(pair):
                both = jnp.where(lane < SECOND, a, pltpu.roll(b, SECOND, 1))
                out[6 * dims.rows + part + c] = both

    for_each_group(body)


def first_bound_kernel(dims, own, mate, cross, other, links, bound, edge):
    def body(g):
        base = 6 * dims.rows
        even, odd = (own, mate) if g % 2 == 0 else (mate, own)
        for pair, ref in enumerate((cross, other) if g < 2 else (other, cross)):
            for h in range(2):
                values = [[ref[base + part + c] for c in range(3)] for part in (LAST, FIRST)]
                matrices = (
                    (LAST_Y, columns(values[0], SECOND * h)),
                    (FIRST_Y, columns(values[1], SECOND * h)),
                    (FIRST_S, columns(values[1], SECOND * h + 3)),
                )
                for at, matrix in matrices:
                    for i in range(3):
                        for j in range(3):
                            links[2 * pair + h, at + 3 * i + j] = matrix[i][j]
        for h in range(GROUPS - 1, -1, -1):
            every = [[table(links, h, at)(i, j) for j in range(3) for i in range(3)] for at in (LAST_Y, FIRST_Y, FIRST_S)]
            last_y, through, first_s = [[m[3 * j : 3 * j + 3] for j in range(3)] for m in every]
            if h < GROUPS - 1:
                ahead = table(links, h + 1, THROUGH)
                echo = [matvec(entries_by_column(first_s), [ahead(i, j) for i in range(3)]) for j in range(3)]
                for j in range(3):
                    through[j] = add(through[j], matvec(entries_by_column(echo), last_y[j]))
                    for i in range(3):
                        links[h, ECHO + 3 * i + j] = echo[j][i]
            else:
                for k in range(9):
                    links[h, ECHO + k] = jnp.zeros(dims.tile, F32)
            for j in range(3):
                for i in range(3):
                    links[h, THROUGH + 3 * i + j] = through[j][i]
        get_even, get_odd = getter(dims, even), getter(dims, odd)
        get_cross, get_other, get_mate = (getter(dims, ref) for ref in (cross, other, mate))
        zero = [jnp.zeros(dims.tile, F32)] * 3
        first = 0 if g < 2 else 2
        for r in range(dims.rows):
            if g < 2:
                s = matvec(table(links, 2, LAST_Y), get_cross(0, r))
                s = matvec(table(links, 2, FIRST_S), matvec(table(links, 3, FIRST_Y), s))
                s = add(s, matvec(table(links, 2, FIRST_Y), get_cross(0, r)))
                s = add(s, get_other(0, r))
                if g == 0:
                    y = zero
                    s = matvec(table(links, 1, FIRST_S), s)
                    s = add(s, matvec(table(links, 1, FIRST_Y), get_even(LAST, r)))
                    s = add(s, get_odd(FIRST, r))
                else:
                    y = get_even(LAST, r)
            else:
                y = get_other(0, r)
                after = add(get_even(LAST, r), matvec(table(links, 2, LAST_Y), y))
                if g == 2:
                    s = add(get_odd(FIRST, r), matvec(table(links, 3, FIRST_Y), after))
                else:
                    y, s = after, zero
            if g % 2 == 0:
                down = zero if g == 0 else get_other(3, r)
                up = get_mate(BOTTOM, r)
            else:
                down = get_mate(TOP, r)
                up = zero if g == GROUPS - 1 else get_other(3, r)
            for c in range(3):
                bound[c, r] = y[c]
                bound[3 + c, r] = s[c]
                edge[c, r] = down[c]
                edge[3 + c, r] = up[c]

    for_each_group(body)


def beside_part(k):
    return [*range(TOP, TOP + 3)] * (k == 1) + [*range(BOTTOM, PARTS)] * (k == GROUPS - 1)


def bound_kernel(dims, links, own, *refs):
    others, (bound, edge) = refs[: GROUPS - 1], refs[GROUPS - 1 :]

    def body(g):
        got = [getter(dims, own if h == g else others[(g - h) % GROUPS - 1]) for h in range(GROUPS)]
        zero = [jnp.zeros(dims.tile, F32)] * 3
        for r in range(dims.rows):
            y = zero
            for h in range(g):
                value = got[h](0, r)
                y = value if h == 0 else add(value, matvec(table(links, h, LAST_Y), y))
            s = zero
            if g < GROUPS - 1:
                s = got[g](LAST, r)
                if g:
                    s = add(s, matvec(table(links, g, LAST_Y), y))
                s = matvec(table(links, g + 1, THROUGH), s)
                after = got[GROUPS - 1](0, r)
                for h in range(GROUPS - 2, g, -1):
                    after = add(got[h](0, r), matvec(table(links, h, FIRST_S), after))
                s = add(s, after)
            down = zero if g == 0 else got[g - 1](3, r)
            up = zero if g == GROUPS - 1 else got[g + 1](3, r)
            for c in range(3):
                bound[c, r] = y[c]
                bound[3 + c, r] = s[c]
                edge[c, r] = down[c]
                edge[3 + c, r] = up[c]

    for_each_group(body)


def absorb_kernel(dims, heff, bound, edge, coefs, values, *refs):
    if len(refs) == 1:
        (out,) = refs
    else:
        local, out, accum_out, accum, sem = refs

    def body(l, carry):
        stiff = values[l, STIFF]
        down = jnp.where(l == 0, 0.5, 0.0) * stiff
        up = jnp.where(l == dims.layers - 1, 0.5, 0.0) * stiff
        for r in range(dims.rows):
            y = [bound[c, r] for c in range(3)]
            s = [bound[3 + c, r] for c in range(3)]
            fix = add(matvec(table(coefs, l, FROM_Y), y), matvec(table(coefs, l, FROM_S), s))
            for c in range(3):
                sides = down * edge[c, r] + up * edge[3 + c, r]
                out[c, l, r] = heff[c, l, r] + 0.5 * fix[c] + sides
                if len(refs) > 1:
                    accum[cells(dims, c, l, turned(dims, r)), :] = local[c, l, r] + fix[c]
        if len(refs) > 1:
            send_lines(dims, l, accum, accum_out, sem.at[0])
        return carry

    loop(dims.layers, body, 0)
    if len(refs) > 1:
        pltpu.make_async_copy(accum, accum_out, sem.at[0]).wait()


def send_lines(dims, layer, src, dst, sem):
    lines = dims.chunks * dims.rows
    for c in range(3):
        where = pl.ds((c * dims.layers + layer) * lines, lines)
        pltpu.make_async_copy(src.at[where], dst.at[where], sem).start()


def shifted_sum(dims, w, lane):
    after = pltpu.roll(w, dims.chunks - 1, 0)
    before = pltpu.roll(w, 1, 0)
    near = pltpu.roll(jnp.where(lane < 1, after, w), LANES - 1, 1)
    near += pltpu.roll(jnp.where(lane >= LANES - 1, before, w), 1, 1)
    far = pltpu.roll(jnp.where(lane < 2, after, w), LANES - 2, 1)
    far += pltpu.roll(jnp.where(lane >= LANES - 2, before, w), 2, 1)
    return NEAR * near + FAR * far


def hash_uniform(mixed):
    mixed = mixed ^ lax.shift_right_logical(mixed, jnp.int32(16))
    mixed = mixed * HASH_A
    mixed = mixed ^ lax.shift_right_logical(mixed, jnp.int32(15))
    mixed = mixed * HASH_B
    mixed = mixed ^ lax.shift_right_logical(mixed, jnp.int32(16))
    return (mixed & 65535).astype(F32) * (1.0 / 32767.5) - 1.0


def local_kernel(dims, first, *refs):
    field, solved, maskf, values, *refs = refs
    if first:
        seed, heff, noise, masked = refs
        group = lax.axis_index("depth")
        place = lax.axis_index("plane")
        within = (
            lax.broadcasted_iota(jnp.int32, dims.tile, 0) * LANES
            + lax.broadcasted_iota(jnp.int32, dims.tile, 1)
        ) * HASH_A + seed[...]
    else:
        noise, heff, masked = refs
    lane = lax.broadcasted_iota(jnp.int32, dims.tile, 1)
    rows = range(dims.rows)

    for c in range(3):
        for r in rows:
            masked[c, 0, r] = jnp.zeros(dims.tile, F32)
            masked[c, dims.layers + 1, r] = jnp.zeros(dims.tile, F32)

    def fill(l, carry):
        for r in rows:
            mask_row = maskf[r]
            for c in range(3):
                masked[c, l + 1, r] = field[c, l, r] * mask_row
        return carry

    lax.fori_loop(0, dims.layers, fill, 0)

    def body(l, carry):
        stiff = values[l, STIFF]
        aniso = values[l, ANISO]
        for c in range(3):
            w = [masked[c, l + 1, r] for r in rows]
            for r in rows:
                total = shifted_sum(dims, w[r], lane)
                for step, weight in ((1, NEAR), (2, FAR)):
                    inside = [w[q] for q in (r - step, r + step) if 0 <= q < dims.rows]
                    if inside:
                        total += weight * functools.reduce(jnp.add, inside)
                total += 0.5 * (masked[c, l, r] + masked[c, l + 2, r])
                h = stiff * total + 0.5 * solved[c, l, r]
                if c == 2:
                    h += aniso * field[c, l, r]
                if first:
                    layer = group * dims.layers + l
                    line = (c * (dims.depth * dims.layers) + layer) * (
                        dims.plane * dims.rows
                    ) + (place * dims.rows + turned(dims, r))
                    value = values[l, THERMAL] * hash_uniform(within + line * dims.width * HASH_A)
                    noise[c, l, r] = value
                    h += value
                else:
                    h += noise[c, l, r]
                heff[c, l, r] = h
        return carry

    lax.fori_loop(0, dims.layers, body, 0)


def finish_kernel(dims, first, start, stop, closing, *refs):
    rows = range(start, stop)
    ends = [(start == 0, 0), (stop == dims.rows, dims.rows - 1)]
    halos, refs = refs[: sum(there for there, _ in ends)], refs[sum(there for there, _ in ends) :]
    halos = list(zip([position for there, position in ends if there], halos))
    field, maskf, heff, coefs, blocks, values, *refs = refs
    last_call = not first and closing
    mate_rows = range(start) if start else range(stop, dims.rows)
    offset = mate_rows[0]
    if first and closing:
        links, mate_middle, mate_base, mate_local, mate_ends, middle, base, local, out_halo, own, *messages = refs
    elif first:
        middle, base, local, out_halo, ends = refs
    elif not last_call:
        base, result = refs
    else:
        base, mate, result_out, result, sem = refs

    def at(r):
        return r if closing else r - start

    def body(l, prev):
        stiff = values[l, STIFF]
        weights = (stiff * NEAR, stiff * FAR)
        alpha = values[l, DAMP]
        scale = values[l, SCALE]
        done = []
        for r in rows:
            v = [field[c, l, r] for c in range(3)]
            h = [heff[c, l, r] for c in range(3)]
            for c in range(3):
                for position, halo in halos:
                    for step in (1, 2):
                        beyond = step - 1 - abs(r - position)
                        if beyond >= 0:
                            h[c] += weights[step - 1] * halo[c, l, beyond]
            torque = cross(v, h)
            twice = cross(v, torque)
            mask_row = maskf[r]
            gain = scale * mask_row
            rate = [(torque[c] + alpha * twice[c]) * gain for c in range(3)]
            if first:
                m1 = unit([v[c] - 0.03 * rate[c] for c in range(3)])
                edge_row = dims.rows - 1 - r if start else r
                for c in range(3):
                    middle[c, l, at(r)] = m1[c]
                    base[c, l, at(r)] = v[c] - 0.015 * rate[c]
                    if edge_row < HALO:
                        out_halo[c, l, edge_row] = m1[c] * mask_row
                y = matvec(table(coefs, l, PIVOT_SOURCE), m1)
                drop = matvec(table(coefs, l, PIVOT_LOWER), prev[r - start])
                y = [a - b for a, b in zip(y, drop)]
                for c in range(3):
                    local[c, l, at(r)] = y[c]
                done.append(y)
                continue
            new = unit([base[c, l, r] - 0.015 * rate[c] for c in range(3)])
            for c in range(3):
                if last_call:
                    result[cells(dims, c, l, turned(dims, r)), :] = new[c]
                else:
                    result[c, l, r - start] = new[c]
        if last_call:
            for c in range(3):
                for r in mate_rows:
                    result[cells(dims, c, l, turned(dims, r)), :] = mate[c, l, r - offset]
            send_lines(dims, l, result, result_out, sem.at[0])
        return done

    if not first:
        loop(dims.layers, lambda l, carry: (body(l, None), carry)[1], 0)
        if last_call:
            pltpu.make_async_copy(result, result_out, sem.at[0]).wait()
        return

    def put(r, sent):
        group = lax.axis_index("depth")
        echo = matvec(table(links, group, ECHO), sent[LAST : LAST + 3])
        down = add(sent[FIRST : FIRST + 3], echo)
        for k, message in enumerate(messages, 1):
            value = [jnp.where(group + k < GROUPS, a, b) for a, b in zip(sent[LAST : LAST + 3], down)]
            value += [sent[p] for p in beside_part(k)]
            for place, tile in enumerate(value):
                message[place * dims.rows + r] = tile
        for c in range(3):
            own[c * dims.rows + r] = sent[LAST + c]

    zero = [[jnp.zeros(dims.tile, F32)] * 3 for _ in rows]
    last = loop(dims.layers, body, zero)
    lines = [(local, at(r)) for r in rows]
    head = sweep_back(dims, lines, lambda l: table(blocks, l, UPPER), zero)
    for r in rows:
        sent = [last[r - start][c] for c in range(3)] + [head[r - start][c] for c in range(3)]
        for l in (dims.layers - 1, 0):
            sent += [middle[c, l, at(r)] * maskf[r] for c in range(3)]
        if closing:
            put(r, sent)
        else:
            for p in range(PARTS):
                ends[p, at(r)] = sent[p]
    if not closing:
        return
    for r in mate_rows:
        put(r, [mate_ends[p, r - offset] for p in range(PARTS)])

    def merge(l, carry):
        for r in mate_rows:
            for c in range(3):
                middle[c, l, r] = mate_middle[c, l, r - offset]
                base[c, l, r] = mate_base[c, l, r - offset]
                local[c, l, r] = mate_local[c, l, r - offset]
        return carry

    lax.fori_loop(0, dims.layers, merge, 0)


def call(kernel, outs, args, scratch=(), ins=None, results=None):
    return pl.pallas_call(
        kernel,
        out_shape=outs,
        in_specs=ins or [vmem()] * len(args),
        out_specs=results or [vmem()] * len(outs),
        scratch_shapes=list(scratch),
        compiler_params=pltpu.CompilerParams(vmem_limit_bytes=VMEM_LIMIT),
        cost_estimate=pl.CostEstimate(flops=1000000, bytes_accessed=1000000, transcendentals=0),
    )(*args)


def ring(count, step):
    return [(i, (i + step) % count) for i in range(count)]


def local(
    magnet,
    mask,
    materials,
    exchange_strength,
    anisotropy,
    damping,
    source_strength,
    thermal_strength,
    pivots,
    lower,
    upper,
    noise_stream,
    counter,
):
    dims = Dims(
        magnet.shape[1],
        magnet.shape[2],
        magnet.shape[3],
        lax.axis_size("depth"),
        lax.axis_size("plane"),
    )
    lines = (3, dims.layers, dims.rows, dims.chunks, LANES)
    view = magnet.reshape(lines).transpose(0, 1, 3, 2, 4).reshape(-1, LANES)
    mask_view = mask.reshape(lines[2:]).transpose(1, 0, 2).reshape(-1, LANES)
    halo = shape(3, dims.layers, HALO, *dims.tile)
    field = shape(*dims.field())
    padded = [pltpu.VMEM((3, dims.layers + 2, dims.rows) + dims.tile, F32)]
    assert dims.depth == GROUPS
    message = PARTS * dims.rows
    edges = shape(6, dims.rows, *dims.tile)

    def across(values):
        pairs = [(i, (i + 1 if i % 2 else i - 1) % dims.plane) for i in range(dims.plane)]
        return lax.ppermute(values, "plane", pairs)

    def beside(values):
        return lax.ppermute(values, "plane", [(i, i ^ 1) for i in range(dims.plane)])

    def exchange(values, step):
        return lax.ppermute(values, "depth", [(i, i ^ step) for i in range(dims.depth)])

    def finish(first, start, stop, closing, halos, fields, heff, extra, outs, *rest):
        kernel = functools.partial(finish_kernel, dims, first, start, stop, closing)
        return call(kernel, outs, (*halos, fields, maskf, heff, coefs, blocks, values, *extra), *rest)

    seed = jnp.full(dims.tile, noise_stream[0] * HASH_B + counter[0] * HASH_C, jnp.int32)
    inputs = (
        view,
        mask_view,
        materials,
        exchange_strength,
        anisotropy,
        damping,
        source_strength,
        thermal_strength,
        pivots.transpose(1, 2, 0),
        lower.transpose(1, 2, 0),
        upper.transpose(1, 2, 0),
    )
    inputs = [pltpu.with_memory_space_constraint(x, pltpu.HBM) for x in inputs]
    spaces = [pltpu.VMEM] * 2 + [pltpu.SMEM] * 9
    held = [space(x.shape, x.dtype) for space, x in zip(spaces, inputs)]
    tiles, maskf, near, blocks, values = call(
        functools.partial(enter_kernel, dims),
        [
            field,
            shape(dims.rows, *dims.tile),
            halo,
            shape(dims.layers, BLOCK_COEFS, *dims.tile),
            shape(dims.layers, LAYER_VALUES, *dims.tile),
        ],
        inputs,
        held + [pltpu.SemaphoreType.DMA((len(inputs),))],
        [hbm()] * len(inputs),
    )
    near_halo = beside(near)
    solved, trail, sent, far = call(
        functools.partial(sweep_kernel, dims),
        [field, shape(3, dims.layers, 1, *dims.tile), shape(message + 6, *dims.tile), halo],
        (tiles, maskf, blocks, values),
    )
    mate = exchange(sent, 1)
    far_halo = across(far)
    (cross,) = call(
        functools.partial(cross_kernel, dims),
        [shape(6 * dims.rows + 6, *dims.tile)],
        (sent, mate),
    )
    other = exchange(cross, 2)
    (coefs,) = call(
        functools.partial(coefficient_kernel, dims),
        [shape(dims.layers, LAYER_COEFS, *dims.tile)],
        (trail, blocks, values),
    )
    links, *bounds = call(
        functools.partial(first_bound_kernel, dims),
        [shape(GROUPS, LINKS, *dims.tile), edges, edges],
        (sent, mate, cross, other),
    )
    heff, noise = call(
        functools.partial(local_kernel, dims, True),
        [field, field],
        (tiles, solved, maskf, values, seed),
        padded,
    )
    inner = dims.rows // 2
    part = shape(3, dims.layers, dims.rows - inner, *dims.tile)
    (heff,) = call(
        functools.partial(absorb_kernel, dims), [field], (heff, *bounds, coefs, values)
    )
    *near_half, near, ends = finish(
        True,
        inner,
        dims.rows,
        False,
        [near_halo],
        tiles,
        heff,
        (),
        [part, part, part, halo, shape(PARTS, dims.rows - inner, *dims.tile)],
    )
    near_halo = beside(near)
    middle, base, solved, far, own, *sent = finish(
        True,
        0,
        inner,
        True,
        [far_halo],
        tiles,
        heff,
        (links, *near_half, ends),
        [field, field, field, halo, shape(3 * dims.rows, *dims.tile)]
        + [shape((3 + len(beside_part(k))) * dims.rows, *dims.tile) for k in range(1, GROUPS)],
    )
    far_halo = across(far)
    others = [
        lax.ppermute(values, "depth", [(i, (i + k) % GROUPS) for i in range(GROUPS)])
        for k, values in enumerate(sent, 1)
    ]
    bounds = call(
        functools.partial(bound_kernel, dims),
        [edges, edges],
        (links, own, *others),
    )
    (heff,) = call(
        functools.partial(local_kernel, dims, False),
        [field],
        (middle, solved, maskf, values, noise),
        padded,
    )
    lined = shape(*view.shape)
    staging = [pltpu.VMEM(view.shape, F32), pltpu.SemaphoreType.DMA((1,))]
    heff, accum = call(
        functools.partial(absorb_kernel, dims),
        [field, lined],
        (heff, *bounds, coefs, values, solved),
        staging,
        None,
        [vmem(), hbm()],
    )
    (near_result,) = finish(
        False, inner, dims.rows, False, [near_halo], middle, heff, (base,), [part]
    )
    (result,) = finish(
        False,
        0,
        inner,
        True,
        [far_halo],
        middle,
        heff,
        (base, near_result),
        [lined],
        staging,
        None,
        [hbm()],
    )

    def whole(lines_view):
        cut = lines_view.reshape(3, dims.layers, dims.chunks, dims.rows, LANES)
        return cut.transpose(0, 1, 3, 2, 4).reshape(magnet.shape)

    return whole(result), whole(accum)


def solution(mesh):
    placed = (
        P(None, "depth", "plane", None),
        P("plane", None),
        P("depth"),
    ) + (P(),) * 10
    return jax.shard_map(
        local,
        mesh=mesh,
        in_specs=placed,
        out_specs=(P(None, "depth", "plane", None), P(None, "depth", "plane", None)),
        check_vma=False,
    )
```

time: 30.4 us -> 29.8 us (0.980)
  starting transfers between devices: 13.1 us -> 17.2 us
  waiting for transfers between devices: 6.04 us -> 2.87 us
  Pallas kernels: 9.06 us -> 7.47 us
    ppermute x10 -> x9, starting transfers between devices: 13.1 us -> 17.2 us  [the longest x2 7.15 us: across(): return lax.ppermute(values, 'plane', pairs)]
    ppermute x10 -> x9, waiting for transfers between devices: 6.04 us -> 2.87 us  [the longest x3 2.03 us: local(): lax.ppermute(values, 'depth', [(i, (i + k) % GROUPS) for i in range(GROUP...]
    pallas_call x8 -> x14, Pallas kernels: 9.06 us -> 7.47 us  [call(): pl.pallas_call(kernel, out_shape=outs, in_specs=ins or [vmem()] * len(arg...]
  transfers between devices with their start and end apart: 10 -> 9, of which waited for: 3 -> 2; matrix products, arithmetic and copies ran while one was open for 0% -> 0% of each run, Pallas kernels for 21% -> 17%
where the time goes in v4:
time: 29.8 us; the launch traced here: 29.6 us
  starting transfers between devices  17.2 us (58%)
  Pallas kernels  7.47 us (25%)
  waiting for transfers between devices  2.87 us (10%)
  between operations  2.05 us (7%)
    pallas_call x14, Pallas kernels, call(): pl.pallas_call(kernel, out_shape=outs, in_specs=ins or [vmem()] * len(arg...  7.47 us
    ppermute x2, starting transfers between devices, across(): return lax.ppermute(values, 'plane', pairs)  7.15 us
    ppermute x2, starting transfers between devices, beside(): lax.ppermute(values, 'plane', [(i, i ^ 1) for i in range(dims.plane)])  4.74 us
    ppermute x3, starting transfers between devices, local(): lax.ppermute(values, 'depth', [(i, (i + k) % GROUPS) for i in range(GROUP...  3.24 us
    ppermute x2, starting transfers between devices, exchange(): lax.ppermute(values, 'depth', [(i, i ^ step) for i in range(dims.depth)])  2.08 us
    ppermute x3, waiting for transfers between devices, local(): lax.ppermute(values, 'depth', [(i, (i + k) % GROUPS) for i in range(GROUP...  2.03 us
    ppermute x2, waiting for transfers between devices, exchange(): lax.ppermute(values, 'depth', [(i, i ^ step) for i in range(dims.depth)])  0.83 us
  transfers between devices with their start and end apart: 9, of which 2 were waited for; matrix products, arithmetic and copies ran while one was open for 0% of the time, Pallas kernels for 17%

profile of v4, /device:TPU:0, one launch (start us, length us, event | category | flops | bytes accessed | tf_op | source)
XLA Modules:
  0.0 29.6 jit_solution(7174165175767758074)
XLA Ops:
  0.6 1.4 %shard_map.140 = (f32[3,8,4,8,128]{4,3,2,1,0:T(8,128)S(1)}, f32[4,8,128]{2,1,0:T(8,128)S(1)}, f32[3,8,2,8,128]{4,3,2,1,0:T(8,128)S(1)}, f32[8,27,8,128]{3,2,1,0:T(8,128)S(1)}, f32[8,6,8,128]{3,2,1,0:T(8,128)S(1)}) custom-call(f32[768,128]{1,0:T(8,128)} %bitcast.25, s32[32,128]{1,0:T(8,128)} %bitcast.26, s32[8]{0:T(128)} %refs_2_.1, f32[4]{0:T(128)} %refs_3_.1, ...), custom_call_target="tpu_custom_call" | custom-call | flops 1000000 | bytes 1000000 | tf_op jit(solution)/shard_map/pallas_call | solution.py:634
  2.0 0.3 %shard_map.141 = (f32[3,8,4,8,128]{4,3,2,1,0:T(8,128)S(1)}, f32[3,8,1,8,128]{4,3,2,1,0:T(8,128)S(1)}, f32[54,8,128]{2,1,0:T(8,128)S(1)}, f32[3,8,2,8,128]{4,3,2,1,0:T(8,128)S(1)}) custom-call(f32[3,8,4,8,128]{4,3,2,1,0:T(8,128)S(1)} %get-tuple-element.33.field.refs_0_.refs_1_, f32[4,8,128]{2,1,0:T(8,128)S(1)} %get-tuple-element.34.maskf.refs_2_, ...), custom_call_target="tpu_custom_call" | custom-call | flops 1000000 | bytes 1000000 | tf_op jit(solution)/shard_map/pallas_call | solution.py:634
  2.4 0.5 %collective-permute-start.1 = (f32[54,8,128]{2,1,0:T(8,128)S(1)}, f32[54,8,128]{2,1,0:T(8,128)S(1)}, u32[]{:S(2)}, u32[]{:S(2)}) collective-permute-start(f32[54,8,128]{2,1,0:T(8,128)S(1)} %get-tuple-element.40.own), channel_id=1, source_target_pairs={{0,8},{8,0},{16,24},{24,16},{1,9},{9,1},{17,25},{25,17},{2,10},{10... | collective-permute-start | bytes 663560 | tf_op jit(solution)/shard_map/ppermute | solution.py:689
  2.9 2.6 %collective-permute-start.3 = (f32[3,8,2,8,128]{4,3,2,1,0:T(8,128)S(1)}, f32[3,8,2,8,128]{4,3,2,1,0:T(8,128)S(1)}, u32[]{:S(2)}, u32[]{:S(2)}) collective-permute-start(f32[3,8,2,8,128]{4,3,2,1,0:T(8,128)S(1)} %get-tuple-element.45), channel_id=1, source_target_pairs={{0,1},{1,0},{2,3},{3,2},{4,5},{5,4},{6,7},{7,6},{8,9},{9,8},{10,11... | collective-permute-start | bytes 589832 | tf_op jit(solution)/shard_map/ppermute | solution.py:686
  5.5 3.5 %collective-permute-start = (f32[3,8,2,8,128]{4,3,2,1,0:T(8,128)S(1)}, f32[3,8,2,8,128]{4,3,2,1,0:T(8,128)S(1)}, u32[]{:S(2)}, u32[]{:S(2)}) collective-permute-start(f32[3,8,2,8,128]{4,3,2,1,0:T(8,128)S(1)} %get-tuple-element.37), channel_id=1, source_target_pairs={{0,7},{1,2},{2,1},{3,4},{4,3},{5,6},{6,5},{7,0},{8,15},{9,10},{10,... | collective-permute-start | bytes 589832 | tf_op jit(solution)/shard_map/ppermute | solution.py:683
  9.0 0.0 collective-permute-done.1.mate
  9.0 0.1 shard_map.143.cross
  9.1 1.6 %collective-permute-start.2 = (f32[30,8,128]{2,1,0:T(8,128)S(1)}, f32[30,8,128]{2,1,0:T(8,128)S(1)}, u32[]{:S(2)}, u32[]{:S(2)}) collective-permute-start(f32[30,8,128]{2,1,0:T(8,128)S(1)} %shard_map.143.cross), channel_id=1, source_target_pairs={{0,16},{8,24},{16,0},{24,8},{1,17},{9,25},{17,1},{25,9},{2,18},{10... | collective-permute-start | bytes 368648 | tf_op jit(solution)/shard_map/ppermute | solution.py:689
  12.0 0.4 %shard_map.145.coefs.refs_4_ = f32[8,36,8,128]{3,2,1,0:T(8,128)S(1)} custom-call(f32[3,8,1,8,128]{4,3,2,1,0:T(8,128)S(1)} %get-tuple-element.43.trail, f32[8,27,8,128]{3,2,1,0:T(8,128)S(1)} %get-tuple-element.35.blocks.refs_5_, f32[8,6,8,128]{3,2,1,0:T(8,128)S(1)} %get-tuple-element.36.values.refs_3_.refs_6_), custom_call_target="tpu_custom_call" | custom-call | flops 1000000 | bytes 1000000 | tf_op jit(solution)/shard_map/pallas_call | solution.py:634
  12.4 1.1 %shard_map.142 = (f32[3,8,4,8,128]{4,3,2,1,0:T(8,128)S(1)}, f32[3,8,4,8,128]{4,3,2,1,0:T(8,128)S(1)}) custom-call(f32[3,8,4,8,128]{4,3,2,1,0:T(8,128)S(1)} %get-tuple-element.33.field.refs_0_.refs_1_, f32[3,8,4,8,128]{4,3,2,1,0:T(8,128)S(1)} %get-tuple-element.38.refs_1_, f32[4,8,128]{2,1,0:T(8,128)S(1)} %get-tuple-element.34.maskf.refs_2_, ...), custom_call_target="tpu_custom_call" | custom-call | flops 1000000 | bytes 1000000 | tf_op jit(solution)/shard_map/pallas_call | solution.py:634
  13.5 0.8 %collective-permute-done.2.other = f32[30,8,128]{2,1,0:T(8,128)S(1)} collective-permute-done((f32[30,8,128]{2,1,0:T(8,128)S(1)}, f32[30,8,128]{2,1,0:T(8,128)S(1)}, u32[]{:S(2)}, u32[]{:S(2)}) %collective-permute-start.2) | collective-permute-done | bytes 122912 | tf_op jit(solution)/shard_map/ppermute | solution.py:689
  14.3 0.3 shard_map.144
  14.6 0.2 shard_map.146.refs_3_
  14.9 0.0 collective-permute-done.3.refs_0_
  14.9 0.3 %shard_map.147 = (f32[3,8,2,8,128]{4,3,2,1,0:T(8,128)S(1)}, f32[3,8,2,8,128]{4,3,2,1,0:T(8,128)S(1)}, f32[3,8,2,8,128]{4,3,2,1,0:T(8,128)S(1)}, f32[3,8,2,8,128]{4,3,2,1,0:T(8,128)S(1)}, f32[12,2,8,128]{3,2,1,0:T(8,128)S(1)}) custom-call(f32[3,8,2,8,128]{4,3,2,1,0:T(8,128)S(1)} %collective-permute-done.3.refs_0_, ...), custom_call_target="tpu_custom_call" | custom-call | flops 1000000 | bytes 1000000 | tf_op jit(solution)/shard_map/pallas_call | solution.py:634
  15.2 2.2 %collective-permute-start.8 = (f32[3,8,2,8,128]{4,3,2,1,0:T(8,128)S(1)}, f32[3,8,2,8,128]{4,3,2,1,0:T(8,128)S(1)}, u32[]{:S(2)}, u32[]{:S(2)}) collective-permute-start(f32[3,8,2,8,128]{4,3,2,1,0:T(8,128)S(1)} %get-tuple-element.62), channel_id=1, source_target_pairs={{0,1},{1,0},{2,3},{3,2},{4,5},{5,4},{6,7},{7,6},{8,9},{9,8},{10,11... | collective-permute-start | bytes 589832 | tf_op jit(solution)/shard_map/ppermute | solution.py:686
  17.3 0.0 collective-permute-done.refs_0_
  17.3 0.4 %shard_map.148 = (f32[3,8,4,8,128]{4,3,2,1,0:T(8,128)S(1)}, f32[3,8,4,8,128]{4,3,2,1,0:T(8,128)S(1)}, f32[3,8,4,8,128]{4,3,2,1,0:T(8,128)S(1)}, f32[3,8,2,8,128]...) custom-call(f32[3,8,2,8,128]{4,3,2,1,0:T(8,128)S(1)} %collective-per, ...), custom_call_target="tpu_custom_call" | custom-call | flops 1000000 | bytes 1000000 | tf_op jit(solution)/shard_map/pallas_call | solution.py:634
  17.7 3.6 %collective-permute-start.4 = (f32[3,8,2,8,128]{4,3,2,1,0:T(8,128)S(1)}, f32[3,8,2,8,128]{4,3,2,1,0:T(8,128)S(1)}, u32[]{:S(2)}, u32[]{:S(2)}) collective-permute-start(f32[3,8,2,8,128]{4,3,2,1,0:T(8,128)S(1)} %get-tuple-element.50), channel_id=1, source_target_pairs={{0,7},{1,2},{2,1},{3,4},{4,3},{5,6},{6,5},{7,0},{8,15},{9,10},{10,... | collective-permute-start | bytes 589832 | tf_op jit(solution)/shard_map/ppermute | solution.py:683
  21.3 0.0 collective-permute-start.5
  21.3 1.7 %collective-permute-start.7 = (f32[24,8,128]{2,1,0:T(8,128)S(1)}, f32[24,8,128]{2,1,0:T(8,128)S(1)}, u32[]{:S(2)}, u32[]{:S(2)}) collective-permute-start(f32[24,8,128]{2,1,0:T(8,128)S(1)} %get-tuple-element.57), channel_id=1, source_target_pairs={{0,24},{8,0},{16,8},{24,16},{1,25},{9,1},{17,9},{25,17},{2,26},{10... | collective-permute-start | bytes 294920 | tf_op jit(solution)/shard_map/ppermute | solution.py:786
  23.1 1.5 %collective-permute-start.6 = (f32[12,8,128]{2,1,0:T(8,128)S(1)}, f32[12,8,128]{2,1,0:T(8,128)S(1)}, u32[]{:S(2)}, u32[]{:S(2)}) collective-permute-start(f32[12,8,128]{2,1,0:T(8,128)S(1)} %get-tuple-element.56), channel_id=1, source_target_pairs={{0,16},{8,24},{16,0},{24,8},{1,17},{9,25},{17,1},{25,9},{2,18},{10... | collective-permute-start | bytes 147464 | tf_op jit(solution)/shard_map/ppermute | solution.py:786
  24.6 1.1 %shard_map.149.heff = f32[3,8,4,8,128]{4,3,2,1,0:T(8,128)S(1)} custom-call(f32[3,8,4,8,128]{4,3,2,1,0:T(8,128)S(1)} %get-tuple-element.51.refs_0_.refs_1_, f32[3,8,4,8,128]{4,3,2,1,0:T(8,128)S(1)} %get-tuple-element.52.refs_1_.refs_0_, f32[4,8,128]{2,1,0:T(8,128)S(1)} %get-tuple-element.34.maskf.refs_2_, ...), custom_call_target="tpu_custom_call" | custom-call | flops 1000000 | bytes 1000000 | tf_op jit(solution)/shard_map/pallas_call | solution.py:634
  25.7 2.0 %collective-permute-done.6.refs_1_ = f32[12,8,128]{2,1,0:T(8,128)S(1)} collective-permute-done((f32[12,8,128]{2,1,0:T(8,128)S(1)}, f32[12,8,128]{2,1,0:T(8,128)S(1)}, u32[]{:S(2)}, u32[]{:S(2)}) %collective-permute-start.6) | collective-permute-done | bytes 49184 | tf_op jit(solution)/shard_map/ppermute | solution.py:786
  27.7 0.0 collective-permute-done.5.refs_0_
  27.7 0.0 collective-permute-done.7.refs_2_
  27.7 0.1 shard_map.150
  27.8 0.8 %shard_map.151 = (f32[3,8,4,8,128]{4,3,2,1,0:T(8,128)S(1)}, f32[768,128]{1,0:T(8,128)}) custom-call(f32[3,8,4,8,128]{4,3,2,1,0:T(8,128)S(1)} %shard_map.149.heff, f32[6,4,8,128]{3,2,1,0:T(8,128)S(1)} %get-tuple-element.58.bound, f32[6,4,8,128]{3,2,1,0:T(8,128)S(1)} %get-tuple-element.59.edge, f32[8,36,8,128]{3,2,1,0:T(8,128)S(1)} %shard_map.145.coefs.refs_4_, ...), custom_call_target="tpu_custom_call" | custom-call | flops 1000000 | bytes 1000000 | tf_op jit(solution)/shard_map/pallas_call | solution.py:634
  28.6 0.0 collective-permute-done.8.refs_0_
  28.6 0.1 shard_map.152.refs_8_
  28.8 0.0 collective-permute-done.4.refs_0_
  28.8 0.8 %shard_map.153 = f32[768,128]{1,0:T(8,128)} custom-call(f32[3,8,2,8,128]{4,3,2,1,0:T(8,128)S(1)} %collective-permute-done.4.refs_0_, f32[3,8,4,8,128]{4,3,2,1,0:T(8,128)S(1)} %get-tuple-element.51.refs_0_.refs_1_, f32[4,8,128]{2,1,0:T(8,128)S(1)} %get-tuple-element.34.maskf.refs_2_, f32[3,8,4,8,128]{4,3,2,1,0:T(8,128)S(1)} %get-tuple-element.60.refs_3_, ...), custom_call_target="tpu_custom_call" | custom-call | flops 1000000 | bytes 1000000 | tf_op jit(solution)/shard_map/pallas_call | solution.py:634
  (1 shorter events, 0.0 us)
Async XLA Ops:
  2.4 6.7 %collective-permute-start.1 = (f32[54,8,128]{2,1,0:T(8,128)S(1)}, f32[54,8,128]{2,1,0:T(8,128)S(1)}, u32[]{:S(2)}, u32[]{:S(2)}) collective-permute-start(f32[54,8,128]{2,1,0:T(8,128)S(1)} %get-tuple-element.40.own), channel_id=1, source_target_pairs={{0,8},{8,0},{16,24},{24,16},{1,9},{9,1},{17,25},{25,17},{2,10},{10... | collective-permute-start | bytes 663560 | tf_op jit(solution)/shard_map/ppermute | solution.py:689
  2.9 12.0 %collective-permute-start.3 = (f32[3,8,2,8,128]{4,3,2,1,0:T(8,128)S(1)}, f32[3,8,2,8,128]{4,3,2,1,0:T(8,128)S(1)}, u32[]{:S(2)}, u32[]{:S(2)}) collective-permute-start(f32[3,8,2,8,128]{4,3,2,1,0:T(8,128)S(1)} %get-tuple-element.45), channel_id=1, source_target_pairs={{0,1},{1,0},{2,3},{3,2},{4,5},{5,4},{6,7},{7,6},{8,9},{9,8},{10,11... | collective-permute-start | bytes 589832 | tf_op jit(solution)/shard_map/ppermute | solution.py:686
  5.5 11.8 %collective-permute-start = (f32[3,8,2,8,128]{4,3,2,1,0:T(8,128)S(1)}, f32[3,8,2,8,128]{4,3,2,1,0:T(8,128)S(1)}, u32[]{:S(2)}, u32[]{:S(2)}) collective-permute-start(f32[3,8,2,8,128]{4,3,2,1,0:T(8,128)S(1)} %get-tuple-element.37), channel_id=1, source_target_pairs={{0,7},{1,2},{2,1},{3,4},{4,3},{5,6},{6,5},{7,0},{8,15},{9,10},{10,... | collective-permute-start | bytes 589832 | tf_op jit(solution)/shard_map/ppermute | solution.py:683
  9.1 5.2 %collective-permute-start.2 = (f32[30,8,128]{2,1,0:T(8,128)S(1)}, f32[30,8,128]{2,1,0:T(8,128)S(1)}, u32[]{:S(2)}, u32[]{:S(2)}) collective-permute-start(f32[30,8,128]{2,1,0:T(8,128)S(1)} %shard_map.143.cross), channel_id=1, source_target_pairs={{0,16},{8,24},{16,0},{24,8},{1,17},{9,25},{17,1},{25,9},{2,18},{10... | collective-permute-start | bytes 368648 | tf_op jit(solution)/shard_map/ppermute | solution.py:689
  15.2 13.4 %collective-permute-start.8 = (f32[3,8,2,8,128]{4,3,2,1,0:T(8,128)S(1)}, f32[3,8,2,8,128]{4,3,2,1,0:T(8,128)S(1)}, u32[]{:S(2)}, u32[]{:S(2)}) collective-permute-start(f32[3,8,2,8,128]{4,3,2,1,0:T(8,128)S(1)} %get-tuple-element.62), channel_id=1, source_target_pairs={{0,1},{1,0},{2,3},{3,2},{4,5},{5,4},{6,7},{7,6},{8,9},{9,8},{10,11... | collective-permute-start | bytes 589832 | tf_op jit(solution)/shard_map/ppermute | solution.py:686
  17.7 11.0 %collective-permute-start.4 = (f32[3,8,2,8,128]{4,3,2,1,0:T(8,128)S(1)}, f32[3,8,2,8,128]{4,3,2,1,0:T(8,128)S(1)}, u32[]{:S(2)}, u32[]{:S(2)}) collective-permute-start(f32[3,8,2,8,128]{4,3,2,1,0:T(8,128)S(1)} %get-tuple-element.50), channel_id=1, source_target_pairs={{0,7},{1,2},{2,1},{3,4},{4,3},{5,6},{6,5},{7,0},{8,15},{9,10},{10,... | collective-permute-start | bytes 589832 | tf_op jit(solution)/shard_map/ppermute | solution.py:683
  21.3 6.4 %collective-permute-start.5 = (f32[24,8,128]{2,1,0:T(8,128)S(1)}, f32[24,8,128]{2,1,0:T(8,128)S(1)}, u32[]{:S(2)}, u32[]{:S(2)}) collective-permute-start(f32[24,8,128]{2,1,0:T(8,128)S(1)} %get-tuple-element.55), channel_id=1, source_target_pairs={{0,8},{8,16},{16,24},{24,0},{1,9},{9,17},{17,25},{25,1},{2,10},{10... | collective-permute-start | bytes 294920 | tf_op jit(solution)/shard_map/ppermute | solution.py:786
  21.3 6.4 %collective-permute-start.7 = (f32[24,8,128]{2,1,0:T(8,128)S(1)}, f32[24,8,128]{2,1,0:T(8,128)S(1)}, u32[]{:S(2)}, u32[]{:S(2)}) collective-permute-start(f32[24,8,128]{2,1,0:T(8,128)S(1)} %get-tuple-element.57), channel_id=1, source_target_pairs={{0,24},{8,0},{16,8},{24,16},{1,25},{9,1},{17,9},{25,17},{2,26},{10... | collective-permute-start | bytes 294920 | tf_op jit(solution)/shard_map/ppermute | solution.py:786
  23.1 4.6 %collective-permute-start.6 = (f32[12,8,128]{2,1,0:T(8,128)S(1)}, f32[12,8,128]{2,1,0:T(8,128)S(1)}, u32[]{:S(2)}, u32[]{:S(2)}) collective-permute-start(f32[12,8,128]{2,1,0:T(8,128)S(1)} %get-tuple-element.56), channel_id=1, source_target_pairs={{0,16},{8,24},{16,0},{24,8},{1,17},{9,25},{17,1},{25,9},{2,18},{10... | collective-permute-start | bytes 147464 | tf_op jit(solution)/shard_map/ppermute | solution.py:786

commit v5 on v4

--- a/solution.py
+++ b/solution.py
@@ -87,7 +87,7 @@
 PIVOT_SOURCE, PIVOT_LOWER, FROM_Y, FROM_S, LAYER_COEFS = 0, 9, 18, 27, 36
 STIFF, ANISO, DAMP, THERMAL, SCALE, SOURCE, LAYER_VALUES = 0, 1, 2, 3, 4, 5, 6
 LAST, FIRST, TOP, BOTTOM, PARTS = 0, 3, 6, 9, 12
-LAST_Y, FIRST_Y, FIRST_S, THROUGH, ECHO, LINKS = 0, 9, 18, 27, 36, 45
+LAST_Y, FIRST_Y, FIRST_S, LINKS = 0, 9, 18, 27
 SECOND = 8
 GROUPS = 4
 
@@ -106,10 +106,6 @@
 
 def entries(matrix):
     return lambda i, j: matrix[i][j]
-
-
-def entries_by_column(matrix):
-    return lambda i, j: matrix[j][i]
 
 
 def sweep_back(dims, lines, upper, start):
@@ -263,11 +259,17 @@
     return lambda part: [ref[base + part + c] for c in range(3)]
 
 
-def cross_kernel(dims, own, mate, out):
+def cross_kernel(dims, own, mate, *refs):
+    links, out = refs if len(refs) == 2 else (None, refs[0])
+
     def body(g):
         even, odd = (own, mate) if g % 2 == 0 else (mate, own)
         get_even, get_odd = getter(dims, even), getter(dims, odd)
-        if g < 2:
+        if links is not None:
+            odd_y, odd_first, even_s = (
+                table(links, h, at) for h, at in ((1, LAST_Y), (3, FIRST_Y), (2, FIRST_S))
+            )
+        elif g < 2:
             odd_y = entries(columns(spread(dims, odd)(LAST), 0))
         else:
             odd_first = entries(columns(spread(dims, odd)(FIRST), 0))
@@ -283,6 +285,10 @@
             for c in range(3):
                 out[c * dims.rows + r] = value[c]
                 out[(3 + c) * dims.rows + r] = side[c]
+        if links is not None:
+            for tile in range(6 * dims.rows, out.shape[0]):
+                out[tile] = jnp.zeros(dims.tile, F32)
+            return
         lane = lax.broadcasted_iota(jnp.int32, dims.tile, 1)
         for part in (LAST, FIRST):
             pair = zip(spread(dims, even)(part), spread(dims, odd)(part))
@@ -293,11 +299,12 @@
     for_each_group(body)
 
 
-def first_bound_kernel(dims, own, mate, cross, other, links, bound, edge):
+def bound_kernel(dims, first, own, mate, cross, other, links, bound, edge):
     def body(g):
         base = 6 * dims.rows
         even, odd = (own, mate) if g % 2 == 0 else (mate, own)
-        for pair, ref in enumerate((cross, other) if g < 2 else (other, cross)):
+        pairs = (cross, other) if g < 2 else (other, cross)
+        for pair, ref in enumerate(pairs if first else ()):
             for h in range(2):
                 values = [[ref[base + part + c] for c in range(3)] for part in (LAST, FIRST)]
                 matrices = (
@@ -309,26 +316,9 @@
                     for i in range(3):
                         for j in range(3):
                             links[2 * pair + h, at + 3 * i + j] = matrix[i][j]
-        for h in range(GROUPS - 1, -1, -1):
-            every = [[table(links, h, at)(i, j) for j in range(3) for i in range(3)] for at in (LAST_Y, FIRST_Y, FIRST_S)]
-            last_y, through, first_s = [[m[3 * j : 3 * j + 3] for j in range(3)] for m in every]
-            if h < GROUPS - 1:
-                ahead = table(links, h + 1, THROUGH)
-                echo = [matvec(entries_by_column(first_s), [ahead(i, j) for i in range(3)]) for j in range(3)]
-                for j in range(3):
-                    through[j] = add(through[j], matvec(entries_by_column(echo), last_y[j]))
-                    for i in range(3):
-                        links[h, ECHO + 3 * i + j] = echo[j][i]
-            else:
-                for k in range(9):
-                    links[h, ECHO + k] = jnp.zeros(dims.tile, F32)
-            for j in range(3):
-                for i in range(3):
-                    links[h, THROUGH + 3 * i + j] = through[j][i]
         get_even, get_odd = getter(dims, even), getter(dims, odd)
         get_cross, get_other, get_mate = (getter(dims, ref) for ref in (cross, other, mate))
         zero = [jnp.zeros(dims.tile, F32)] * 3
-        first = 0 if g < 2 else 2
         for r in range(dims.rows):
             if g < 2:
                 s = matvec(table(links, 2, LAST_Y), get_cross(0, r))
@@ -364,47 +354,11 @@
     for_each_group(body)
 
 
-def beside_part(k):
-    return [*range(TOP, TOP + 3)] * (k == 1) + [*range(BOTTOM, PARTS)] * (k == GROUPS - 1)
-
-
-def bound_kernel(dims, links, own, *refs):
-    others, (bound, edge) = refs[: GROUPS - 1], refs[GROUPS - 1 :]
-
-    def body(g):
-        got = [getter(dims, own if h == g else others[(g - h) % GROUPS - 1]) for h in range(GROUPS)]
-        zero = [jnp.zeros(dims.tile, F32)] * 3
-        for r in range(dims.rows):
-            y = zero
-            for h in range(g):
-                value = got[h](0, r)
-                y = value if h == 0 else add(value, matvec(table(links, h, LAST_Y), y))
-            s = zero
-            if g < GROUPS - 1:
-                s = got[g](LAST, r)
-                if g:
-                    s = add(s, matvec(table(links, g, LAST_Y), y))
-                s = matvec(table(links, g + 1, THROUGH), s)
-                after = got[GROUPS - 1](0, r)
-                for h in range(GROUPS - 2, g, -1):
-                    after = add(got[h](0, r), matvec(table(links, h, FIRST_S), after))
-                s = add(s, after)
-            down = zero if g == 0 else got[g - 1](3, r)
-            up = zero if g == GROUPS - 1 else got[g + 1](3, r)
-            for c in range(3):
-                bound[c, r] = y[c]
-                bound[3 + c, r] = s[c]
-                edge[c, r] = down[c]
-                edge[3 + c, r] = up[c]
-
-    for_each_group(body)
-
-
 def absorb_kernel(dims, heff, bound, edge, coefs, values, *refs):
     if len(refs) == 1:
         (out,) = refs
     else:
-        local, out, accum_out, accum, sem = refs
+        local, out, accum = refs
 
     def body(l, carry):
         stiff = values[l, STIFF]
@@ -419,13 +373,9 @@
                 out[c, l, r] = heff[c, l, r] + 0.5 * fix[c] + sides
                 if len(refs) > 1:
                     accum[cells(dims, c, l, turned(dims, r)), :] = local[c, l, r] + fix[c]
-        if len(refs) > 1:
-            send_lines(dims, l, accum, accum_out, sem.at[0])
         return carry
 
     loop(dims.layers, body, 0)
-    if len(refs) > 1:
-        pltpu.make_async_copy(accum, accum_out, sem.at[0]).wait()
 
 
 def send_lines(dims, layer, src, dst, sem):
@@ -514,120 +464,133 @@
     lax.fori_loop(0, dims.layers, body, 0)
 
 
-def finish_kernel(dims, first, start, stop, closing, *refs):
-    rows = range(start, stop)
-    ends = [(start == 0, 0), (stop == dims.rows, dims.rows - 1)]
-    halos, refs = refs[: sum(there for there, _ in ends)], refs[sum(there for there, _ in ends) :]
-    halos = list(zip([position for there, position in ends if there], halos))
-    field, maskf, heff, coefs, blocks, values, *refs = refs
-    last_call = not first and closing
-    mate_rows = range(start) if start else range(stop, dims.rows)
-    offset = mate_rows[0]
-    if first and closing:
-        links, mate_middle, mate_base, mate_local, mate_ends, middle, base, local, out_halo, own, *messages = refs
-    elif first:
-        middle, base, local, out_halo, ends = refs
-    elif not last_call:
-        base, result = refs
-    else:
-        base, mate, result_out, result, sem = refs
-
-    def at(r):
-        return r if closing else r - start
+def largest(m):
+    x, y, z = [jnp.abs(v) for v in m]
+    first = x >= jnp.maximum(y, z)
+    return first, jnp.logical_and(jnp.logical_not(first), y >= z)
+
+
+def tangent_parts(m, change):
+    first, second = largest(m)
+    last = jnp.logical_or(first, second)
+    return [jnp.where(first, change[1], change[0]), jnp.where(last, change[2], change[1])]
+
+
+def tangent_whole(m, parts):
+    first, second = largest(m)
+    last = jnp.logical_or(first, second)
+    a, b = parts
+    rest = a * jnp.where(first, m[1], m[0]) + b * jnp.where(last, m[2], m[1])
+    along = jnp.where(first, m[0], jnp.where(second, m[1], m[2]))
+    c = -rest / jnp.where(along == 0.0, 1.0, along)
+    return [
+        jnp.where(first, c, a),
+        jnp.where(first, a, jnp.where(second, c, b)),
+        jnp.where(last, b, c),
+    ]
+
+
+def middle_halo(l, start_halo, change_halo):
+    lines = []
+    for k in range(HALO):
+        w = [start_halo[c, l, k] for c in range(3)]
+        change = tangent_whole(w, [change_halo[c, l, k] for c in range(2)])
+        m1 = [w[c] - 0.03 * change[c] for c in range(3)]
+        square = m1[0] * m1[0] + m1[1] * m1[1] + m1[2] * m1[2]
+        scale = lax.rsqrt(jnp.maximum(square, 1e-30))
+        lines.append([v * scale for v in m1])
+    return lines
+
+
+def first_halo(l, halo):
+    return [[halo[c, l, k] for c in range(3)] for k in range(HALO)]
+
+
+def rate(dims, l, r, halos, field, maskf, heff, values):
+    stiff = values[l, STIFF]
+    v = [field[c, l, r] for c in range(3)]
+    h = [heff[c, l, r] for c in range(3)]
+    for step, weight in ((1, NEAR), (2, FAR)):
+        for position, halo in halos:
+            beyond = step - 1 - abs(r - position)
+            if beyond >= 0:
+                h = [h[c] + (stiff * weight) * halo[beyond][c] for c in range(3)]
+    torque = cross(v, h)
+    twice = cross(v, torque)
+    gain = values[l, SCALE] * maskf[r]
+    return v, [(torque[c] + values[l, DAMP] * twice[c]) * gain for c in range(3)]
+
+
+def first_rate_kernel(dims, *refs):
+    far_halo, near_halo, field, maskf, heff, coefs, blocks, values, *refs = refs
+    middle, base, local, far, near, message = refs
+    rows = range(dims.rows)
 
     def body(l, prev):
-        stiff = values[l, STIFF]
-        weights = (stiff * NEAR, stiff * FAR)
-        alpha = values[l, DAMP]
-        scale = values[l, SCALE]
+        halos = [(0, first_halo(l, far_halo)), (dims.rows - 1, first_halo(l, near_halo))]
         done = []
         for r in rows:
-            v = [field[c, l, r] for c in range(3)]
-            h = [heff[c, l, r] for c in range(3)]
-            for c in range(3):
-                for position, halo in halos:
-                    for step in (1, 2):
-                        beyond = step - 1 - abs(r - position)
-                        if beyond >= 0:
-                            h[c] += weights[step - 1] * halo[c, l, beyond]
-            torque = cross(v, h)
-            twice = cross(v, torque)
-            mask_row = maskf[r]
-            gain = scale * mask_row
-            rate = [(torque[c] + alpha * twice[c]) * gain for c in range(3)]
-            if first:
-                m1 = unit([v[c] - 0.03 * rate[c] for c in range(3)])
-                edge_row = dims.rows - 1 - r if start else r
-                for c in range(3):
-                    middle[c, l, at(r)] = m1[c]
-                    base[c, l, at(r)] = v[c] - 0.015 * rate[c]
-                    if edge_row < HALO:
-                        out_halo[c, l, edge_row] = m1[c] * mask_row
-                y = matvec(table(coefs, l, PIVOT_SOURCE), m1)
-                drop = matvec(table(coefs, l, PIVOT_LOWER), prev[r - start])
-                y = [a - b for a, b in zip(y, drop)]
-                for c in range(3):
-                    local[c, l, at(r)] = y[c]
-                done.append(y)
-                continue
-            new = unit([base[c, l, r] - 0.015 * rate[c] for c in range(3)])
-            for c in range(3):
-                if last_call:
-                    result[cells(dims, c, l, turned(dims, r)), :] = new[c]
-                else:
-                    result[c, l, r - start] = new[c]
-        if last_call:
-            for c in range(3):
-                for r in mate_rows:
-                    result[cells(dims, c, l, turned(dims, r)), :] = mate[c, l, r - offset]
-            send_lines(dims, l, result, result_out, sem.at[0])
+            v, change = rate(dims, l, r, halos, field, maskf, heff, values)
+            m1 = unit([v[c] - 0.03 * change[c] for c in range(3)])
+            for c in range(3):
+                middle[c, l, r] = m1[c]
+                base[c, l, r] = v[c] - 0.015 * change[c]
+            for c, part in enumerate(tangent_parts(v, change)):
+                if r < HALO:
+                    far[c, l, r] = part
+                if r >= dims.rows - HALO:
+                    near[c, l, dims.rows - 1 - r] = part
+            y = matvec(table(coefs, l, PIVOT_SOURCE), m1)
+            drop = matvec(table(coefs, l, PIVOT_LOWER), prev[r])
+            y = [a - b for a, b in zip(y, drop)]
+            for c in range(3):
+                local[c, l, r] = y[c]
+            done.append(y)
         return done
-
-    if not first:
-        loop(dims.layers, lambda l, carry: (body(l, None), carry)[1], 0)
-        if last_call:
-            pltpu.make_async_copy(result, result_out, sem.at[0]).wait()
-        return
-
-    def put(r, sent):
-        group = lax.axis_index("depth")
-        echo = matvec(table(links, group, ECHO), sent[LAST : LAST + 3])
-        down = add(sent[FIRST : FIRST + 3], echo)
-        for k, message in enumerate(messages, 1):
-            value = [jnp.where(group + k < GROUPS, a, b) for a, b in zip(sent[LAST : LAST + 3], down)]
-            value += [sent[p] for p in beside_part(k)]
-            for place, tile in enumerate(value):
-                message[place * dims.rows + r] = tile
-        for c in range(3):
-            own[c * dims.rows + r] = sent[LAST + c]
 
     zero = [[jnp.zeros(dims.tile, F32)] * 3 for _ in rows]
     last = loop(dims.layers, body, zero)
-    lines = [(local, at(r)) for r in rows]
-    head = sweep_back(dims, lines, lambda l: table(blocks, l, UPPER), zero)
+    head = sweep_back(dims, [(local, r) for r in rows], lambda l: table(blocks, l, UPPER), zero)
     for r in rows:
-        sent = [last[r - start][c] for c in range(3)] + [head[r - start][c] for c in range(3)]
+        sent = last[r] + head[r]
         for l in (dims.layers - 1, 0):
-            sent += [middle[c, l, at(r)] * maskf[r] for c in range(3)]
-        if closing:
-            put(r, sent)
-        else:
-            for p in range(PARTS):
-                ends[p, at(r)] = sent[p]
-    if not closing:
-        return
-    for r in mate_rows:
-        put(r, [mate_ends[p, r - offset] for p in range(PARTS)])
-
-    def merge(l, carry):
-        for r in mate_rows:
-            for c in range(3):
-                middle[c, l, r] = mate_middle[c, l, r - offset]
-                base[c, l, r] = mate_base[c, l, r - offset]
-                local[c, l, r] = mate_local[c, l, r - offset]
+            sent += [middle[c, l, r] * maskf[r] for c in range(3)]
+        for p in range(PARTS):
+            message[p * dims.rows + r] = sent[p]
+
+
+def second_rate_kernel(
+    dims, rows, position, start_halo, change_halo, field, maskf, heff, values, base, *refs
+):
+    if len(refs) == 1:
+        (out,) = refs
+    else:
+        mate, accum, result_out, accum_out, result, sem = refs
+        accum_copy = pltpu.make_async_copy(accum, accum_out, sem.at[1])
+        accum_copy.start()
+        rest = [r for r in range(dims.rows) if r not in rows]
+
+    def body(l, carry):
+        halos = [(position, middle_halo(l, start_halo, change_halo))]
+        for r in rows:
+            _, change = rate(dims, l, r, halos, field, maskf, heff, values)
+            new = unit([base[c, l, r] - 0.015 * change[c] for c in range(3)])
+            for c in range(3):
+                if len(refs) == 1:
+                    out[c, l, r - rows[0]] = new[c]
+                else:
+                    result[cells(dims, c, l, turned(dims, r)), :] = new[c]
+        if len(refs) > 1:
+            for c in range(3):
+                for r in rest:
+                    result[cells(dims, c, l, turned(dims, r)), :] = mate[c, l, r - rest[0]]
+            send_lines(dims, l, result, result_out, sem.at[0])
         return carry
 
-    lax.fori_loop(0, dims.layers, merge, 0)
+    loop(dims.layers, body, 0)
+    if len(refs) > 1:
+        pltpu.make_async_copy(result, result_out, sem.at[0]).wait()
+        accum_copy.wait()
 
 
 def call(kernel, outs, args, scratch=(), ins=None, results=None):
@@ -672,6 +635,7 @@
     view = magnet.reshape(lines).transpose(0, 1, 3, 2, 4).reshape(-1, LANES)
     mask_view = mask.reshape(lines[2:]).transpose(1, 0, 2).reshape(-1, LANES)
     halo = shape(3, dims.layers, HALO, *dims.tile)
+    rates = shape(2, dims.layers, HALO, *dims.tile)
     field = shape(*dims.field())
     padded = [pltpu.VMEM((3, dims.layers + 2, dims.rows) + dims.tile, F32)]
     assert dims.depth == GROUPS
@@ -688,9 +652,9 @@
     def exchange(values, step):
         return lax.ppermute(values, "depth", [(i, i ^ step) for i in range(dims.depth)])
 
-    def finish(first, start, stop, closing, halos, fields, heff, extra, outs, *rest):
-        kernel = functools.partial(finish_kernel, dims, first, start, stop, closing)
-        return call(kernel, outs, (*halos, fields, maskf, heff, coefs, blocks, values, *extra), *rest)
+    def second_rate(rows, position, halos, extra, outs, *rest):
+        kernel = functools.partial(second_rate_kernel, dims, rows, position)
+        return call(kernel, outs, (*halos, middle, maskf, heff, values, base, *extra), *rest)
 
     seed = jnp.full(dims.tile, noise_stream[0] * HASH_B + counter[0] * HASH_C, jnp.int32)
     inputs = (
@@ -742,7 +706,7 @@
         (trail, blocks, values),
     )
     links, *bounds = call(
-        functools.partial(first_bound_kernel, dims),
+        functools.partial(bound_kernel, dims, True),
         [shape(GROUPS, LINKS, *dims.tile), edges, edges],
         (sent, mate, cross, other),
     )
@@ -752,44 +716,27 @@
         (tiles, solved, maskf, values, seed),
         padded,
     )
-    inner = dims.rows // 2
-    part = shape(3, dims.layers, dims.rows - inner, *dims.tile)
     (heff,) = call(
         functools.partial(absorb_kernel, dims), [field], (heff, *bounds, coefs, values)
     )
-    *near_half, near, ends = finish(
-        True,
-        inner,
-        dims.rows,
-        False,
-        [near_halo],
-        tiles,
-        heff,
-        (),
-        [part, part, part, halo, shape(PARTS, dims.rows - inner, *dims.tile)],
-    )
-    near_halo = beside(near)
-    middle, base, solved, far, own, *sent = finish(
-        True,
-        0,
-        inner,
-        True,
-        [far_halo],
-        tiles,
-        heff,
-        (links, *near_half, ends),
-        [field, field, field, halo, shape(3 * dims.rows, *dims.tile)]
-        + [shape((3 + len(beside_part(k))) * dims.rows, *dims.tile) for k in range(1, GROUPS)],
-    )
-    far_halo = across(far)
-    others = [
-        lax.ppermute(values, "depth", [(i, (i + k) % GROUPS) for i in range(GROUPS)])
-        for k, values in enumerate(sent, 1)
-    ]
+    middle, base, solved, far, near, sent = call(
+        functools.partial(first_rate_kernel, dims),
+        [field, field, field, rates, rates, shape(message, *dims.tile)],
+        (far_halo, near_halo, tiles, maskf, heff, coefs, blocks, values),
+    )
+    mate = exchange(sent, 1)
+    near_halos = [near_halo, beside(near)]
+    far_halos = [far_halo, across(far)]
+    (cross,) = call(
+        functools.partial(cross_kernel, dims),
+        [shape(6 * dims.rows, *dims.tile)],
+        (sent, mate, links),
+    )
+    other = exchange(cross, 2)
     bounds = call(
-        functools.partial(bound_kernel, dims),
+        functools.partial(bound_kernel, dims, False),
         [edges, edges],
-        (links, own, *others),
+        (sent, mate, cross, other, links),
     )
     (heff,) = call(
         functools.partial(local_kernel, dims, False),
@@ -798,31 +745,25 @@
         padded,
     )
     lined = shape(*view.shape)
-    staging = [pltpu.VMEM(view.shape, F32), pltpu.SemaphoreType.DMA((1,))]
-    heff, accum = call(
+    staging = [pltpu.VMEM(view.shape, F32), pltpu.SemaphoreType.DMA((2,))]
+    heff, accum_lines = call(
         functools.partial(absorb_kernel, dims),
         [field, lined],
         (heff, *bounds, coefs, values, solved),
+    )
+    inner = dims.rows // 2
+    part = shape(3, dims.layers, inner, *dims.tile)
+    upper_rows, lower_rows = range(inner, dims.rows), range(inner)
+    (near_result,) = second_rate(upper_rows, dims.rows - 1, near_halos, (), [part])
+    result, accum = second_rate(
+        lower_rows,
+        0,
+        far_halos,
+        (near_result, accum_lines),
+        [lined, lined],
         staging,
         None,
-        [vmem(), hbm()],
-    )
-    (near_result,) = finish(
-        False, inner, dims.rows, False, [near_halo], middle, heff, (base,), [part]
-    )
-    (result,) = finish(
-        False,
-        0,
-        inner,
-        True,
-        [far_halo],
-        middle,
-        heff,
-        (base, near_result),
-        [lined],
-        staging,
-        None,
-        [hbm()],
+        [hbm(), hbm()],
     )
 
     def whole(lines_view):

time: 29.8 us -> 27.7 us (0.930)
  starting transfers between devices: 17.2 us -> 15.2 us
  Pallas kernels: 7.47 us -> 7 us
  waiting for transfers between devices: 2.87 us -> 3.22 us
    ppermute x3 -> x0, starting transfers between devices: 3.24 us -> none  [local(): lax.ppermute(values, 'depth', [(i, (i + k) % GROUPS) for i in range(GROUP...]
    ppermute x3 -> x0, waiting for transfers between devices: 2.03 us -> none  [local(): lax.ppermute(values, 'depth', [(i, (i + k) % GROUPS) for i in range(GROUP...]
    ppermute x2 -> x4, waiting for transfers between devices: 0.83 us -> 2.85 us  [exchange(): lax.ppermute(values, 'depth', [(i, i ^ step) for i in range(dims.depth)])]
    ppermute x2 -> x4, starting transfers between devices: 2.08 us -> 3.71 us  [exchange(): lax.ppermute(values, 'depth', [(i, i ^ step) for i in range(dims.depth)])]
    pallas_call x14, Pallas kernels: 7.47 us -> 7 us  [call(): pl.pallas_call(kernel, out_shape=outs, in_specs=ins or [vmem()] * len(arg...]
    ppermute x2, waiting for transfers between devices: 0.01 us -> 0.36 us  [across(): return lax.ppermute(values, 'plane', pairs)]
    ppermute x2, starting transfers between devices: 4.74 us -> 4.42 us  [beside(): lax.ppermute(values, 'plane', [(i, i ^ 1) for i in range(dims.plane)])]
  transfers between devices with their start and end apart: 9 -> 8, of which waited for: 2 -> 3; matrix products, arithmetic and copies ran while one was open for 0% -> 0% of each run, Pallas kernels for 17% -> 14%
where the time goes in v5:
time: 27.7 us; the launch traced here: 27.5 us
  starting transfers between devices  15.2 us (55%)
  Pallas kernels  7 us (25%)
  waiting for transfers between devices  3.22 us (12%)
  between operations  2.05 us (7%)
    ppermute x2, starting transfers between devices, across(): return lax.ppermute(values, 'plane', pairs)  7.09 us
    pallas_call x14, Pallas kernels, call(): pl.pallas_call(kernel, out_shape=outs, in_specs=ins or [vmem()] * len(arg...  7 us
    ppermute x2, starting transfers between devices, beside(): lax.ppermute(values, 'plane', [(i, i ^ 1) for i in range(dims.plane)])  4.42 us
    ppermute x4, starting transfers between devices, exchange(): lax.ppermute(values, 'depth', [(i, i ^ step) for i in range(dims.depth)])  3.71 us
    ppermute x4, waiting for transfers between devices, exchange(): lax.ppermute(values, 'depth', [(i, i ^ step) for i in range(dims.depth)])  2.85 us
  transfers between devices with their start and end apart: 8, of which 3 were waited for; matrix products, arithmetic and copies ran while one was open for 0% of the time, Pallas kernels for 14%

profile of v5, /device:TPU:0, one launch (start us, length us, event | category | flops | bytes accessed | tf_op | source)
XLA Modules:
  0.0 27.5 jit_solution(10935971698599999552)
XLA Ops:
  0.6 1.4 %shard_map.140 = (f32[3,8,4,8,128]{4,3,2,1,0:T(8,128)S(1)}, f32[4,8,128]{2,1,0:T(8,128)S(1)}, f32[3,8,2,8,128]{4,3,2,1,0:T(8,128)S(1)}, f32[8,27,8,128]{3,2,1,0:T(8,128)S(1)}, f32[8,6,8,128]{3,2,1,0:T(8,128)S(1)}) custom-call(f32[768,128]{1,0:T(8,128)} %bitcast.24, s32[32,128]{1,0:T(8,128)} %bitcast.25, s32[8]{0:T(128)} %refs_2_.1, f32[4]{0:T(128)} %refs_3_.1, ...), custom_call_target="tpu_custom_call" | custom-call | flops 1000000 | bytes 1000000 | tf_op jit(solution)/shard_map/pallas_call | solution.py:597
  2.0 0.3 %shard_map.141 = (f32[3,8,4,8,128]{4,3,2,1,0:T(8,128)S(1)}, f32[3,8,1,8,128]{4,3,2,1,0:T(8,128)S(1)}, f32[54,8,128]{2,1,0:T(8,128)S(1)}, f32[3,8,2,8,128]{4,3,2,1,0:T(8,128)S(1)}) custom-call(f32[3,8,4,8,128]{4,3,2,1,0:T(8,128)S(1)} %get-tuple-element.28.field.refs_0_.refs_2_, f32[4,8,128]{2,1,0:T(8,128)S(1)} %get-tuple-element.29.maskf.refs_2_.refs_3_, ...), custom_call_target="tpu_custom_call" | custom-call | flops 1000000 | bytes 1000000 | tf_op jit(solution)/shard_map/pallas_call | solution.py:597
  2.4 0.5 %collective-permute-start.2 = (f32[54,8,128]{2,1,0:T(8,128)S(1)}, f32[54,8,128]{2,1,0:T(8,128)S(1)}, u32[]{:S(2)}, u32[]{:S(2)}) collective-permute-start(f32[54,8,128]{2,1,0:T(8,128)S(1)} %get-tuple-element.36.own), channel_id=1, source_target_pairs={{0,8},{8,0},{16,24},{24,16},{1,9},{9,1},{17,25},{25,17},{2,10},{10... | collective-permute-start | bytes 663560 | tf_op jit(solution)/shard_map/ppermute | solution.py:653
  2.9 2.6 %collective-permute-start.1 = (f32[3,8,2,8,128]{4,3,2,1,0:T(8,128)S(1)}, f32[3,8,2,8,128]{4,3,2,1,0:T(8,128)S(1)}, u32[]{:S(2)}, u32[]{:S(2)}) collective-permute-start(f32[3,8,2,8,128]{4,3,2,1,0:T(8,128)S(1)} %get-tuple-element.33), channel_id=1, source_target_pairs={{0,1},{1,0},{2,3},{3,2},{4,5},{5,4},{6,7},{7,6},{8,9},{9,8},{10,11... | collective-permute-start | bytes 589832 | tf_op jit(solution)/shard_map/ppermute | solution.py:650
  5.5 3.5 %collective-permute-start = (f32[3,8,2,8,128]{4,3,2,1,0:T(8,128)S(1)}, f32[3,8,2,8,128]{4,3,2,1,0:T(8,128)S(1)}, u32[]{:S(2)}, u32[]{:S(2)}) collective-permute-start(f32[3,8,2,8,128]{4,3,2,1,0:T(8,128)S(1)} %get-tuple-element.32), channel_id=1, source_target_pairs={{0,7},{1,2},{2,1},{3,4},{4,3},{5,6},{6,5},{7,0},{8,15},{9,10},{10,... | collective-permute-start | bytes 589832 | tf_op jit(solution)/shard_map/ppermute | solution.py:647
  9.0 0.0 collective-permute-done.2.mate
  9.0 0.1 shard_map.143.cross
  9.1 1.6 %collective-permute-start.3 = (f32[30,8,128]{2,1,0:T(8,128)S(1)}, f32[30,8,128]{2,1,0:T(8,128)S(1)}, u32[]{:S(2)}, u32[]{:S(2)}) collective-permute-start(f32[30,8,128]{2,1,0:T(8,128)S(1)} %shard_map.143.cross), channel_id=1, source_target_pairs={{0,16},{8,24},{16,0},{24,8},{1,17},{9,25},{17,1},{25,9},{2,18},{10... | collective-permute-start | bytes 368648 | tf_op jit(solution)/shard_map/ppermute | solution.py:653
  12.0 0.4 %shard_map.145.coefs.refs_5_ = f32[8,36,8,128]{3,2,1,0:T(8,128)S(1)} custom-call(f32[3,8,1,8,128]{4,3,2,1,0:T(8,128)S(1)} %get-tuple-element.39.trail, f32[8,27,8,128]{3,2,1,0:T(8,128)S(1)} %get-tuple-element.30.blocks.refs_6_, f32[8,6,8,128]{3,2,1,0:T(8,128)S(1)} %get-tuple-element.31.values.refs_3_.refs_7_), custom_call_target="tpu_custom_call" | custom-call | flops 1000000 | bytes 1000000 | tf_op jit(solution)/shard_map/pallas_call | solution.py:597
  12.4 1.1 %shard_map.142 = (f32[3,8,4,8,128]{4,3,2,1,0:T(8,128)S(1)}, f32[3,8,4,8,128]{4,3,2,1,0:T(8,128)S(1)}) custom-call(f32[3,8,4,8,128]{4,3,2,1,0:T(8,128)S(1)} %get-tuple-element.28.field.refs_0_.refs_2_, f32[3,8,4,8,128]{4,3,2,1,0:T(8,128)S(1)} %get-tuple-element.34.refs_1_, f32[4,8,128]{2,1,0:T(8,128)S(1)} %get-tuple-element.29.maskf.refs_2_.refs_3_, ...), custom_call_target="tpu_custom_call" | custom-call | flops 1000000 | bytes 1000000 | tf_op jit(solution)/shard_map/pallas_call | solution.py:597
  13.5 0.8 %collective-permute-done.3.other = f32[30,8,128]{2,1,0:T(8,128)S(1)} collective-permute-done((f32[30,8,128]{2,1,0:T(8,128)S(1)}, f32[30,8,128]{2,1,0:T(8,128)S(1)}, u32[]{:S(2)}, u32[]{:S(2)}) %collective-permute-start.3) | collective-permute-done | bytes 122912 | tf_op jit(solution)/shard_map/ppermute | solution.py:653
  14.3 0.2 shard_map.144
  14.6 0.2 shard_map.146.refs_4_
  14.8 0.0 collective-permute-done.1.refs_1_.start_halo
  14.8 0.4 %collective-permute-done.refs_0_.start_halo = f32[3,8,2,8,128]{4,3,2,1,0:T(8,128)S(1)} collective-permute-done((f32[3,8,2,8,128]{4,3,2,1,0:T(8,128)S(1)}, f32[3,8,2,8,128]{4,3,2,1,0:T(8,128)S(1)}, u32[]{:S(2)}, u32[]{:S(2)}) %collective-permute-start) | collective-permute-done | bytes 196640 | tf_op jit(solution)/shard_map/ppermute | solution.py:647
  15.2 0.6 %shard_map.147 = (f32[3,8,4,8,128]{4,3,2,1,0:T(8,128)S(1)}, f32[3,8,4,8,128]{4,3,2,1,0:T(8,128)S(1)}, f32[3,8,4,8,128]{4,3,2,1,0:T(8,128)S(1)}, f32[2,8,2,8,128]...) custom-call(f32[3,8,2,8,128]{4,3,2,1,0:T(8,128)S(1)} %collective-permute-done.refs_0_.start_halo, ...), custom_call_target="tpu_custom_call" | custom-call | flops 1000000 | bytes 1000000 | tf_op jit(solution)/shard_map/pallas_call | solution.py:597
  15.8 0.1 collective-permute-start.5
  15.9 1.8 %collective-permute-start.7 = (f32[2,8,2,8,128]{4,3,2,1,0:T(8,128)S(1)}, f32[2,8,2,8,128]{4,3,2,1,0:T(8,128)S(1)}, u32[]{:S(2)}, u32[]{:S(2)}) collective-permute-start(f32[2,8,2,8,128]{4,3,2,1,0:T(8,128)S(1)} %get-tuple-element.50), channel_id=1, source_target_pairs={{0,1},{1,0},{2,3},{3,2},{4,5},{5,4},{6,7},{7,6},{8,9},{9,8},{10,11... | collective-permute-start | bytes 393224 | tf_op jit(solution)/shard_map/ppermute | solution.py:650
  17.7 3.5 %collective-permute-start.4 = (f32[2,8,2,8,128]{4,3,2,1,0:T(8,128)S(1)}, f32[2,8,2,8,128]{4,3,2,1,0:T(8,128)S(1)}, u32[]{:S(2)}, u32[]{:S(2)}) collective-permute-start(f32[2,8,2,8,128]{4,3,2,1,0:T(8,128)S(1)} %get-tuple-element.40), channel_id=1, source_target_pairs={{0,7},{1,2},{2,1},{3,4},{4,3},{5,6},{6,5},{7,0},{8,15},{9,10},{10,... | collective-permute-start | bytes 393224 | tf_op jit(solution)/shard_map/ppermute | solution.py:647
  21.2 0.0 collective-permute-done.5.mate
  21.3 1.6 %collective-permute-start.6 = (f32[24,8,128]{2,1,0:T(8,128)S(1)}, f32[24,8,128]{2,1,0:T(8,128)S(1)}, u32[]{:S(2)}, u32[]{:S(2)}) collective-permute-start(f32[24,8,128]{2,1,0:T(8,128)S(1)} %shard_map.149.cross), channel_id=1, source_target_pairs={{0,16},{8,24},{16,0},{24,8},{1,17},{9,25},{17,1},{25,9},{2,18},{10... | collective-permute-start | bytes 294920 | tf_op jit(solution)/shard_map/ppermute | solution.py:653
  22.8 1.1 %shard_map.148.heff = f32[3,8,4,8,128]{4,3,2,1,0:T(8,128)S(1)} custom-call(f32[3,8,4,8,128]{4,3,2,1,0:T(8,128)S(1)} %get-tuple-element.41.refs_0_.field, f32[3,8,4,8,128]{4,3,2,1,0:T(8,128)S(1)} %get-tuple-element.42.refs_1_.refs_0_, f32[4,8,128]{2,1,0:T(8,128)S(1)} %get-tuple-element.29.maskf.refs_2_.refs_3_, ...), custom_call_target="tpu_custom_call" | custom-call | flops 1000000 | bytes 1000000 | tf_op jit(solution)/shard_map/pallas_call | solution.py:597
  23.9 2.0 %collective-permute-done.6.other = f32[24,8,128]{2,1,0:T(8,128)S(1)} collective-permute-done((f32[24,8,128]{2,1,0:T(8,128)S(1)}, f32[24,8,128]{2,1,0:T(8,128)S(1)}, u32[]{:S(2)}, u32[]{:S(2)}) %collective-permute-start.6) | collective-permute-done | bytes 98336 | tf_op jit(solution)/shard_map/ppermute | solution.py:653
  25.9 0.1 shard_map.150
  26.0 0.3 shard_map.151
  26.3 0.0 collective-permute-done.7.change_halo
  26.3 0.3 shard_map.152.refs_0_
  26.6 0.0 collective-permute-done.4.change_halo
  26.6 0.9 %shard_map.153 = (f32[768,128]{1,0:T(8,128)}, f32[768,128]{1,0:T(8,128)}) custom-call(f32[3,8,2,8,128]{4,3,2,1,0:T(8,128)S(1)} %collective-permute-done.refs_0_.start_halo, f32[2,8,2,8,128]{4,3,2,1,0:T(8,128)S(1)} %collective-permute-done.4.change_halo, f32[3,8,4,8,128]{4,3,2,1,0:T(8,128)S(1)} %get-tuple-element.41.refs_0_.field, ...), custom_call_target="tpu_custom_call" | custom-call | flops 1000000 | bytes 1000000 | tf_op jit(solution)/shard_map/pallas_call | solution.py:597
  (2 shorter events, 0.0 us)
Async XLA Ops:
  2.4 6.7 %collective-permute-start.2 = (f32[54,8,128]{2,1,0:T(8,128)S(1)}, f32[54,8,128]{2,1,0:T(8,128)S(1)}, u32[]{:S(2)}, u32[]{:S(2)}) collective-permute-start(f32[54,8,128]{2,1,0:T(8,128)S(1)} %get-tuple-element.36.own), channel_id=1, source_target_pairs={{0,8},{8,0},{16,24},{24,16},{1,9},{9,1},{17,25},{25,17},{2,10},{10... | collective-permute-start | bytes 663560 | tf_op jit(solution)/shard_map/ppermute | solution.py:653
  2.9 11.9 %collective-permute-start.1 = (f32[3,8,2,8,128]{4,3,2,1,0:T(8,128)S(1)}, f32[3,8,2,8,128]{4,3,2,1,0:T(8,128)S(1)}, u32[]{:S(2)}, u32[]{:S(2)}) collective-permute-start(f32[3,8,2,8,128]{4,3,2,1,0:T(8,128)S(1)} %get-tuple-element.33), channel_id=1, source_target_pairs={{0,1},{1,0},{2,3},{3,2},{4,5},{5,4},{6,7},{7,6},{8,9},{9,8},{10,11... | collective-permute-start | bytes 589832 | tf_op jit(solution)/shard_map/ppermute | solution.py:650
  5.5 9.7 %collective-permute-start = (f32[3,8,2,8,128]{4,3,2,1,0:T(8,128)S(1)}, f32[3,8,2,8,128]{4,3,2,1,0:T(8,128)S(1)}, u32[]{:S(2)}, u32[]{:S(2)}) collective-permute-start(f32[3,8,2,8,128]{4,3,2,1,0:T(8,128)S(1)} %get-tuple-element.32), channel_id=1, source_target_pairs={{0,7},{1,2},{2,1},{3,4},{4,3},{5,6},{6,5},{7,0},{8,15},{9,10},{10,... | collective-permute-start | bytes 589832 | tf_op jit(solution)/shard_map/ppermute | solution.py:647
  9.1 5.2 %collective-permute-start.3 = (f32[30,8,128]{2,1,0:T(8,128)S(1)}, f32[30,8,128]{2,1,0:T(8,128)S(1)}, u32[]{:S(2)}, u32[]{:S(2)}) collective-permute-start(f32[30,8,128]{2,1,0:T(8,128)S(1)} %shard_map.143.cross), channel_id=1, source_target_pairs={{0,16},{8,24},{16,0},{24,8},{1,17},{9,25},{17,1},{25,9},{2,18},{10... | collective-permute-start | bytes 368648 | tf_op jit(solution)/shard_map/ppermute | solution.py:653
  15.8 5.5 %collective-permute-start.5 = (f32[48,8,128]{2,1,0:T(8,128)S(1)}, f32[48,8,128]{2,1,0:T(8,128)S(1)}, u32[]{:S(2)}, u32[]{:S(2)}) collective-permute-start(f32[48,8,128]{2,1,0:T(8,128)S(1)} %get-tuple-element.44.own), channel_id=1, source_target_pairs={{0,8},{8,0},{16,24},{24,16},{1,9},{9,1},{17,25},{25,17},{2,10},{10... | collective-permute-start | bytes 589832 | tf_op jit(solution)/shard_map/ppermute | solution.py:653
  15.9 10.4 %collective-permute-start.7 = (f32[2,8,2,8,128]{4,3,2,1,0:T(8,128)S(1)}, f32[2,8,2,8,128]{4,3,2,1,0:T(8,128)S(1)}, u32[]{:S(2)}, u32[]{:S(2)}) collective-permute-start(f32[2,8,2,8,128]{4,3,2,1,0:T(8,128)S(1)} %get-tuple-element.50), channel_id=1, source_target_pairs={{0,1},{1,0},{2,3},{3,2},{4,5},{5,4},{6,7},{7,6},{8,9},{9,8},{10,11... | collective-permute-start | bytes 393224 | tf_op jit(solution)/shard_map/ppermute | solution.py:650
  17.7 8.9 %collective-permute-start.4 = (f32[2,8,2,8,128]{4,3,2,1,0:T(8,128)S(1)}, f32[2,8,2,8,128]{4,3,2,1,0:T(8,128)S(1)}, u32[]{:S(2)}, u32[]{:S(2)}) collective-permute-start(f32[2,8,2,8,128]{4,3,2,1,0:T(8,128)S(1)} %get-tuple-element.40), channel_id=1, source_target_pairs={{0,7},{1,2},{2,1},{3,4},{4,3},{5,6},{6,5},{7,0},{8,15},{9,10},{10,... | collective-permute-start | bytes 393224 | tf_op jit(solution)/shard_map/ppermute | solution.py:647
  21.3 4.7 %collective-permute-start.6 = (f32[24,8,128]{2,1,0:T(8,128)S(1)}, f32[24,8,128]{2,1,0:T(8,128)S(1)}, u32[]{:S(2)}, u32[]{:S(2)}) collective-permute-start(f32[24,8,128]{2,1,0:T(8,128)S(1)} %shard_map.149.cross), channel_id=1, source_target_pairs={{0,16},{8,24},{16,0},{24,8},{1,17},{9,25},{17,1},{25,9},{2,18},{10... | collective-permute-start | bytes 294920 | tf_op jit(solution)/shard_map/ppermute | solution.py:653

commit v6 on v5

--- a/solution.py
+++ b/solution.py
@@ -12,7 +12,7 @@
 FAR = -1.0 / 12.0
 HALO = 2
 VMEM_LIMIT = 16 * 1024 * 1024
-UNROLL = 4
+UNROLL = 8
 F32 = jnp.float32
 
 
@@ -143,29 +143,21 @@
     ]
     for copy in copies:
         copy.start()
-    for copy in copies:
-        copy.wait()
+    return copies
 
 
 def enter_kernel(dims, *refs):
     inputs, refs = refs[:11], refs[11:]
     field, maskf, near, blocks, values, *held, sems = refs
-    fetch(inputs, held, sems)
+    copies = fetch(inputs, held, sems)
     magnet, mask, materials, stiffness, anisotropy, damping, source, thermal, *matrices = held
     group = lax.axis_index("depth")
     rows = range(dims.rows)
     lines = [turned(dims, r) for r in rows]
-    for r in rows:
-        maskf[r] = mask[pl.ds(lines[r], dims.chunks, stride=dims.rows), :].astype(F32)
-
-    def layer(l, carry):
-        for r in rows:
-            mask_row = maskf[r]
-            for c in range(3):
-                v = magnet[cells(dims, c, l, lines[r]), :]
-                field[c, l, r] = v
-                if r >= dims.rows - HALO:
-                    near[c, l, dims.rows - 1 - r] = v * mask_row
+    for copy in copies[2:]:
+        copy.wait()
+
+    def coefficients(l, carry):
         at = group * dims.layers + l
         material = materials[l]
         for k, ref in enumerate(matrices):
@@ -180,6 +172,21 @@
             values[l, k] = jnp.full(dims.tile, ref[material], F32)
         return carry
 
+    def layer(l, carry):
+        for r in rows:
+            mask_row = maskf[r]
+            for c in range(3):
+                v = magnet[cells(dims, c, l, lines[r]), :]
+                field[c, l, r] = v
+                if r >= dims.rows - HALO:
+                    near[c, l, dims.rows - 1 - r] = v * mask_row
+        return carry
+
+    loop(dims.layers, coefficients, 0)
+    for copy in copies[:2]:
+        copy.wait()
+    for r in rows:
+        maskf[r] = mask[pl.ds(lines[r], dims.chunks, stride=dims.rows), :].astype(F32)
     loop(dims.layers, layer, 0)
 
 
@@ -244,10 +251,6 @@
         @pl.when(group == g)
         def _():
             body(g)
-
-
-def getter(dims, ref):
-    return lambda part, r: [ref[(part + c) * dims.rows + r] for c in range(3)]
 
 
 def getter(dims, ref):
@@ -354,25 +357,36 @@
     for_each_group(body)
 
 
-def absorb_kernel(dims, heff, bound, edge, coefs, values, *refs):
-    if len(refs) == 1:
-        (out,) = refs
-    else:
-        local, out, accum = refs
-
+def others_part(dims, l, r, bound, edge, coefs, values):
+    stiff = values[l, STIFF]
+    down = jnp.where(l == 0, 0.5, 0.0) * stiff
+    up = jnp.where(l == dims.layers - 1, 0.5, 0.0) * stiff
+    y = [bound[c, r] for c in range(3)]
+    s = [bound[3 + c, r] for c in range(3)]
+    fix = add(matvec(table(coefs, l, FROM_Y), y), matvec(table(coefs, l, FROM_S), s))
+    field = [0.5 * fix[c] + down * edge[c, r] + up * edge[3 + c, r] for c in range(3)]
+    return fix, field
+
+
+def absorb_kernel(dims, heff, bound, edge, coefs, values, out):
     def body(l, carry):
-        stiff = values[l, STIFF]
-        down = jnp.where(l == 0, 0.5, 0.0) * stiff
-        up = jnp.where(l == dims.layers - 1, 0.5, 0.0) * stiff
         for r in range(dims.rows):
-            y = [bound[c, r] for c in range(3)]
-            s = [bound[3 + c, r] for c in range(3)]
-            fix = add(matvec(table(coefs, l, FROM_Y), y), matvec(table(coefs, l, FROM_S), s))
-            for c in range(3):
-                sides = down * edge[c, r] + up * edge[3 + c, r]
-                out[c, l, r] = heff[c, l, r] + 0.5 * fix[c] + sides
-                if len(refs) > 1:
-                    accum[cells(dims, c, l, turned(dims, r)), :] = local[c, l, r] + fix[c]
+            _, more = others_part(dims, l, r, bound, edge, coefs, values)
+            for c in range(3):
+                out[c, l, r] = heff[c, l, r] + more[c]
+        return carry
+
+    loop(dims.layers, body, 0)
+
+
+def halo_kernel(dims, rows, position, start_halo, change_halo, heff, values, out):
+    def body(l, carry):
+        lines = middle_halo(l, start_halo, change_halo)
+        for r in rows:
+            h = [heff[c, l, r] for c in range(3)]
+            h = add_halos(h, l, r, [(position, lines)], values)
+            for c in range(3):
+                out[c, l, r - rows[0]] = h[c]
         return carry
 
     loop(dims.layers, body, 0)
@@ -506,15 +520,18 @@
     return [[halo[c, l, k] for c in range(3)] for k in range(HALO)]
 
 
-def rate(dims, l, r, halos, field, maskf, heff, values):
+def add_halos(h, l, r, halos, values):
     stiff = values[l, STIFF]
-    v = [field[c, l, r] for c in range(3)]
-    h = [heff[c, l, r] for c in range(3)]
     for step, weight in ((1, NEAR), (2, FAR)):
         for position, halo in halos:
             beyond = step - 1 - abs(r - position)
             if beyond >= 0:
                 h = [h[c] + (stiff * weight) * halo[beyond][c] for c in range(3)]
+    return h
+
+
+def rate(l, r, h, field, maskf, values):
+    v = [field[c, l, r] for c in range(3)]
     torque = cross(v, h)
     twice = cross(v, torque)
     gain = values[l, SCALE] * maskf[r]
@@ -530,7 +547,8 @@
         halos = [(0, first_halo(l, far_halo)), (dims.rows - 1, first_halo(l, near_halo))]
         done = []
         for r in rows:
-            v, change = rate(dims, l, r, halos, field, maskf, heff, values)
+            h = add_halos([heff[c, l, r] for c in range(3)], l, r, halos, values)
+            v, change = rate(l, r, h, field, maskf, values)
             m1 = unit([v[c] - 0.03 * change[c] for c in range(3)])
             for c in range(3):
                 middle[c, l, r] = m1[c]
@@ -559,38 +577,34 @@
             message[p * dims.rows + r] = sent[p]
 
 
-def second_rate_kernel(
-    dims, rows, position, start_halo, change_halo, field, maskf, heff, values, base, *refs
-):
-    if len(refs) == 1:
-        (out,) = refs
-    else:
-        mate, accum, result_out, accum_out, result, sem = refs
-        accum_copy = pltpu.make_async_copy(accum, accum_out, sem.at[1])
-        accum_copy.start()
-        rest = [r for r in range(dims.rows) if r not in rows]
+def last_kernel(dims, *refs):
+    own, mate, cross, other, links, start_halo, change_halo, *refs = refs
+    field, maskf, heff, upper_heff, coefs, values, base, local, *refs = refs
+    result_out, accum_out, bound, edge, result, accum, sem = refs
+    bound_kernel(dims, False, own, mate, cross, other, links, bound, edge)
+    upper = dims.rows // 2
 
     def body(l, carry):
-        halos = [(position, middle_halo(l, start_halo, change_halo))]
-        for r in rows:
-            _, change = rate(dims, l, r, halos, field, maskf, heff, values)
+        halos = [(0, middle_halo(l, start_halo, change_halo))]
+        for r in range(dims.rows):
+            fix, more = others_part(dims, l, r, bound, edge, coefs, values)
+            for c in range(3):
+                accum[cells(dims, c, l, turned(dims, r)), :] = local[c, l, r] + fix[c]
+            if r < upper:
+                h = add_halos([heff[c, l, r] for c in range(3)], l, r, halos, values)
+            else:
+                h = [upper_heff[c, l, r - upper] for c in range(3)]
+            _, change = rate(l, r, add(h, more), field, maskf, values)
             new = unit([base[c, l, r] - 0.015 * change[c] for c in range(3)])
             for c in range(3):
-                if len(refs) == 1:
-                    out[c, l, r - rows[0]] = new[c]
-                else:
-                    result[cells(dims, c, l, turned(dims, r)), :] = new[c]
-        if len(refs) > 1:
-            for c in range(3):
-                for r in rest:
-                    result[cells(dims, c, l, turned(dims, r)), :] = mate[c, l, r - rest[0]]
-            send_lines(dims, l, result, result_out, sem.at[0])
+                result[cells(dims, c, l, turned(dims, r)), :] = new[c]
+        send_lines(dims, l, accum, accum_out, sem.at[1])
+        send_lines(dims, l, result, result_out, sem.at[0])
         return carry
 
     loop(dims.layers, body, 0)
-    if len(refs) > 1:
-        pltpu.make_async_copy(result, result_out, sem.at[0]).wait()
-        accum_copy.wait()
+    pltpu.make_async_copy(result, result_out, sem.at[0]).wait()
+    pltpu.make_async_copy(accum, accum_out, sem.at[1]).wait()
 
 
 def call(kernel, outs, args, scratch=(), ins=None, results=None):
@@ -652,10 +666,6 @@
     def exchange(values, step):
         return lax.ppermute(values, "depth", [(i, i ^ step) for i in range(dims.depth)])
 
-    def second_rate(rows, position, halos, extra, outs, *rest):
-        kernel = functools.partial(second_rate_kernel, dims, rows, position)
-        return call(kernel, outs, (*halos, middle, maskf, heff, values, base, *extra), *rest)
-
     seed = jnp.full(dims.tile, noise_stream[0] * HASH_B + counter[0] * HASH_C, jnp.int32)
     inputs = (
         view,
@@ -733,11 +743,6 @@
         (sent, mate, links),
     )
     other = exchange(cross, 2)
-    bounds = call(
-        functools.partial(bound_kernel, dims, False),
-        [edges, edges],
-        (sent, mate, cross, other, links),
-    )
     (heff,) = call(
         functools.partial(local_kernel, dims, False),
         [field],
@@ -745,23 +750,34 @@
         padded,
     )
     lined = shape(*view.shape)
-    staging = [pltpu.VMEM(view.shape, F32), pltpu.SemaphoreType.DMA((2,))]
-    heff, accum_lines = call(
-        functools.partial(absorb_kernel, dims),
-        [field, lined],
-        (heff, *bounds, coefs, values, solved),
-    )
     inner = dims.rows // 2
-    part = shape(3, dims.layers, inner, *dims.tile)
-    upper_rows, lower_rows = range(inner, dims.rows), range(inner)
-    (near_result,) = second_rate(upper_rows, dims.rows - 1, near_halos, (), [part])
-    result, accum = second_rate(
-        lower_rows,
-        0,
-        far_halos,
-        (near_result, accum_lines),
+    (upper_heff,) = call(
+        functools.partial(halo_kernel, dims, range(inner, dims.rows), dims.rows - 1),
+        [shape(3, dims.layers, dims.rows - inner, *dims.tile)],
+        (*near_halos, heff, values),
+    )
+    result, accum = call(
+        functools.partial(last_kernel, dims),
         [lined, lined],
-        staging,
+        (
+            sent,
+            mate,
+            cross,
+            other,
+            links,
+            *far_halos,
+            middle,
+            maskf,
+            heff,
+            upper_heff,
+            coefs,
+            values,
+            base,
+            solved,
+        ),
+        [pltpu.VMEM(edges.shape, F32)] * 2
+        + [pltpu.VMEM(view.shape, F32)] * 2
+        + [pltpu.SemaphoreType.DMA((2,))],
         None,
         [hbm(), hbm()],
     )

time: 27.7 us -> 27.3 us (0.986)
  Pallas kernels: 7 us -> 6.72 us
    ppermute x4, waiting for transfers between devices: 2.85 us -> 0.9 us  [exchange(): lax.ppermute(values, 'depth', [(i, i ^ step) for i in range(dims.depth)])]
    ppermute x2, waiting for transfers between devices: 0.36 us -> 2.25 us  [across(): return lax.ppermute(values, 'plane', pairs)]
    pallas_call x14 -> x12, Pallas kernels: 7 us -> 6.72 us  [call(): pl.pallas_call(kernel, out_shape=outs, in_specs=ins or [vmem()] * len(arg...]
  transfers between devices with their start and end apart: 8 -> 8, of which waited for: 3 -> 3; matrix products, arithmetic and copies ran while one was open for 0% -> 0% of each run, Pallas kernels for 14% -> 12%
where the time goes in v6:
time: 27.3 us; the launch traced here: 27.1 us
  starting transfers between devices  15.2 us (56%)
  Pallas kernels  6.72 us (25%)
  waiting for transfers between devices  3.15 us (12%)
  between operations  2.03 us (7%)
    ppermute x2, starting transfers between devices, across(): return lax.ppermute(values, 'plane', pairs)  7.09 us
    pallas_call x12, Pallas kernels, call(): pl.pallas_call(kernel, out_shape=outs, in_specs=ins or [vmem()] * len(arg...  6.72 us
    ppermute x2, starting transfers between devices, beside(): lax.ppermute(values, 'plane', [(i, i ^ 1) for i in range(dims.plane)])  4.42 us
    ppermute x4, starting transfers between devices, exchange(): lax.ppermute(values, 'depth', [(i, i ^ step) for i in range(dims.depth)])  3.71 us
    ppermute x2, waiting for transfers between devices, across(): return lax.ppermute(values, 'plane', pairs)  2.25 us
    ppermute x4, waiting for transfers between devices, exchange(): lax.ppermute(values, 'depth', [(i, i ^ step) for i in range(dims.depth)])  0.9 us
  transfers between devices with their start and end apart: 8, of which 3 were waited for; matrix products, arithmetic and copies ran while one was open for 0% of the time, Pallas kernels for 12%

profile of v6, /device:TPU:0, one launch (start us, length us, event | category | flops | bytes accessed | tf_op | source)
XLA Modules:
  0.0 27.1 jit_solution(10804271587431689651)
XLA Ops:
  0.6 1.4 %shard_map.140 = (f32[3,8,4,8,128]{4,3,2,1,0:T(8,128)S(1)}, f32[4,8,128]{2,1,0:T(8,128)S(1)}, f32[3,8,2,8,128]{4,3,2,1,0:T(8,128)S(1)}, f32[8,27,8,128]{3,2,1,0:T(8,128)S(1)}, f32[8,6,8,128]{3,2,1,0:T(8,128)S(1)}) custom-call(f32[768,128]{1,0:T(8,128)} %bitcast.24, s32[32,128]{1,0:T(8,128)} %bitcast.25, s32[8]{0:T(128)} %refs_2_.1, f32[4]{0:T(128)} %refs_3_.1, ...), custom_call_target="tpu_custom_call" | custom-call | flops 1000000 | bytes 1000000 | tf_op jit(solution)/shard_map/pallas_call | solution.py:611
  2.0 0.3 %shard_map.141 = (f32[3,8,4,8,128]{4,3,2,1,0:T(8,128)S(1)}, f32[3,8,1,8,128]{4,3,2,1,0:T(8,128)S(1)}, f32[54,8,128]{2,1,0:T(8,128)S(1)}, f32[3,8,2,8,128]{4,3,2,1,0:T(8,128)S(1)}) custom-call(f32[3,8,4,8,128]{4,3,2,1,0:T(8,128)S(1)} %get-tuple-element.24.field.refs_0_.refs_2_, f32[4,8,128]{2,1,0:T(8,128)S(1)} %get-tuple-element.25.maskf.refs_2_.refs_3_.refs_8_, ...), custom_call_target="tpu_custom_call" | custom-call | flops 1000000 | bytes 1000000 | tf_op jit(solution)/shard_map/pallas_call | solution.py:611
  2.3 0.5 %collective-permute-start.2 = (f32[54,8,128]{2,1,0:T(8,128)S(1)}, f32[54,8,128]{2,1,0:T(8,128)S(1)}, u32[]{:S(2)}, u32[]{:S(2)}) collective-permute-start(f32[54,8,128]{2,1,0:T(8,128)S(1)} %get-tuple-element.32.own), channel_id=1, source_target_pairs={{0,8},{8,0},{16,24},{24,16},{1,9},{9,1},{17,25},{25,17},{2,10},{10... | collective-permute-start | bytes 663560 | tf_op jit(solution)/shard_map/ppermute | solution.py:667
  2.8 2.6 %collective-permute-start.1 = (f32[3,8,2,8,128]{4,3,2,1,0:T(8,128)S(1)}, f32[3,8,2,8,128]{4,3,2,1,0:T(8,128)S(1)}, u32[]{:S(2)}, u32[]{:S(2)}) collective-permute-start(f32[3,8,2,8,128]{4,3,2,1,0:T(8,128)S(1)} %get-tuple-element.29), channel_id=1, source_target_pairs={{0,1},{1,0},{2,3},{3,2},{4,5},{5,4},{6,7},{7,6},{8,9},{9,8},{10,11... | collective-permute-start | bytes 589832 | tf_op jit(solution)/shard_map/ppermute | solution.py:664
  5.4 3.5 %collective-permute-start = (f32[3,8,2,8,128]{4,3,2,1,0:T(8,128)S(1)}, f32[3,8,2,8,128]{4,3,2,1,0:T(8,128)S(1)}, u32[]{:S(2)}, u32[]{:S(2)}) collective-permute-start(f32[3,8,2,8,128]{4,3,2,1,0:T(8,128)S(1)} %get-tuple-element.28), channel_id=1, source_target_pairs={{0,7},{1,2},{2,1},{3,4},{4,3},{5,6},{6,5},{7,0},{8,15},{9,10},{10,... | collective-permute-start | bytes 589832 | tf_op jit(solution)/shard_map/ppermute | solution.py:661
  9.0 0.0 collective-permute-done.2.mate
  9.0 0.1 shard_map.143.cross
  9.1 1.6 %collective-permute-start.3 = (f32[30,8,128]{2,1,0:T(8,128)S(1)}, f32[30,8,128]{2,1,0:T(8,128)S(1)}, u32[]{:S(2)}, u32[]{:S(2)}) collective-permute-start(f32[30,8,128]{2,1,0:T(8,128)S(1)} %shard_map.143.cross), channel_id=1, source_target_pairs={{0,16},{8,24},{16,0},{24,8},{1,17},{9,25},{17,1},{25,9},{2,18},{10... | collective-permute-start | bytes 368648 | tf_op jit(solution)/shard_map/ppermute | solution.py:667
  12.0 0.3 %shard_map.145.coefs.refs_5_.refs_11_ = f32[8,36,8,128]{3,2,1,0:T(8,128)S(1)} custom-call(f32[3,8,1,8,128]{4,3,2,1,0:T(8,128)S(1)} %get-tuple-element.35.trail, f32[8,27,8,128]{3,2,1,0:T(8,128)S(1)} %get-tuple-element.26.blocks.refs_6_, f32[8,6,8,128]{3,2,1,0:T(8,128)S(1)} %get-tuple-element.27.values.refs_3_.refs_7_.refs_12_), custom_call_target="tpu_custom_call" | custom-call | flops 1000000 | bytes 1000000 | tf_op jit(solution)/shard_map/pallas_call | solution.py:611
  12.3 1.1 %shard_map.142 = (f32[3,8,4,8,128]{4,3,2,1,0:T(8,128)S(1)}, f32[3,8,4,8,128]{4,3,2,1,0:T(8,128)S(1)}) custom-call(f32[3,8,4,8,128]{4,3,2,1,0:T(8,128)S(1)} %get-tuple-element.24.field.refs_0_.refs_2_, f32[3,8,4,8,128]{4,3,2,1,0:T(8,128)S(1)} %get-tuple-element.30.refs_1_, f32[4,8,128]{2,1,0:T(8,128)S(1)} %get-tuple-element.25.maskf.refs_2_.refs_3_.refs_8_, ...), custom_call_target="tpu_custom_call" | custom-call | flops 1000000 | bytes 1000000 | tf_op jit(solution)/shard_map/pallas_call | solution.py:611
  13.4 0.9 %collective-permute-done.3.other = f32[30,8,128]{2,1,0:T(8,128)S(1)} collective-permute-done((f32[30,8,128]{2,1,0:T(8,128)S(1)}, f32[30,8,128]{2,1,0:T(8,128)S(1)}, u32[]{:S(2)}, u32[]{:S(2)}) %collective-permute-start.3) | collective-permute-done | bytes 122912 | tf_op jit(solution)/shard_map/ppermute | solution.py:667
  14.3 0.2 shard_map.144
  14.5 0.3 shard_map.146.refs_4_
  14.8 0.0 collective-permute-done.1.refs_1_.start_halo
  14.8 0.4 %collective-permute-done.refs_0_.refs_5_ = f32[3,8,2,8,128]{4,3,2,1,0:T(8,128)S(1)} collective-permute-done((f32[3,8,2,8,128]{4,3,2,1,0:T(8,128)S(1)}, f32[3,8,2,8,128]{4,3,2,1,0:T(8,128)S(1)}, u32[]{:S(2)}, u32[]{:S(2)}) %collective-permute-start) | collective-permute-done | bytes 196640 | tf_op jit(solution)/shard_map/ppermute | solution.py:661
  15.1 0.5 %shard_map.147 = (f32[3,8,4,8,128]{4,3,2,1,0:T(8,128)S(1)}, f32[3,8,4,8,128]{4,3,2,1,0:T(8,128)S(1)}, f32[3,8,4,8,128]{4,3,2,1,0:T(8,128)S(1)}, f32[2,8,2,8,128]...) custom-call(f32[3,8,2,8,128]{4,3,2,1,0:T(8,128)S(1)} %collective-permute-done.refs_0_.refs_5_, ...), custom_call_target="tpu_custom_call" | custom-call | flops 1000000 | bytes 1000000 | tf_op jit(solution)/shard_map/pallas_call | solution.py:611
  15.7 0.1 collective-permute-start.4
  15.8 1.8 %collective-permute-start.7 = (f32[2,8,2,8,128]{4,3,2,1,0:T(8,128)S(1)}, f32[2,8,2,8,128]{4,3,2,1,0:T(8,128)S(1)}, u32[]{:S(2)}, u32[]{:S(2)}) collective-permute-start(f32[2,8,2,8,128]{4,3,2,1,0:T(8,128)S(1)} %get-tuple-element.42), channel_id=1, source_target_pairs={{0,1},{1,0},{2,3},{3,2},{4,5},{5,4},{6,7},{7,6},{8,9},{9,8},{10,11... | collective-permute-start | bytes 393224 | tf_op jit(solution)/shard_map/ppermute | solution.py:664
  17.6 3.5 %collective-permute-start.6 = (f32[2,8,2,8,128]{4,3,2,1,0:T(8,128)S(1)}, f32[2,8,2,8,128]{4,3,2,1,0:T(8,128)S(1)}, u32[]{:S(2)}, u32[]{:S(2)}) collective-permute-start(f32[2,8,2,8,128]{4,3,2,1,0:T(8,128)S(1)} %get-tuple-element.38), channel_id=1, source_target_pairs={{0,7},{1,2},{2,1},{3,4},{4,3},{5,6},{6,5},{7,0},{8,15},{9,10},{10,... | collective-permute-start | bytes 393224 | tf_op jit(solution)/shard_map/ppermute | solution.py:661
  21.1 0.0 collective-permute-done.4.mate.refs_1_
  21.2 1.6 %collective-permute-start.5 = (f32[24,8,128]{2,1,0:T(8,128)S(1)}, f32[24,8,128]{2,1,0:T(8,128)S(1)}, u32[]{:S(2)}, u32[]{:S(2)}) collective-permute-start(f32[24,8,128]{2,1,0:T(8,128)S(1)} %shard_map.148.refs_2_), channel_id=1, source_target_pairs={{0,16},{8,24},{16,0},{24,8},{1,17},{9,25},{17,1},{25,9},{2,18},{10... | collective-permute-start | bytes 294920 | tf_op jit(solution)/shard_map/ppermute | solution.py:667
  22.7 1.1 %shard_map.149.heff.refs_9_ = f32[3,8,4,8,128]{4,3,2,1,0:T(8,128)S(1)} custom-call(f32[3,8,4,8,128]{4,3,2,1,0:T(8,128)S(1)} %get-tuple-element.39.refs_0_.refs_7_, f32[3,8,4,8,128]{4,3,2,1,0:T(8,128)S(1)} %get-tuple-element.40.refs_1_.refs_14_, f32[4,8,128]{2,1,0:T(8,128)S(1)} %get-tuple-element.25.maskf.refs_2_.refs_3_.refs_8_, ...), custom_call_target="tpu_custom_call" | custom-call | flops 1000000 | bytes 1000000 | tf_op jit(solution)/shard_map/pallas_call | solution.py:611
  23.8 0.0 collective-permute-done.7.change_halo
  23.8 0.1 shard_map.150.refs_10_
  24.0 1.9 %collective-permute-done.6.refs_6_ = f32[2,8,2,8,128]{4,3,2,1,0:T(8,128)S(1)} collective-permute-done((f32[2,8,2,8,128]{4,3,2,1,0:T(8,128)S(1)}, f32[2,8,2,8,128]{4,3,2,1,0:T(8,128)S(1)}, u32[]{:S(2)}, u32[]{:S(2)}) %collective-permute-start.6) | collective-permute-done | bytes 131104 | tf_op jit(solution)/shard_map/ppermute | solution.py:661
  25.8 0.0 collective-permute-done.5.refs_3_
  25.8 1.3 %shard_map.151 = (f32[768,128]{1,0:T(8,128)}, f32[768,128]{1,0:T(8,128)}) custom-call(f32[48,8,128]{2,1,0:T(8,128)S(1)} %get-tuple-element.36.own.refs_0_, f32[48,8,128]{2,1,0:T(8,128)S(1)} %collective-permute-done.4.mate.refs_1_, f32[24,8,128]{2,1,0:T(8,128)S(1)} %shard_map.148.refs_2_, f32[24,8,128]{2,1,0:T(8,128)S(1)} %collective-permute-done.5.refs_3_, ...), custom_call_target="tpu_custom_call" | custom-call | flops 1000000 | bytes 1000000 | tf_op jit(solution)/shard_map/pallas_call | solution.py:611
  (2 shorter events, 0.0 us)
Async XLA Ops:
  2.3 6.7 %collective-permute-start.2 = (f32[54,8,128]{2,1,0:T(8,128)S(1)}, f32[54,8,128]{2,1,0:T(8,128)S(1)}, u32[]{:S(2)}, u32[]{:S(2)}) collective-permute-start(f32[54,8,128]{2,1,0:T(8,128)S(1)} %get-tuple-element.32.own), channel_id=1, source_target_pairs={{0,8},{8,0},{16,24},{24,16},{1,9},{9,1},{17,25},{25,17},{2,10},{10... | collective-permute-start | bytes 663560 | tf_op jit(solution)/shard_map/ppermute | solution.py:667
  2.8 11.9 %collective-permute-start.1 = (f32[3,8,2,8,128]{4,3,2,1,0:T(8,128)S(1)}, f32[3,8,2,8,128]{4,3,2,1,0:T(8,128)S(1)}, u32[]{:S(2)}, u32[]{:S(2)}) collective-permute-start(f32[3,8,2,8,128]{4,3,2,1,0:T(8,128)S(1)} %get-tuple-element.29), channel_id=1, source_target_pairs={{0,1},{1,0},{2,3},{3,2},{4,5},{5,4},{6,7},{7,6},{8,9},{9,8},{10,11... | collective-permute-start | bytes 589832 | tf_op jit(solution)/shard_map/ppermute | solution.py:664
  5.4 9.7 %collective-permute-start = (f32[3,8,2,8,128]{4,3,2,1,0:T(8,128)S(1)}, f32[3,8,2,8,128]{4,3,2,1,0:T(8,128)S(1)}, u32[]{:S(2)}, u32[]{:S(2)}) collective-permute-start(f32[3,8,2,8,128]{4,3,2,1,0:T(8,128)S(1)} %get-tuple-element.28), channel_id=1, source_target_pairs={{0,7},{1,2},{2,1},{3,4},{4,3},{5,6},{6,5},{7,0},{8,15},{9,10},{10,... | collective-permute-start | bytes 589832 | tf_op jit(solution)/shard_map/ppermute | solution.py:661
  9.1 5.2 %collective-permute-start.3 = (f32[30,8,128]{2,1,0:T(8,128)S(1)}, f32[30,8,128]{2,1,0:T(8,128)S(1)}, u32[]{:S(2)}, u32[]{:S(2)}) collective-permute-start(f32[30,8,128]{2,1,0:T(8,128)S(1)} %shard_map.143.cross), channel_id=1, source_target_pairs={{0,16},{8,24},{16,0},{24,8},{1,17},{9,25},{17,1},{25,9},{2,18},{10... | collective-permute-start | bytes 368648 | tf_op jit(solution)/shard_map/ppermute | solution.py:667
  15.7 5.5 %collective-permute-start.4 = (f32[48,8,128]{2,1,0:T(8,128)S(1)}, f32[48,8,128]{2,1,0:T(8,128)S(1)}, u32[]{:S(2)}, u32[]{:S(2)}) collective-permute-start(f32[48,8,128]{2,1,0:T(8,128)S(1)} %get-tuple-element.36.own.refs_0_), channel_id=1, source_target_pairs={{0,8},{8,0},{16,24},{24,16},{1,9},{9,1},{17,25},{25,17},{2,10},{10... | collective-permute-start | bytes 589832 | tf_op jit(solution)/shard_map/ppermute | solution.py:667
  15.8 8.1 %collective-permute-start.7 = (f32[2,8,2,8,128]{4,3,2,1,0:T(8,128)S(1)}, f32[2,8,2,8,128]{4,3,2,1,0:T(8,128)S(1)}, u32[]{:S(2)}, u32[]{:S(2)}) collective-permute-start(f32[2,8,2,8,128]{4,3,2,1,0:T(8,128)S(1)} %get-tuple-element.42), channel_id=1, source_target_pairs={{0,1},{1,0},{2,3},{3,2},{4,5},{5,4},{6,7},{7,6},{8,9},{9,8},{10,11... | collective-permute-start | bytes 393224 | tf_op jit(solution)/shard_map/ppermute | solution.py:664
  17.6 8.3 %collective-permute-start.6 = (f32[2,8,2,8,128]{4,3,2,1,0:T(8,128)S(1)}, f32[2,8,2,8,128]{4,3,2,1,0:T(8,128)S(1)}, u32[]{:S(2)}, u32[]{:S(2)}) collective-permute-start(f32[2,8,2,8,128]{4,3,2,1,0:T(8,128)S(1)} %get-tuple-element.38), channel_id=1, source_target_pairs={{0,7},{1,2},{2,1},{3,4},{4,3},{5,6},{6,5},{7,0},{8,15},{9,10},{10,... | collective-permute-start | bytes 393224 | tf_op jit(solution)/shard_map/ppermute | solution.py:661
  21.2 4.7 %collective-permute-start.5 = (f32[24,8,128]{2,1,0:T(8,128)S(1)}, f32[24,8,128]{2,1,0:T(8,128)S(1)}, u32[]{:S(2)}, u32[]{:S(2)}) collective-permute-start(f32[24,8,128]{2,1,0:T(8,128)S(1)} %shard_map.148.refs_2_), channel_id=1, source_target_pairs={{0,16},{8,24},{16,0},{24,8},{1,17},{9,25},{17,1},{25,9},{2,18},{10... | collective-permute-start | bytes 294920 | tf_op jit(solution)/shard_map/ppermute | solution.py:667

commit v7 on v6

--- a/solution.py
+++ b/solution.py
@@ -85,7 +85,7 @@
 
 PIVOT, LOWER, UPPER, BLOCK_COEFS = 0, 9, 18, 27
 PIVOT_SOURCE, PIVOT_LOWER, FROM_Y, FROM_S, LAYER_COEFS = 0, 9, 18, 27, 36
-STIFF, ANISO, DAMP, THERMAL, SCALE, SOURCE, LAYER_VALUES = 0, 1, 2, 3, 4, 5, 6
+STIFF, ANISO, DAMP, THERMAL, SCALE, LAYER_VALUES = 0, 1, 2, 3, 4, 5
 LAST, FIRST, TOP, BOTTOM, PARTS = 0, 3, 6, 9, 12
 LAST_Y, FIRST_Y, FIRST_S, LINKS = 0, 9, 18, 27
 SECOND = 8
@@ -141,16 +141,16 @@
         pltpu.make_async_copy(src, dst, sems.at[k])
         for k, (src, dst) in enumerate(zip(inputs, held))
     ]
-    for copy in copies:
+    for copy in reversed(copies):
         copy.start()
     return copies
 
 
 def enter_kernel(dims, *refs):
-    inputs, refs = refs[:11], refs[11:]
-    field, maskf, near, blocks, values, *held, sems = refs
+    inputs, refs = refs[:7], refs[7:]
+    field, maskf, near, blocks, beta, *held, sems = refs
     copies = fetch(inputs, held, sems)
-    magnet, mask, materials, stiffness, anisotropy, damping, source, thermal, *matrices = held
+    magnet, mask, materials, source, *matrices = held
     group = lax.axis_index("depth")
     rows = range(dims.rows)
     lines = [turned(dims, r) for r in rows]
@@ -159,17 +159,11 @@
 
     def coefficients(l, carry):
         at = group * dims.layers + l
-        material = materials[l]
+        beta[l] = jnp.full(dims.tile, source[materials[l]], F32)
         for k, ref in enumerate(matrices):
             for i in range(3):
                 for j in range(3):
                     blocks[l, 9 * k + 3 * i + j] = jnp.full(dims.tile, ref[i, j, at], F32)
-        alpha = jnp.full(dims.tile, damping[material], F32)
-        values[l, DAMP] = alpha
-        values[l, SCALE] = 1.0 / (1.0 + alpha * alpha)
-        rest = ((STIFF, stiffness), (ANISO, anisotropy), (THERMAL, thermal), (SOURCE, source))
-        for k, ref in rest:
-            values[l, k] = jnp.full(dims.tile, ref[material], F32)
         return carry
 
     def layer(l, carry):
@@ -190,11 +184,11 @@
     loop(dims.layers, layer, 0)
 
 
-def sweep_kernel(dims, field, maskf, blocks, values, local, trail, message, far):
+def sweep_kernel(dims, field, maskf, blocks, source, local, trail, message, far):
     rows = range(dims.rows)
 
     def forward(l, prev):
-        beta = values[l, SOURCE]
+        beta = source[l]
         done = []
         for r in [*rows, None]:
             drop = matvec(table(blocks, l, LOWER), prev[len(done)])
@@ -227,10 +221,23 @@
             message[p * dims.rows + r] = sent[p]
 
 
-def coefficient_kernel(dims, trail, blocks, values, coefs):
+def coefficient_kernel(dims, trail, blocks, source, *refs):
+    inputs, (coefs, values, *held, sems) = refs[:5], refs[5:]
+    copies = fetch(inputs, held, sems)
+    materials, stiffness, anisotropy, damping, thermal = held
+
+    def constants(l, carry):
+        material = materials[l]
+        alpha = jnp.full(dims.tile, damping[material], F32)
+        values[l, DAMP] = alpha
+        values[l, SCALE] = 1.0 / (1.0 + alpha * alpha)
+        for k, ref in ((STIFF, stiffness), (ANISO, anisotropy), (THERMAL, thermal)):
+            values[l, k] = jnp.full(dims.tile, ref[material], F32)
+        return carry
+
     def layer(l, carry):
         pivot, low = table(blocks, l, PIVOT), table(blocks, l, LOWER)
-        beta = values[l, SOURCE]
+        beta = source[l]
         for i in range(3):
             for j in range(3):
                 coefs[l, PIVOT_SOURCE + 3 * i + j] = pivot(i, j) * beta
@@ -242,6 +249,9 @@
         return carry
 
     loop(dims.layers, layer, 0)
+    for copy in copies:
+        copy.wait()
+    loop(dims.layers, constants, 0)
 
 
 def for_each_group(body):
@@ -671,26 +681,30 @@
         view,
         mask_view,
         materials,
+        source_strength,
+        pivots.transpose(1, 2, 0),
+        lower.transpose(1, 2, 0),
+        upper.transpose(1, 2, 0),
+    )
+    constants = (
+        materials,
         exchange_strength,
         anisotropy,
         damping,
-        source_strength,
         thermal_strength,
-        pivots.transpose(1, 2, 0),
-        lower.transpose(1, 2, 0),
-        upper.transpose(1, 2, 0),
     )
     inputs = [pltpu.with_memory_space_constraint(x, pltpu.HBM) for x in inputs]
-    spaces = [pltpu.VMEM] * 2 + [pltpu.SMEM] * 9
+    constants = [pltpu.with_memory_space_constraint(x, pltpu.HBM) for x in constants]
+    spaces = [pltpu.VMEM] * 2 + [pltpu.SMEM] * 5
     held = [space(x.shape, x.dtype) for space, x in zip(spaces, inputs)]
-    tiles, maskf, near, blocks, values = call(
+    tiles, maskf, near, blocks, source = call(
         functools.partial(enter_kernel, dims),
         [
             field,
             shape(dims.rows, *dims.tile),
             halo,
             shape(dims.layers, BLOCK_COEFS, *dims.tile),
-            shape(dims.layers, LAYER_VALUES, *dims.tile),
+            shape(dims.layers, *dims.tile),
         ],
         inputs,
         held + [pltpu.SemaphoreType.DMA((len(inputs),))],
@@ -700,7 +714,7 @@
     solved, trail, sent, far = call(
         functools.partial(sweep_kernel, dims),
         [field, shape(3, dims.layers, 1, *dims.tile), shape(message + 6, *dims.tile), halo],
-        (tiles, maskf, blocks, values),
+        (tiles, maskf, blocks, source),
     )
     mate = exchange(sent, 1)
     far_halo = across(far)
@@ -710,10 +724,16 @@
         (sent, mate),
     )
     other = exchange(cross, 2)
-    (coefs,) = call(
+    coefs, values = call(
         functools.partial(coefficient_kernel, dims),
-        [shape(dims.layers, LAYER_COEFS, *dims.tile)],
-        (trail, blocks, values),
+        [
+            shape(dims.layers, LAYER_COEFS, *dims.tile),
+            shape(dims.layers, LAYER_VALUES, *dims.tile),
+        ],
+        (trail, blocks, source, *constants),
+        [pltpu.SMEM(x.shape, x.dtype) for x in constants]
+        + [pltpu.SemaphoreType.DMA((len(constants),))],
+        [vmem()] * 3 + [hbm()] * len(constants),
     )
     links, *bounds = call(
         functools.partial(bound_kernel, dims, True),

time: 27.3 us -> 27.1 us (level)
  waiting for transfers between devices: 3.15 us -> 2.66 us
  Pallas kernels: 6.72 us -> 7.01 us
    ppermute x4, waiting for transfers between devices: 0.9 us -> 0.4 us  [exchange(): lax.ppermute(values, 'depth', [(i, i ^ step) for i in range(dims.depth)])]
    pallas_call x12, Pallas kernels: 6.72 us -> 7.01 us  [call(): pl.pallas_call(kernel, out_shape=outs, in_specs=ins or [vmem()] * len(arg...]
  transfers between devices with their start and end apart: 8 -> 8, of which waited for: 3 -> 3; matrix products, arithmetic and copies ran while one was open for 0% -> 0% of each run, Pallas kernels for 12% -> 14%
where the time goes in v7:
time: 27.1 us; the launch traced here: 26.9 us
  starting transfers between devices  15.2 us (56%)
  Pallas kernels  7.01 us (26%)
  waiting for transfers between devices  2.66 us (10%)
  between operations  2.04 us (8%)
    ppermute x2, starting transfers between devices, across(): return lax.ppermute(values, 'plane', pairs)  7.09 us
    pallas_call x12, Pallas kernels, call(): pl.pallas_call(kernel, out_shape=outs, in_specs=ins or [vmem()] * len(arg...  7.01 us
    ppermute x2, starting transfers between devices, beside(): lax.ppermute(values, 'plane', [(i, i ^ 1) for i in range(dims.plane)])  4.42 us
    ppermute x4, starting transfers between devices, exchange(): lax.ppermute(values, 'depth', [(i, i ^ step) for i in range(dims.depth)])  3.71 us
    ppermute x2, waiting for transfers between devices, across(): return lax.ppermute(values, 'plane', pairs)  2.26 us
  transfers between devices with their start and end apart: 8, of which 3 were waited for; matrix products, arithmetic and copies ran while one was open for 0% of the time, Pallas kernels for 14%

profile of v7, /device:TPU:0, one launch (start us, length us, event | category | flops | bytes accessed | tf_op | source)
XLA Modules:
  0.0 26.9 jit_solution(14000323840873612931)
XLA Ops:
  0.6 1.2 %shard_map.140 = (f32[3,8,4,8,128]{4,3,2,1,0:T(8,128)S(1)}, f32[4,8,128]{2,1,0:T(8,128)S(1)}, f32[3,8,2,8,128]{4,3,2,1,0:T(8,128)S(1)}, f32[8,27,8,128]{3,2,1,0:T(8,128)S(1)}, f32[8,8,128]{2,1,0:T(8,128)S(1)}) custom-call(f32[768,128]{1,0:T(8,128)} %bitcast.24, s32[32,128]{1,0:T(8,128)} %bitcast.25, s32[8]{0:T(128)} %refs_0_.1, f32[4]{0:T(128)} %refs_3_.2, ...), custom_call_target="tpu_custom_call" | custom-call | flops 1000000 | bytes 1000000 | tf_op jit(solution)/shard_map/pallas_call | solution.py:621
  1.8 0.3 %shard_map.141 = (f32[3,8,4,8,128]{4,3,2,1,0:T(8,128)S(1)}, f32[3,8,1,8,128]{4,3,2,1,0:T(8,128)S(1)}, f32[54,8,128]{2,1,0:T(8,128)S(1)}, f32[3,8,2,8,128]{4,3,2,1,0:T(8,128)S(1)}) custom-call(f32[3,8,4,8,128]{4,3,2,1,0:T(8,128)S(1)} %get-tuple-element.26.field.refs_0_.refs_2_, f32[4,8,128]{2,1,0:T(8,128)S(1)} %get-tuple-element.27.maskf.refs_2_.refs_3_.refs_8_, ...), custom_call_target="tpu_custom_call" | custom-call | flops 1000000 | bytes 1000000 | tf_op jit(solution)/shard_map/pallas_call | solution.py:621
  2.1 0.5 %collective-permute-start.2 = (f32[54,8,128]{2,1,0:T(8,128)S(1)}, f32[54,8,128]{2,1,0:T(8,128)S(1)}, u32[]{:S(2)}, u32[]{:S(2)}) collective-permute-start(f32[54,8,128]{2,1,0:T(8,128)S(1)} %get-tuple-element.36.own), channel_id=1, source_target_pairs={{0,8},{8,0},{16,24},{24,16},{1,9},{9,1},{17,25},{25,17},{2,10},{10... | collective-permute-start | bytes 663560 | tf_op jit(solution)/shard_map/ppermute | solution.py:677
  2.7 2.6 %collective-permute-start.1 = (f32[3,8,2,8,128]{4,3,2,1,0:T(8,128)S(1)}, f32[3,8,2,8,128]{4,3,2,1,0:T(8,128)S(1)}, u32[]{:S(2)}, u32[]{:S(2)}) collective-permute-start(f32[3,8,2,8,128]{4,3,2,1,0:T(8,128)S(1)} %get-tuple-element.31), channel_id=1, source_target_pairs={{0,1},{1,0},{2,3},{3,2},{4,5},{5,4},{6,7},{7,6},{8,9},{9,8},{10,11... | collective-permute-start | bytes 589832 | tf_op jit(solution)/shard_map/ppermute | solution.py:674
  5.2 3.5 %collective-permute-start = (f32[3,8,2,8,128]{4,3,2,1,0:T(8,128)S(1)}, f32[3,8,2,8,128]{4,3,2,1,0:T(8,128)S(1)}, u32[]{:S(2)}, u32[]{:S(2)}) collective-permute-start(f32[3,8,2,8,128]{4,3,2,1,0:T(8,128)S(1)} %get-tuple-element.30), channel_id=1, source_target_pairs={{0,7},{1,2},{2,1},{3,4},{4,3},{5,6},{6,5},{7,0},{8,15},{9,10},{10,... | collective-permute-start | bytes 589832 | tf_op jit(solution)/shard_map/ppermute | solution.py:671
  8.8 0.0 collective-permute-done.2.mate
  8.8 0.1 shard_map.144.cross
  8.9 1.6 %collective-permute-start.3 = (f32[30,8,128]{2,1,0:T(8,128)S(1)}, f32[30,8,128]{2,1,0:T(8,128)S(1)}, u32[]{:S(2)}, u32[]{:S(2)}) collective-permute-start(f32[30,8,128]{2,1,0:T(8,128)S(1)} %shard_map.144.cross), channel_id=1, source_target_pairs={{0,16},{8,24},{16,0},{24,8},{1,17},{9,25},{17,1},{25,9},{2,18},{10... | collective-permute-start | bytes 368648 | tf_op jit(solution)/shard_map/ppermute | solution.py:677
  11.8 0.8 %shard_map.142 = (f32[8,36,8,128]{3,2,1,0:T(8,128)S(1)}, f32[8,5,8,128]{3,2,1,0:T(8,128)S(1)}) custom-call(f32[3,8,1,8,128]{4,3,2,1,0:T(8,128)S(1)} %get-tuple-element.33.trail, f32[8,27,8,128]{3,2,1,0:T(8,128)S(1)} %get-tuple-element.28.blocks.refs_6_, f32[8,8,128]{2,1,0:T(8,128)S(1)} %get-tuple-element.29.source, s32[8]{0:T(128)} %refs_0_.1, f32[4]{0:T(128)} %refs_1_.1, ...), custom_call_target="tpu_custom_call" | custom-call | flops 1000000 | bytes 1000000 | tf_op jit(solution)/shard_map/pallas_call | solution.py:621
  12.6 1.1 %shard_map.143 = (f32[3,8,4,8,128]{4,3,2,1,0:T(8,128)S(1)}, f32[3,8,4,8,128]{4,3,2,1,0:T(8,128)S(1)}) custom-call(f32[3,8,4,8,128]{4,3,2,1,0:T(8,128)S(1)} %get-tuple-element.26.field.refs_0_.refs_2_, f32[3,8,4,8,128]{4,3,2,1,0:T(8,128)S(1)} %get-tuple-element.32.refs_1_, f32[4,8,128]{2,1,0:T(8,128)S(1)} %get-tuple-element.27.maskf.refs_2_.refs_3_.refs_8_, ...), custom_call_target="tpu_custom_call" | custom-call | flops 1000000 | bytes 1000000 | tf_op jit(solution)/shard_map/pallas_call | solution.py:621
  13.7 0.4 %collective-permute-done.3.other = f32[30,8,128]{2,1,0:T(8,128)S(1)} collective-permute-done((f32[30,8,128]{2,1,0:T(8,128)S(1)}, f32[30,8,128]{2,1,0:T(8,128)S(1)}, u32[]{:S(2)}, u32[]{:S(2)}) %collective-permute-start.3) | collective-permute-done | bytes 122912 | tf_op jit(solution)/shard_map/ppermute | solution.py:677
  14.1 0.2 shard_map.145
  14.3 0.2 shard_map.146.refs_4_
  14.6 0.0 collective-permute-done.1.refs_1_.start_halo
  14.6 0.4 %collective-permute-done.refs_0_.refs_5_ = f32[3,8,2,8,128]{4,3,2,1,0:T(8,128)S(1)} collective-permute-done((f32[3,8,2,8,128]{4,3,2,1,0:T(8,128)S(1)}, f32[3,8,2,8,128]{4,3,2,1,0:T(8,128)S(1)}, u32[]{:S(2)}, u32[]{:S(2)}) %collective-permute-start) | collective-permute-done | bytes 196640 | tf_op jit(solution)/shard_map/ppermute | solution.py:671
  15.0 0.5 %shard_map.147 = (f32[3,8,4,8,128]{4,3,2,1,0:T(8,128)S(1)}, f32[3,8,4,8,128]{4,3,2,1,0:T(8,128)S(1)}, f32[3,8,4,8,128]{4,3,2,1,0:T(8,128)S(1)}, f32[2,8,2,8,128]...) custom-call(f32[3,8,2,8,128]{4,3,2,1,0:T(8,128)S(1)} %collective-permute-done.refs_0_.refs_5_, ...), custom_call_target="tpu_custom_call" | custom-call | flops 1000000 | bytes 1000000 | tf_op jit(solution)/shard_map/pallas_call | solution.py:621
  15.5 0.1 collective-permute-start.4
  15.6 1.8 %collective-permute-start.7 = (f32[2,8,2,8,128]{4,3,2,1,0:T(8,128)S(1)}, f32[2,8,2,8,128]{4,3,2,1,0:T(8,128)S(1)}, u32[]{:S(2)}, u32[]{:S(2)}) collective-permute-start(f32[2,8,2,8,128]{4,3,2,1,0:T(8,128)S(1)} %get-tuple-element.46), channel_id=1, source_target_pairs={{0,1},{1,0},{2,3},{3,2},{4,5},{5,4},{6,7},{7,6},{8,9},{9,8},{10,11... | collective-permute-start | bytes 393224 | tf_op jit(solution)/shard_map/ppermute | solution.py:674
  17.4 3.5 %collective-permute-start.6 = (f32[2,8,2,8,128]{4,3,2,1,0:T(8,128)S(1)}, f32[2,8,2,8,128]{4,3,2,1,0:T(8,128)S(1)}, u32[]{:S(2)}, u32[]{:S(2)}) collective-permute-start(f32[2,8,2,8,128]{4,3,2,1,0:T(8,128)S(1)} %get-tuple-element.42), channel_id=1, source_target_pairs={{0,7},{1,2},{2,1},{3,4},{4,3},{5,6},{6,5},{7,0},{8,15},{9,10},{10,... | collective-permute-start | bytes 393224 | tf_op jit(solution)/shard_map/ppermute | solution.py:671
  20.9 0.0 collective-permute-done.4.mate.refs_1_
  21.0 1.6 %collective-permute-start.5 = (f32[24,8,128]{2,1,0:T(8,128)S(1)}, f32[24,8,128]{2,1,0:T(8,128)S(1)}, u32[]{:S(2)}, u32[]{:S(2)}) collective-permute-start(f32[24,8,128]{2,1,0:T(8,128)S(1)} %shard_map.148.refs_2_), channel_id=1, source_target_pairs={{0,16},{8,24},{16,0},{24,8},{1,17},{9,25},{17,1},{25,9},{2,18},{10... | collective-permute-start | bytes 294920 | tf_op jit(solution)/shard_map/ppermute | solution.py:677
  22.5 1.1 %shard_map.149.heff.refs_9_ = f32[3,8,4,8,128]{4,3,2,1,0:T(8,128)S(1)} custom-call(f32[3,8,4,8,128]{4,3,2,1,0:T(8,128)S(1)} %get-tuple-element.43.refs_0_.refs_7_, f32[3,8,4,8,128]{4,3,2,1,0:T(8,128)S(1)} %get-tuple-element.44.refs_1_.refs_14_, f32[4,8,128]{2,1,0:T(8,128)S(1)} %get-tuple-element.27.maskf.refs_2_.refs_3_.refs_8_, ...), custom_call_target="tpu_custom_call" | custom-call | flops 1000000 | bytes 1000000 | tf_op jit(solution)/shard_map/pallas_call | solution.py:621
  23.6 0.0 collective-permute-done.7.change_halo
  23.6 0.1 shard_map.150.refs_10_
  23.8 1.9 %collective-permute-done.6.refs_6_ = f32[2,8,2,8,128]{4,3,2,1,0:T(8,128)S(1)} collective-permute-done((f32[2,8,2,8,128]{4,3,2,1,0:T(8,128)S(1)}, f32[2,8,2,8,128]{4,3,2,1,0:T(8,128)S(1)}, u32[]{:S(2)}, u32[]{:S(2)}) %collective-permute-start.6) | collective-permute-done | bytes 131104 | tf_op jit(solution)/shard_map/ppermute | solution.py:671
  25.6 0.0 collective-permute-done.5.refs_3_
  25.7 1.3 %shard_map.151 = (f32[768,128]{1,0:T(8,128)}, f32[768,128]{1,0:T(8,128)}) custom-call(f32[48,8,128]{2,1,0:T(8,128)S(1)} %get-tuple-element.40.own.refs_0_, f32[48,8,128]{2,1,0:T(8,128)S(1)} %collective-permute-done.4.mate.refs_1_, f32[24,8,128]{2,1,0:T(8,128)S(1)} %shard_map.148.refs_2_, f32[24,8,128]{2,1,0:T(8,128)S(1)} %collective-permute-done.5.refs_3_, ...), custom_call_target="tpu_custom_call" | custom-call | flops 1000000 | bytes 1000000 | tf_op jit(solution)/shard_map/pallas_call | solution.py:621
  (2 shorter events, 0.0 us)
Async XLA Ops:
  2.1 6.7 %collective-permute-start.2 = (f32[54,8,128]{2,1,0:T(8,128)S(1)}, f32[54,8,128]{2,1,0:T(8,128)S(1)}, u32[]{:S(2)}, u32[]{:S(2)}) collective-permute-start(f32[54,8,128]{2,1,0:T(8,128)S(1)} %get-tuple-element.36.own), channel_id=1, source_target_pairs={{0,8},{8,0},{16,24},{24,16},{1,9},{9,1},{17,25},{25,17},{2,10},{10... | collective-permute-start | bytes 663560 | tf_op jit(solution)/shard_map/ppermute | solution.py:677
  2.7 11.9 %collective-permute-start.1 = (f32[3,8,2,8,128]{4,3,2,1,0:T(8,128)S(1)}, f32[3,8,2,8,128]{4,3,2,1,0:T(8,128)S(1)}, u32[]{:S(2)}, u32[]{:S(2)}) collective-permute-start(f32[3,8,2,8,128]{4,3,2,1,0:T(8,128)S(1)} %get-tuple-element.31), channel_id=1, source_target_pairs={{0,1},{1,0},{2,3},{3,2},{4,5},{5,4},{6,7},{7,6},{8,9},{9,8},{10,11... | collective-permute-start | bytes 589832 | tf_op jit(solution)/shard_map/ppermute | solution.py:674
  5.2 9.7 %collective-permute-start = (f32[3,8,2,8,128]{4,3,2,1,0:T(8,128)S(1)}, f32[3,8,2,8,128]{4,3,2,1,0:T(8,128)S(1)}, u32[]{:S(2)}, u32[]{:S(2)}) collective-permute-start(f32[3,8,2,8,128]{4,3,2,1,0:T(8,128)S(1)} %get-tuple-element.30), channel_id=1, source_target_pairs={{0,7},{1,2},{2,1},{3,4},{4,3},{5,6},{6,5},{7,0},{8,15},{9,10},{10,... | collective-permute-start | bytes 589832 | tf_op jit(solution)/shard_map/ppermute | solution.py:671
  8.9 5.2 %collective-permute-start.3 = (f32[30,8,128]{2,1,0:T(8,128)S(1)}, f32[30,8,128]{2,1,0:T(8,128)S(1)}, u32[]{:S(2)}, u32[]{:S(2)}) collective-permute-start(f32[30,8,128]{2,1,0:T(8,128)S(1)} %shard_map.144.cross), channel_id=1, source_target_pairs={{0,16},{8,24},{16,0},{24,8},{1,17},{9,25},{17,1},{25,9},{2,18},{10... | collective-permute-start | bytes 368648 | tf_op jit(solution)/shard_map/ppermute | solution.py:677
  15.5 5.5 %collective-permute-start.4 = (f32[48,8,128]{2,1,0:T(8,128)S(1)}, f32[48,8,128]{2,1,0:T(8,128)S(1)}, u32[]{:S(2)}, u32[]{:S(2)}) collective-permute-start(f32[48,8,128]{2,1,0:T(8,128)S(1)} %get-tuple-element.40.own.refs_0_), channel_id=1, source_target_pairs={{0,8},{8,0},{16,24},{24,16},{1,9},{9,1},{17,25},{25,17},{2,10},{10... | collective-permute-start | bytes 589832 | tf_op jit(solution)/shard_map/ppermute | solution.py:677
  15.6 8.1 %collective-permute-start.7 = (f32[2,8,2,8,128]{4,3,2,1,0:T(8,128)S(1)}, f32[2,8,2,8,128]{4,3,2,1,0:T(8,128)S(1)}, u32[]{:S(2)}, u32[]{:S(2)}) collective-permute-start(f32[2,8,2,8,128]{4,3,2,1,0:T(8,128)S(1)} %get-tuple-element.46), channel_id=1, source_target_pairs={{0,1},{1,0},{2,3},{3,2},{4,5},{5,4},{6,7},{7,6},{8,9},{9,8},{10,11... | collective-permute-start | bytes 393224 | tf_op jit(solution)/shard_map/ppermute | solution.py:674
  17.4 8.3 %collective-permute-start.6 = (f32[2,8,2,8,128]{4,3,2,1,0:T(8,128)S(1)}, f32[2,8,2,8,128]{4,3,2,1,0:T(8,128)S(1)}, u32[]{:S(2)}, u32[]{:S(2)}) collective-permute-start(f32[2,8,2,8,128]{4,3,2,1,0:T(8,128)S(1)} %get-tuple-element.42), channel_id=1, source_target_pairs={{0,7},{1,2},{2,1},{3,4},{4,3},{5,6},{6,5},{7,0},{8,15},{9,10},{10,... | collective-permute-start | bytes 393224 | tf_op jit(solution)/shard_map/ppermute | solution.py:671
  21.0 4.7 %collective-permute-start.5 = (f32[24,8,128]{2,1,0:T(8,128)S(1)}, f32[24,8,128]{2,1,0:T(8,128)S(1)}, u32[]{:S(2)}, u32[]{:S(2)}) collective-permute-start(f32[24,8,128]{2,1,0:T(8,128)S(1)} %shard_map.148.refs_2_), channel_id=1, source_target_pairs={{0,16},{8,24},{16,0},{24,8},{1,17},{9,25},{17,1},{25,9},{2,18},{10... | collective-permute-start | bytes 294920 | tf_op jit(solution)/shard_map/ppermute | solution.py:677

commit v8 on v7

--- a/solution.py
+++ b/solution.py
@@ -148,7 +148,7 @@
 
 def enter_kernel(dims, *refs):
     inputs, refs = refs[:7], refs[7:]
-    field, maskf, near, blocks, beta, *held, sems = refs
+    field, maskf, near, blocks, beta, local, trail, message, *held, sems = refs
     copies = fetch(inputs, held, sems)
     magnet, mask, materials, source, *matrices = held
     group = lax.axis_index("depth")
@@ -166,50 +166,38 @@
                     blocks[l, 9 * k + 3 * i + j] = jnp.full(dims.tile, ref[i, j, at], F32)
         return carry
 
-    def layer(l, carry):
-        for r in rows:
-            mask_row = maskf[r]
-            for c in range(3):
-                v = magnet[cells(dims, c, l, lines[r]), :]
-                field[c, l, r] = v
-                if r >= dims.rows - HALO:
-                    near[c, l, dims.rows - 1 - r] = v * mask_row
-        return carry
+    def forward(l, prev):
+        done = []
+        for r in [*rows, None]:
+            f = [0.0] * 3
+            if r is not None:
+                v = [magnet[cells(dims, c, l, lines[r]), :] for c in range(3)]
+                f = [beta[l] * a for a in v]
+                for c in range(3):
+                    field[c, l, r] = v[c]
+                    if r >= dims.rows - HALO:
+                        near[c, l, dims.rows - 1 - r] = v[c] * maskf[r]
+            drop = matvec(table(blocks, l, LOWER), prev[len(done)])
+            y = matvec(table(blocks, l, PIVOT), [a - b for a, b in zip(f, drop)])
+            for c in range(3):
+                if r is None:
+                    trail[c, l, 0] = y[c]
+                else:
+                    local[c, l, r] = y[c]
+            done.append(y)
+        return done
 
     loop(dims.layers, coefficients, 0)
     for copy in copies[:2]:
         copy.wait()
     for r in rows:
         maskf[r] = mask[pl.ds(lines[r], dims.chunks, stride=dims.rows), :].astype(F32)
-    loop(dims.layers, layer, 0)
-
-
-def sweep_kernel(dims, field, maskf, blocks, source, local, trail, message, far):
-    rows = range(dims.rows)
-
-    def forward(l, prev):
-        beta = source[l]
-        done = []
-        for r in [*rows, None]:
-            drop = matvec(table(blocks, l, LOWER), prev[len(done)])
-            f = [-a for a in drop] if r is None else [beta * field[c, l, r] - drop[c] for c in range(3)]
-            y = matvec(table(blocks, l, PIVOT), f)
-            for c in range(3):
-                if r is None:
-                    trail[c, l, 0] = y[c]
-                else:
-                    local[c, l, r] = y[c]
-                    if r < HALO:
-                        far[c, l, r] = field[c, l, r] * maskf[r]
-            done.append(y)
-        return done
-
     zero = [[jnp.zeros(dims.tile, F32)] * 3 for _ in rows]
     lane = lax.broadcasted_iota(jnp.int32, dims.tile, 1)
     before, after = [[(lane == first + c).astype(F32) for c in range(3)] for first in (0, 3)]
     last = loop(dims.layers, forward, zero + [before])
-    lines = [(local, r) for r in rows] + [(trail, 0)]
-    first = sweep_back(dims, lines, lambda l: table(blocks, l, UPPER), zero + [after])
+    back = [(local, r) for r in rows] + [(trail, 0)]
+    first = sweep_back(dims, back, lambda l: table(blocks, l, UPPER), zero + [after])
     for c in range(3):
         message[PARTS * dims.rows + LAST + c] = last[-1][c]
         message[PARTS * dims.rows + FIRST + c] = first[-1][c]
@@ -273,7 +261,15 @@
 
 
 def cross_kernel(dims, own, mate, *refs):
-    links, out = refs if len(refs) == 2 else (None, refs[0])
+    links = None
+    if len(refs) == 2:
+        links, out = refs
+    else:
+        field, maskf, out, far = refs
+        for l in range(dims.layers):
+            for r in range(HALO):
+                for c in range(3):
+                    far[c, l, r] = field[c, l, r] * maskf[r]
 
     def body(g):
         even, odd = (own, mate) if g % 2 == 0 else (mate, own)
@@ -697,7 +693,7 @@
     constants = [pltpu.with_memory_space_constraint(x, pltpu.HBM) for x in constants]
     spaces = [pltpu.VMEM] * 2 + [pltpu.SMEM] * 5
     held = [space(x.shape, x.dtype) for space, x in zip(spaces, inputs)]
-    tiles, maskf, near, blocks, source = call(
+    tiles, maskf, near, blocks, source, solved, trail, sent = call(
         functools.partial(enter_kernel, dims),
         [
             field,
@@ -705,24 +701,22 @@
             halo,
             shape(dims.layers, BLOCK_COEFS, *dims.tile),
             shape(dims.layers, *dims.tile),
+            field,
+            shape(3, dims.layers, 1, *dims.tile),
+            shape(message + 6, *dims.tile),
         ],
         inputs,
         held + [pltpu.SemaphoreType.DMA((len(inputs),))],
         [hbm()] * len(inputs),
     )
     near_halo = beside(near)
-    solved, trail, sent, far = call(
-        functools.partial(sweep_kernel, dims),
-        [field, shape(3, dims.layers, 1, *dims.tile), shape(message + 6, *dims.tile), halo],
-        (tiles, maskf, blocks, source),
-    )
     mate = exchange(sent, 1)
+    cross, far = call(
+        functools.partial(cross_kernel, dims),
+        [shape(6 * dims.rows + 6, *dims.tile), halo],
+        (sent, mate, tiles, maskf),
+    )
     far_halo = across(far)
-    (cross,) = call(
-        functools.partial(cross_kernel, dims),
-        [shape(6 * dims.rows + 6, *dims.tile)],
-        (sent, mate),
-    )
     other = exchange(cross, 2)
     coefs, values = call(
         functools.partial(coefficient_kernel, dims),

time: 27.1 us -> 27 us (level)
  starting transfers between devices: 15.2 us -> 15.6 us
  waiting for transfers between devices: 2.66 us -> 2.27 us
    ppermute x2, starting transfers between devices: 7.09 us -> 8.04 us  [across(): return lax.ppermute(values, 'plane', pairs)]
    ppermute x2, starting transfers between devices: 4.42 us -> 3.89 us  [beside(): lax.ppermute(values, 'plane', [(i, i ^ 1) for i in range(dims.plane)])]
    ppermute x2, waiting for transfers between devices: 2.26 us -> 1.9 us  [across(): return lax.ppermute(values, 'plane', pairs)]
    pallas_call x12 -> x11, Pallas kernels: 7.01 us -> 6.98 us  [call(): pl.pallas_call(kernel, out_shape=outs, in_specs=ins or [vmem()] * len(arg...]
  transfers between devices with their start and end apart: 8 -> 8, of which waited for: 3 -> 2; matrix products, arithmetic and copies ran while one was open for 0% -> 0% of each run, Pallas kernels for 14% -> 14%
where the time goes in v8:
time: 27 us; the launch traced here: 26.9 us
  starting transfers between devices  15.6 us (58%)
  Pallas kernels  6.98 us (26%)
  waiting for transfers between devices  2.27 us (8%)
  between operations  2.04 us (8%)
    ppermute x2, starting transfers between devices, across(): return lax.ppermute(values, 'plane', pairs)  8.04 us
    pallas_call x11, Pallas kernels, call(): pl.pallas_call(kernel, out_shape=outs, in_specs=ins or [vmem()] * len(arg...  6.98 us
    ppermute x2, starting transfers between devices, beside(): lax.ppermute(values, 'plane', [(i, i ^ 1) for i in range(dims.plane)])  3.89 us
    ppermute x4, starting transfers between devices, exchange(): lax.ppermute(values, 'depth', [(i, i ^ step) for i in range(dims.depth)])  3.65 us
    ppermute x2, waiting for transfers between devices, across(): return lax.ppermute(values, 'plane', pairs)  1.9 us
  transfers between devices with their start and end apart: 8, of which 2 were waited for; matrix products, arithmetic and copies ran while one was open for 0% of the time, Pallas kernels for 14%

profile of v8, /device:TPU:0, one launch (start us, length us, event | category | flops | bytes accessed | tf_op | source)
XLA Modules:
  0.0 26.9 jit_solution(126573817900988566)
XLA Ops:
  0.6 1.4 %shard_map.140 = (f32[3,8,4,8,128]{4,3,2,1,0:T(8,128)S(1)}, f32[4,8,128]{2,1,0:T(8,128)S(1)}, f32[3,8,2,8,128]{4,3,2,1,0:T(8,128)S(1)}, f32[8,27,8,128]{3,2,1,0:...) custom-call(f32[768,128]{1,0:T(8,128)} %bitcast.24, ...), custom_call_target="tpu_custom_call" | custom-call | flops 1000000 | bytes 1000000 | tf_op jit(solution)/shard_map/pallas_call | solution.py:617
  2.1 0.5 %collective-permute-start = (f32[54,8,128]{2,1,0:T(8,128)S(1)}, f32[54,8,128]{2,1,0:T(8,128)S(1)}, u32[]{:S(2)}, u32[]{:S(2)}) collective-permute-start(f32[54,8,128]{2,1,0:T(8,128)S(1)} %get-tuple-element.27.own), channel_id=1, source_target_pairs={{0,8},{8,0},{16,24},{24,16},{1,9},{9,1},{17,25},{25,17},{2,10},{10... | collective-permute-start | bytes 663560 | tf_op jit(solution)/shard_map/ppermute | solution.py:673
  2.6 2.6 %collective-permute-start.2 = (f32[3,8,2,8,128]{4,3,2,1,0:T(8,128)S(1)}, f32[3,8,2,8,128]{4,3,2,1,0:T(8,128)S(1)}, u32[]{:S(2)}, u32[]{:S(2)}) collective-permute-start(f32[3,8,2,8,128]{4,3,2,1,0:T(8,128)S(1)} %get-tuple-element.31), channel_id=1, source_target_pairs={{0,1},{1,0},{2,3},{3,2},{4,5},{5,4},{6,7},{7,6},{8,9},{9,8},{10,11... | collective-permute-start | bytes 589832 | tf_op jit(solution)/shard_map/ppermute | solution.py:670
  5.2 0.0 collective-permute-done.mate
  5.2 0.1 shard_map.141
  5.3 4.5 %collective-permute-start.1 = (f32[3,8,2,8,128]{4,3,2,1,0:T(8,128)S(1)}, f32[3,8,2,8,128]{4,3,2,1,0:T(8,128)S(1)}, u32[]{:S(2)}, u32[]{:S(2)}) collective-permute-start(f32[3,8,2,8,128]{4,3,2,1,0:T(8,128)S(1)} %get-tuple-element.30), channel_id=1, source_target_pairs={{0,7},{1,2},{2,1},{3,4},{4,3},{5,6},{6,5},{7,0},{8,15},{9,10},{10,... | collective-permute-start | bytes 589832 | tf_op jit(solution)/shard_map/ppermute | solution.py:667
  9.8 1.5 %collective-permute-start.3 = (f32[30,8,128]{2,1,0:T(8,128)S(1)}, f32[30,8,128]{2,1,0:T(8,128)S(1)}, u32[]{:S(2)}, u32[]{:S(2)}) collective-permute-start(f32[30,8,128]{2,1,0:T(8,128)S(1)} %get-tuple-element.38.cross), channel_id=1, source_target_pairs={{0,16},{8,24},{16,0},{24,8},{1,17},{9,25},{17,1},{25,9},{2,18},{10... | collective-permute-start | bytes 368648 | tf_op jit(solution)/shard_map/ppermute | solution.py:673
  12.6 0.8 %shard_map.142 = (f32[8,36,8,128]{3,2,1,0:T(8,128)S(1)}, f32[8,5,8,128]{3,2,1,0:T(8,128)S(1)}) custom-call(f32[3,8,1,8,128]{4,3,2,1,0:T(8,128)S(1)} %get-tuple-element.33.trail, f32[8,27,8,128]{3,2,1,0:T(8,128)S(1)} %get-tuple-element.34.blocks.refs_6_, f32[8,8,128]{2,1,0:T(8,128)S(1)} %get-tuple-element.35.source, s32[8]{0:T(128)} %refs_0_.1, f32[4]{0:T(128)} %refs_1_.1, ...), custom_call_target="tpu_custom_call" | custom-call | flops 1000000 | bytes 1000000 | tf_op jit(solution)/shard_map/pallas_call | solution.py:617
  13.4 1.1 %shard_map.143 = (f32[3,8,4,8,128]{4,3,2,1,0:T(8,128)S(1)}, f32[3,8,4,8,128]{4,3,2,1,0:T(8,128)S(1)}) custom-call(f32[3,8,4,8,128]{4,3,2,1,0:T(8,128)S(1)} %get-tuple-element.28.refs_0_.refs_2_, f32[3,8,4,8,128]{4,3,2,1,0:T(8,128)S(1)} %get-tuple-element.32.refs_1_, f32[4,8,128]{2,1,0:T(8,128)S(1)} %get-tuple-element.29.refs_1_.refs_2_.refs_3_.refs_8_, ...), custom_call_target="tpu_custom_call" | custom-call | flops 1000000 | bytes 1000000 | tf_op jit(solution)/shard_map/pallas_call | solution.py:617
  14.5 0.4 %collective-permute-done.3.other = f32[30,8,128]{2,1,0:T(8,128)S(1)} collective-permute-done((f32[30,8,128]{2,1,0:T(8,128)S(1)}, f32[30,8,128]{2,1,0:T(8,128)S(1)}, u32[]{:S(2)}, u32[]{:S(2)}) %collective-permute-start.3) | collective-permute-done | bytes 122912 | tf_op jit(solution)/shard_map/ppermute | solution.py:673
  14.9 0.2 shard_map.144
  15.1 0.3 shard_map.145.refs_4_
  15.4 0.0 collective-permute-done.2.refs_1_.start_halo
  15.4 0.0 collective-permute-done.1.refs_0_.refs_5_
  15.4 0.5 %shard_map.146 = (f32[3,8,4,8,128]{4,3,2,1,0:T(8,128)S(1)}, f32[3,8,4,8,128]{4,3,2,1,0:T(8,128)S(1)}, f32[3,8,4,8,128]{4,3,2,1,0:T(8,128)S(1)}, f32[2,8,2,8,128]...) custom-call(f32[3,8,2,8,128]{4,3,2,1,0:T(8,128)S(1)} %collective-permute-done.1.refs_0_.refs_5_, ...), custom_call_target="tpu_custom_call" | custom-call | flops 1000000 | bytes 1000000 | tf_op jit(solution)/shard_map/pallas_call | solution.py:617
  16.0 0.1 collective-permute-start.4
  16.0 1.3 %collective-permute-start.7 = (f32[2,8,2,8,128]{4,3,2,1,0:T(8,128)S(1)}, f32[2,8,2,8,128]{4,3,2,1,0:T(8,128)S(1)}, u32[]{:S(2)}, u32[]{:S(2)}) collective-permute-start(f32[2,8,2,8,128]{4,3,2,1,0:T(8,128)S(1)} %get-tuple-element.48), channel_id=1, source_target_pairs={{0,1},{1,0},{2,3},{3,2},{4,5},{5,4},{6,7},{7,6},{8,9},{9,8},{10,11... | collective-permute-start | bytes 393224 | tf_op jit(solution)/shard_map/ppermute | solution.py:670
  17.3 3.5 %collective-permute-start.6 = (f32[2,8,2,8,128]{4,3,2,1,0:T(8,128)S(1)}, f32[2,8,2,8,128]{4,3,2,1,0:T(8,128)S(1)}, u32[]{:S(2)}, u32[]{:S(2)}) collective-permute-start(f32[2,8,2,8,128]{4,3,2,1,0:T(8,128)S(1)} %get-tuple-element.44), channel_id=1, source_target_pairs={{0,7},{1,2},{2,1},{3,4},{4,3},{5,6},{6,5},{7,0},{8,15},{9,10},{10,... | collective-permute-start | bytes 393224 | tf_op jit(solution)/shard_map/ppermute | solution.py:667
  20.9 0.0 collective-permute-done.4.mate.refs_1_
  20.9 1.6 %collective-permute-start.5 = (f32[24,8,128]{2,1,0:T(8,128)S(1)}, f32[24,8,128]{2,1,0:T(8,128)S(1)}, u32[]{:S(2)}, u32[]{:S(2)}) collective-permute-start(f32[24,8,128]{2,1,0:T(8,128)S(1)} %shard_map.147.refs_2_), channel_id=1, source_target_pairs={{0,16},{8,24},{16,0},{24,8},{1,17},{9,25},{17,1},{25,9},{2,18},{10... | collective-permute-start | bytes 294920 | tf_op jit(solution)/shard_map/ppermute | solution.py:673
  22.5 1.1 %shard_map.148.heff.refs_9_ = f32[3,8,4,8,128]{4,3,2,1,0:T(8,128)S(1)} custom-call(f32[3,8,4,8,128]{4,3,2,1,0:T(8,128)S(1)} %get-tuple-element.45.refs_0_.refs_7_, f32[3,8,4,8,128]{4,3,2,1,0:T(8,128)S(1)} %get-tuple-element.46.refs_1_.refs_14_, f32[4,8,128]{2,1,0:T(8,128)S(1)} %get-tuple-element.29.refs_1_.refs_2_.refs_3_.refs_8_, ...), custom_call_target="tpu_custom_call" | custom-call | flops 1000000 | bytes 1000000 | tf_op jit(solution)/shard_map/pallas_call | solution.py:617
  23.6 0.0 collective-permute-done.7.change_halo
  23.6 0.1 shard_map.149.refs_10_
  23.7 1.9 %collective-permute-done.6.refs_6_ = f32[2,8,2,8,128]{4,3,2,1,0:T(8,128)S(1)} collective-permute-done((f32[2,8,2,8,128]{4,3,2,1,0:T(8,128)S(1)}, f32[2,8,2,8,128]{4,3,2,1,0:T(8,128)S(1)}, u32[]{:S(2)}, u32[]{:S(2)}) %collective-permute-start.6) | collective-permute-done | bytes 131104 | tf_op jit(solution)/shard_map/ppermute | solution.py:667
  25.6 0.0 collective-permute-done.5.refs_3_
  25.6 1.3 %shard_map.150 = (f32[768,128]{1,0:T(8,128)}, f32[768,128]{1,0:T(8,128)}) custom-call(f32[48,8,128]{2,1,0:T(8,128)S(1)} %get-tuple-element.42.own.refs_0_, f32[48,8,128]{2,1,0:T(8,128)S(1)} %collective-permute-done.4.mate.refs_1_, f32[24,8,128]{2,1,0:T(8,128)S(1)} %shard_map.147.refs_2_, f32[24,8,128]{2,1,0:T(8,128)S(1)} %collective-permute-done.5.refs_3_, ...), custom_call_target="tpu_custom_call" | custom-call | flops 1000000 | bytes 1000000 | tf_op jit(solution)/shard_map/pallas_call | solution.py:617
  (2 shorter events, 0.0 us)
Async XLA Ops:
  2.1 3.1 %collective-permute-start = (f32[54,8,128]{2,1,0:T(8,128)S(1)}, f32[54,8,128]{2,1,0:T(8,128)S(1)}, u32[]{:S(2)}, u32[]{:S(2)}) collective-permute-start(f32[54,8,128]{2,1,0:T(8,128)S(1)} %get-tuple-element.27.own), channel_id=1, source_target_pairs={{0,8},{8,0},{16,24},{24,16},{1,9},{9,1},{17,25},{25,17},{2,10},{10... | collective-permute-start | bytes 663560 | tf_op jit(solution)/shard_map/ppermute | solution.py:673
  2.6 12.8 %collective-permute-start.2 = (f32[3,8,2,8,128]{4,3,2,1,0:T(8,128)S(1)}, f32[3,8,2,8,128]{4,3,2,1,0:T(8,128)S(1)}, u32[]{:S(2)}, u32[]{:S(2)}) collective-permute-start(f32[3,8,2,8,128]{4,3,2,1,0:T(8,128)S(1)} %get-tuple-element.31), channel_id=1, source_target_pairs={{0,1},{1,0},{2,3},{3,2},{4,5},{5,4},{6,7},{7,6},{8,9},{9,8},{10,11... | collective-permute-start | bytes 589832 | tf_op jit(solution)/shard_map/ppermute | solution.py:670
  5.3 10.1 %collective-permute-start.1 = (f32[3,8,2,8,128]{4,3,2,1,0:T(8,128)S(1)}, f32[3,8,2,8,128]{4,3,2,1,0:T(8,128)S(1)}, u32[]{:S(2)}, u32[]{:S(2)}) collective-permute-start(f32[3,8,2,8,128]{4,3,2,1,0:T(8,128)S(1)} %get-tuple-element.30), channel_id=1, source_target_pairs={{0,7},{1,2},{2,1},{3,4},{4,3},{5,6},{6,5},{7,0},{8,15},{9,10},{10,... | collective-permute-start | bytes 589832 | tf_op jit(solution)/shard_map/ppermute | solution.py:667
  9.8 5.1 %collective-permute-start.3 = (f32[30,8,128]{2,1,0:T(8,128)S(1)}, f32[30,8,128]{2,1,0:T(8,128)S(1)}, u32[]{:S(2)}, u32[]{:S(2)}) collective-permute-start(f32[30,8,128]{2,1,0:T(8,128)S(1)} %get-tuple-element.38.cross), channel_id=1, source_target_pairs={{0,16},{8,24},{16,0},{24,8},{1,17},{9,25},{17,1},{25,9},{2,18},{10... | collective-permute-start | bytes 368648 | tf_op jit(solution)/shard_map/ppermute | solution.py:673
  16.0 4.9 %collective-permute-start.4 = (f32[48,8,128]{2,1,0:T(8,128)S(1)}, f32[48,8,128]{2,1,0:T(8,128)S(1)}, u32[]{:S(2)}, u32[]{:S(2)}) collective-permute-start(f32[48,8,128]{2,1,0:T(8,128)S(1)} %get-tuple-element.42.own.refs_0_), channel_id=1, source_target_pairs={{0,8},{8,0},{16,24},{24,16},{1,9},{9,1},{17,25},{25,17},{2,10},{10... | collective-permute-start | bytes 589832 | tf_op jit(solution)/shard_map/ppermute | solution.py:673
  16.0 7.5 %collective-permute-start.7 = (f32[2,8,2,8,128]{4,3,2,1,0:T(8,128)S(1)}, f32[2,8,2,8,128]{4,3,2,1,0:T(8,128)S(1)}, u32[]{:S(2)}, u32[]{:S(2)}) collective-permute-start(f32[2,8,2,8,128]{4,3,2,1,0:T(8,128)S(1)} %get-tuple-element.48), channel_id=1, source_target_pairs={{0,1},{1,0},{2,3},{3,2},{4,5},{5,4},{6,7},{7,6},{8,9},{9,8},{10,11... | collective-permute-start | bytes 393224 | tf_op jit(solution)/shard_map/ppermute | solution.py:670
  17.3 8.3 %collective-permute-start.6 = (f32[2,8,2,8,128]{4,3,2,1,0:T(8,128)S(1)}, f32[2,8,2,8,128]{4,3,2,1,0:T(8,128)S(1)}, u32[]{:S(2)}, u32[]{:S(2)}) collective-permute-start(f32[2,8,2,8,128]{4,3,2,1,0:T(8,128)S(1)} %get-tuple-element.44), channel_id=1, source_target_pairs={{0,7},{1,2},{2,1},{3,4},{4,3},{5,6},{6,5},{7,0},{8,15},{9,10},{10,... | collective-permute-start | bytes 393224 | tf_op jit(solution)/shard_map/ppermute | solution.py:667
  20.9 4.7 %collective-permute-start.5 = (f32[24,8,128]{2,1,0:T(8,128)S(1)}, f32[24,8,128]{2,1,0:T(8,128)S(1)}, u32[]{:S(2)}, u32[]{:S(2)}) collective-permute-start(f32[24,8,128]{2,1,0:T(8,128)S(1)} %shard_map.147.refs_2_), channel_id=1, source_target_pairs={{0,16},{8,24},{16,0},{24,8},{1,17},{9,25},{17,1},{25,9},{2,18},{10... | collective-permute-start | bytes 294920 | tf_op jit(solution)/shard_map/ppermute | solution.py:673

commit v9 on v7

--- a/solution.py
+++ b/solution.py
@@ -428,6 +428,67 @@
     return (mixed & 65535).astype(F32) * (1.0 / 32767.5) - 1.0
 
 
+def others_part(dims, l, r, bound, edge, coefs, values):
+    stiff = values[l, STIFF]
+    down = jnp.where(l == 0, 0.5, 0.0) * stiff
+    up = jnp.where(l == dims.layers - 1, 0.5, 0.0) * stiff
+    y = [bound[c, r] for c in range(3)]
+    s = [bound[3 + c, r] for c in range(3)]
+    fix = add(matvec(table(coefs, l, FROM_Y), y), matvec(table(coefs, l, FROM_S), s))
+    field = [0.5 * fix[c] + down * edge[c, r] + up * edge[3 + c, r] for c in range(3)]
+    return fix, field
+
+
+def absorb_kernel(dims, heff, bound, edge, coefs, values, out):
+    def body(l, carry):
+        for r in range(dims.rows):
+            _, more = others_part(dims, l, r, bound, edge, coefs, values)
+            for c in range(3):
+                out[c, l, r] = heff[c, l, r] + more[c]
+        return carry
+
+    loop(dims.layers, body, 0)
+
+
+def halo_kernel(dims, rows, position, start_halo, change_halo, heff, values, out):
+    def body(l, carry):
+        lines = middle_halo(l, start_halo, change_halo)
+        for r in rows:
+            h = [heff[c, l, r] for c in range(3)]
+            h = add_halos(h, l, r, [(position, lines)], values)
+            for c in range(3):
+                out[c, l, r - rows[0]] = h[c]
+        return carry
+
+    loop(dims.layers, body, 0)
+
+
+def send_lines(dims, layer, src, dst, sem):
+    lines = dims.chunks * dims.rows
+    for c in range(3):
+        where = pl.ds((c * dims.layers + layer) * lines, lines)
+        pltpu.make_async_copy(src.at[where], dst.at[where], sem).start()
+
+
+def shifted_sum(dims, w, lane):
+    after = pltpu.roll(w, dims.chunks - 1, 0)
+    before = pltpu.roll(w, 1, 0)
+    near = pltpu.roll(jnp.where(lane < 1, after, w), LANES - 1, 1)
+    near += pltpu.roll(jnp.where(lane >= LANES - 1, before, w), 1, 1)
+    far = pltpu.roll(jnp.where(lane < 2, after, w), LANES - 2, 1)
+    far += pltpu.roll(jnp.where(lane >= LANES - 2, before, w), 2, 1)
+    return NEAR * near + FAR * far
+
+
+def hash_uniform(mixed):
+    mixed = mixed ^ lax.shift_right_logical(mixed, jnp.int32(16))
+    mixed = mixed * HASH_A
+    mixed = mixed ^ lax.shift_right_logical(mixed, jnp.int32(15))
+    mixed = mixed * HASH_B
+    mixed = mixed ^ lax.shift_right_logical(mixed, jnp.int32(16))
+    return (mixed & 65535).astype(F32) * (1.0 / 32767.5) - 1.0
+
+
 def local_kernel(dims, first, *refs):
     field, solved, maskf, values, *refs = refs
     if first:
@@ -455,7 +516,7 @@
                 masked[c, l + 1, r] = field[c, l, r] * mask_row
         return carry
 
-    lax.fori_loop(0, dims.layers, fill, 0)
+    loop(dims.layers, fill, 0)
 
     def body(l, carry):
         stiff = values[l, STIFF]
@@ -485,7 +546,7 @@
                 heff[c, l, r] = h
         return carry
 
-    lax.fori_loop(0, dims.layers, body, 0)
+    loop(dims.layers, body, 0)
 
 
 def largest(m):

time: 27.1 us -> 27.1 us (level)
  waiting for transfers between devices: 2.66 us -> 3.84 us
  Pallas kernels: 7.01 us -> 5.84 us
    pallas_call x12, Pallas kernels: 7.01 us -> 5.84 us  [call(): pl.pallas_call(kernel, out_shape=outs, in_specs=ins or [vmem()] * len(arg...]
    ppermute x4, waiting for transfers between devices: 0.4 us -> 0.96 us  [exchange(): lax.ppermute(values, 'depth', [(i, i ^ step) for i in range(dims.depth)])]
    ppermute x2, waiting for transfers between devices: 0.01 us -> 0.56 us  [beside(): lax.ppermute(values, 'plane', [(i, i ^ 1) for i in range(dims.plane)])]
  transfers between devices with their start and end apart: 8 -> 8, of which waited for: 3 -> 4; matrix products, arithmetic and copies ran while one was open for 0% -> 0% of each run, Pallas kernels for 14% -> 10%
where the time goes in v9:
time: 27.1 us; the launch traced here: 26.9 us
  starting transfers between devices  15.2 us (56%)
  Pallas kernels  5.84 us (22%)
  waiting for transfers between devices  3.84 us (14%)
  between operations  2.03 us (7%)
    ppermute x2, starting transfers between devices, across(): return lax.ppermute(values, 'plane', pairs)  7.09 us
    pallas_call x12, Pallas kernels, call(): pl.pallas_call(kernel, out_shape=outs, in_specs=ins or [vmem()] * len(arg...  5.84 us
    ppermute x2, starting transfers between devices, beside(): lax.ppermute(values, 'plane', [(i, i ^ 1) for i in range(dims.plane)])  4.42 us
    ppermute x4, starting transfers between devices, exchange(): lax.ppermute(values, 'depth', [(i, i ^ step) for i in range(dims.depth)])  3.71 us
    ppermute x2, waiting for transfers between devices, across(): return lax.ppermute(values, 'plane', pairs)  2.33 us
    ppermute x4, waiting for transfers between devices, exchange(): lax.ppermute(values, 'depth', [(i, i ^ step) for i in range(dims.depth)])  0.96 us
    ppermute x2, waiting for transfers between devices, beside(): lax.ppermute(values, 'plane', [(i, i ^ 1) for i in range(dims.plane)])  0.56 us
  transfers between devices with their start and end apart: 8, of which 4 were waited for; matrix products, arithmetic and copies ran while one was open for 0% of the time, Pallas kernels for 10%

profile of v9, /device:TPU:0, one launch (start us, length us, event | category | flops | bytes accessed | tf_op | source)
XLA Modules:
  0.0 26.9 jit_solution(1035809089413509602)
XLA Ops:
  0.6 1.2 %shard_map.140 = (f32[3,8,4,8,128]{4,3,2,1,0:T(8,128)S(1)}, f32[4,8,128]{2,1,0:T(8,128)S(1)}, f32[3,8,2,8,128]{4,3,2,1,0:T(8,128)S(1)}, f32[8,27,8,128]{3,2,1,0:T(8,128)S(1)}, f32[8,8,128]{2,1,0:T(8,128)S(1)}) custom-call(f32[768,128]{1,0:T(8,128)} %bitcast.24, s32[32,128]{1,0:T(8,128)} %bitcast.25, s32[8]{0:T(128)} %refs_0_.1, f32[4]{0:T(128)} %refs_3_.2, ...), custom_call_target="tpu_custom_call" | custom-call | flops 1000000 | bytes 1000000 | tf_op jit(solution)/shard_map/pallas_call | solution.py:682
  1.8 0.3 %shard_map.141 = (f32[3,8,4,8,128]{4,3,2,1,0:T(8,128)S(1)}, f32[3,8,1,8,128]{4,3,2,1,0:T(8,128)S(1)}, f32[54,8,128]{2,1,0:T(8,128)S(1)}, f32[3,8,2,8,128]{4,3,2,1,0:T(8,128)S(1)}) custom-call(f32[3,8,4,8,128]{4,3,2,1,0:T(8,128)S(1)} %get-tuple-element.26.field.refs_0_.refs_2_, f32[4,8,128]{2,1,0:T(8,128)S(1)} %get-tuple-element.27.maskf.refs_2_.refs_3_.refs_8_, ...), custom_call_target="tpu_custom_call" | custom-call | flops 1000000 | bytes 1000000 | tf_op jit(solution)/shard_map/pallas_call | solution.py:682
  2.1 0.5 %collective-permute-start.2 = (f32[54,8,128]{2,1,0:T(8,128)S(1)}, f32[54,8,128]{2,1,0:T(8,128)S(1)}, u32[]{:S(2)}, u32[]{:S(2)}) collective-permute-start(f32[54,8,128]{2,1,0:T(8,128)S(1)} %get-tuple-element.36.own), channel_id=1, source_target_pairs={{0,8},{8,0},{16,24},{24,16},{1,9},{9,1},{17,25},{25,17},{2,10},{10... | collective-permute-start | bytes 663560 | tf_op jit(solution)/shard_map/ppermute | solution.py:738
  2.7 2.6 %collective-permute-start.1 = (f32[3,8,2,8,128]{4,3,2,1,0:T(8,128)S(1)}, f32[3,8,2,8,128]{4,3,2,1,0:T(8,128)S(1)}, u32[]{:S(2)}, u32[]{:S(2)}) collective-permute-start(f32[3,8,2,8,128]{4,3,2,1,0:T(8,128)S(1)} %get-tuple-element.31), channel_id=1, source_target_pairs={{0,1},{1,0},{2,3},{3,2},{4,5},{5,4},{6,7},{7,6},{8,9},{9,8},{10,11... | collective-permute-start | bytes 589832 | tf_op jit(solution)/shard_map/ppermute | solution.py:735
  5.2 3.5 %collective-permute-start = (f32[3,8,2,8,128]{4,3,2,1,0:T(8,128)S(1)}, f32[3,8,2,8,128]{4,3,2,1,0:T(8,128)S(1)}, u32[]{:S(2)}, u32[]{:S(2)}) collective-permute-start(f32[3,8,2,8,128]{4,3,2,1,0:T(8,128)S(1)} %get-tuple-element.30), channel_id=1, source_target_pairs={{0,7},{1,2},{2,1},{3,4},{4,3},{5,6},{6,5},{7,0},{8,15},{9,10},{10,... | collective-permute-start | bytes 589832 | tf_op jit(solution)/shard_map/ppermute | solution.py:732
  8.8 0.0 collective-permute-done.2.mate
  8.8 0.1 shard_map.144.cross
  8.9 1.6 %collective-permute-start.3 = (f32[30,8,128]{2,1,0:T(8,128)S(1)}, f32[30,8,128]{2,1,0:T(8,128)S(1)}, u32[]{:S(2)}, u32[]{:S(2)}) collective-permute-start(f32[30,8,128]{2,1,0:T(8,128)S(1)} %shard_map.144.cross), channel_id=1, source_target_pairs={{0,16},{8,24},{16,0},{24,8},{1,17},{9,25},{17,1},{25,9},{2,18},{10... | collective-permute-start | bytes 368648 | tf_op jit(solution)/shard_map/ppermute | solution.py:738
  11.8 0.8 %shard_map.142 = (f32[8,36,8,128]{3,2,1,0:T(8,128)S(1)}, f32[8,5,8,128]{3,2,1,0:T(8,128)S(1)}) custom-call(f32[3,8,1,8,128]{4,3,2,1,0:T(8,128)S(1)} %get-tuple-element.33.trail, f32[8,27,8,128]{3,2,1,0:T(8,128)S(1)} %get-tuple-element.28.blocks.refs_6_, f32[8,8,128]{2,1,0:T(8,128)S(1)} %get-tuple-element.29.source, s32[8]{0:T(128)} %refs_0_.1, f32[4]{0:T(128)} %refs_1_.1, ...), custom_call_target="tpu_custom_call" | custom-call | flops 1000000 | bytes 1000000 | tf_op jit(solution)/shard_map/pallas_call | solution.py:682
  12.6 0.5 %shard_map.143 = (f32[3,8,4,8,128]{4,3,2,1,0:T(8,128)S(1)}, f32[3,8,4,8,128]{4,3,2,1,0:T(8,128)S(1)}) custom-call(f32[3,8,4,8,128]{4,3,2,1,0:T(8,128)S(1)} %get-tuple-element.26.field.refs_0_.refs_2_, f32[3,8,4,8,128]{4,3,2,1,0:T(8,128)S(1)} %get-tuple-element.32.refs_1_, f32[4,8,128]{2,1,0:T(8,128)S(1)} %get-tuple-element.27.maskf.refs_2_.refs_3_.refs_8_, ...), custom_call_target="tpu_custom_call" | custom-call | flops 1000000 | bytes 1000000 | tf_op jit(solution)/shard_map/pallas_call | solution.py:682
  13.1 0.9 %collective-permute-done.3.other = f32[30,8,128]{2,1,0:T(8,128)S(1)} collective-permute-done((f32[30,8,128]{2,1,0:T(8,128)S(1)}, f32[30,8,128]{2,1,0:T(8,128)S(1)}, u32[]{:S(2)}, u32[]{:S(2)}) %collective-permute-start.3) | collective-permute-done | bytes 122912 | tf_op jit(solution)/shard_map/ppermute | solution.py:738
  14.1 0.2 shard_map.145
  14.3 0.2 shard_map.146.refs_4_
  14.6 0.0 collective-permute-done.1.refs_1_.start_halo
  14.6 0.4 %collective-permute-done.refs_0_.refs_5_ = f32[3,8,2,8,128]{4,3,2,1,0:T(8,128)S(1)} collective-permute-done((f32[3,8,2,8,128]{4,3,2,1,0:T(8,128)S(1)}, f32[3,8,2,8,128]{4,3,2,1,0:T(8,128)S(1)}, u32[]{:S(2)}, u32[]{:S(2)}) %collective-permute-start) | collective-permute-done | bytes 196640 | tf_op jit(solution)/shard_map/ppermute | solution.py:732
  15.0 0.5 %shard_map.147 = (f32[3,8,4,8,128]{4,3,2,1,0:T(8,128)S(1)}, f32[3,8,4,8,128]{4,3,2,1,0:T(8,128)S(1)}, f32[3,8,4,8,128]{4,3,2,1,0:T(8,128)S(1)}, f32[2,8,2,8,128]...) custom-call(f32[3,8,2,8,128]{4,3,2,1,0:T(8,128)S(1)} %collective-permute-done.refs_0_.refs_5_, ...), custom_call_target="tpu_custom_call" | custom-call | flops 1000000 | bytes 1000000 | tf_op jit(solution)/shard_map/pallas_call | solution.py:682
  15.5 0.1 collective-permute-start.4
  15.6 1.8 %collective-permute-start.7 = (f32[2,8,2,8,128]{4,3,2,1,0:T(8,128)S(1)}, f32[2,8,2,8,128]{4,3,2,1,0:T(8,128)S(1)}, u32[]{:S(2)}, u32[]{:S(2)}) collective-permute-start(f32[2,8,2,8,128]{4,3,2,1,0:T(8,128)S(1)} %get-tuple-element.46), channel_id=1, source_target_pairs={{0,1},{1,0},{2,3},{3,2},{4,5},{5,4},{6,7},{7,6},{8,9},{9,8},{10,11... | collective-permute-start | bytes 393224 | tf_op jit(solution)/shard_map/ppermute | solution.py:735
  17.4 3.5 %collective-permute-start.6 = (f32[2,8,2,8,128]{4,3,2,1,0:T(8,128)S(1)}, f32[2,8,2,8,128]{4,3,2,1,0:T(8,128)S(1)}, u32[]{:S(2)}, u32[]{:S(2)}) collective-permute-start(f32[2,8,2,8,128]{4,3,2,1,0:T(8,128)S(1)} %get-tuple-element.42), channel_id=1, source_target_pairs={{0,7},{1,2},{2,1},{3,4},{4,3},{5,6},{6,5},{7,0},{8,15},{9,10},{10,... | collective-permute-start | bytes 393224 | tf_op jit(solution)/shard_map/ppermute | solution.py:732
  20.9 0.0 collective-permute-done.4.mate.refs_1_
  21.0 1.6 %collective-permute-start.5 = (f32[24,8,128]{2,1,0:T(8,128)S(1)}, f32[24,8,128]{2,1,0:T(8,128)S(1)}, u32[]{:S(2)}, u32[]{:S(2)}) collective-permute-start(f32[24,8,128]{2,1,0:T(8,128)S(1)} %shard_map.148.refs_2_), channel_id=1, source_target_pairs={{0,16},{8,24},{16,0},{24,8},{1,17},{9,25},{17,1},{25,9},{2,18},{10... | collective-permute-start | bytes 294920 | tf_op jit(solution)/shard_map/ppermute | solution.py:738
  22.5 0.5 %shard_map.149.heff.refs_9_ = f32[3,8,4,8,128]{4,3,2,1,0:T(8,128)S(1)} custom-call(f32[3,8,4,8,128]{4,3,2,1,0:T(8,128)S(1)} %get-tuple-element.43.refs_0_.refs_7_, f32[3,8,4,8,128]{4,3,2,1,0:T(8,128)S(1)} %get-tuple-element.44.refs_1_.refs_14_, f32[4,8,128]{2,1,0:T(8,128)S(1)} %get-tuple-element.27.maskf.refs_2_.refs_3_.refs_8_, ...), custom_call_target="tpu_custom_call" | custom-call | flops 1000000 | bytes 1000000 | tf_op jit(solution)/shard_map/pallas_call | solution.py:682
  23.0 0.6 %collective-permute-done.7.change_halo = f32[2,8,2,8,128]{4,3,2,1,0:T(8,128)S(1)} collective-permute-done((f32[2,8,2,8,128]{4,3,2,1,0:T(8,128)S(1)}, f32[2,8,2,8,128]{4,3,2,1,0:T(8,128)S(1)}, u32[]{:S(2)}, u32[]{:S(2)}) %collective-permute-start.7) | collective-permute-done | bytes 131104 | tf_op jit(solution)/shard_map/ppermute | solution.py:735
  23.6 0.1 shard_map.150.refs_10_
  23.7 2.0 %collective-permute-done.6.refs_6_ = f32[2,8,2,8,128]{4,3,2,1,0:T(8,128)S(1)} collective-permute-done((f32[2,8,2,8,128]{4,3,2,1,0:T(8,128)S(1)}, f32[2,8,2,8,128]{4,3,2,1,0:T(8,128)S(1)}, u32[]{:S(2)}, u32[]{:S(2)}) %collective-permute-start.6) | collective-permute-done | bytes 131104 | tf_op jit(solution)/shard_map/ppermute | solution.py:732
  25.6 0.0 collective-permute-done.5.refs_3_
  25.7 1.3 %shard_map.151 = (f32[768,128]{1,0:T(8,128)}, f32[768,128]{1,0:T(8,128)}) custom-call(f32[48,8,128]{2,1,0:T(8,128)S(1)} %get-tuple-element.40.own.refs_0_, f32[48,8,128]{2,1,0:T(8,128)S(1)} %collective-permute-done.4.mate.refs_1_, f32[24,8,128]{2,1,0:T(8,128)S(1)} %shard_map.148.refs_2_, f32[24,8,128]{2,1,0:T(8,128)S(1)} %collective-permute-done.5.refs_3_, ...), custom_call_target="tpu_custom_call" | custom-call | flops 1000000 | bytes 1000000 | tf_op jit(solution)/shard_map/pallas_call | solution.py:682
  (2 shorter events, 0.0 us)
Async XLA Ops:
  2.1 6.7 %collective-permute-start.2 = (f32[54,8,128]{2,1,0:T(8,128)S(1)}, f32[54,8,128]{2,1,0:T(8,128)S(1)}, u32[]{:S(2)}, u32[]{:S(2)}) collective-permute-start(f32[54,8,128]{2,1,0:T(8,128)S(1)} %get-tuple-element.36.own), channel_id=1, source_target_pairs={{0,8},{8,0},{16,24},{24,16},{1,9},{9,1},{17,25},{25,17},{2,10},{10... | collective-permute-start | bytes 663560 | tf_op jit(solution)/shard_map/ppermute | solution.py:738
  2.7 11.9 %collective-permute-start.1 = (f32[3,8,2,8,128]{4,3,2,1,0:T(8,128)S(1)}, f32[3,8,2,8,128]{4,3,2,1,0:T(8,128)S(1)}, u32[]{:S(2)}, u32[]{:S(2)}) collective-permute-start(f32[3,8,2,8,128]{4,3,2,1,0:T(8,128)S(1)} %get-tuple-element.31), channel_id=1, source_target_pairs={{0,1},{1,0},{2,3},{3,2},{4,5},{5,4},{6,7},{7,6},{8,9},{9,8},{10,11... | collective-permute-start | bytes 589832 | tf_op jit(solution)/shard_map/ppermute | solution.py:735
  5.2 9.7 %collective-permute-start = (f32[3,8,2,8,128]{4,3,2,1,0:T(8,128)S(1)}, f32[3,8,2,8,128]{4,3,2,1,0:T(8,128)S(1)}, u32[]{:S(2)}, u32[]{:S(2)}) collective-permute-start(f32[3,8,2,8,128]{4,3,2,1,0:T(8,128)S(1)} %get-tuple-element.30), channel_id=1, source_target_pairs={{0,7},{1,2},{2,1},{3,4},{4,3},{5,6},{6,5},{7,0},{8,15},{9,10},{10,... | collective-permute-start | bytes 589832 | tf_op jit(solution)/shard_map/ppermute | solution.py:732
  8.9 5.2 %collective-permute-start.3 = (f32[30,8,128]{2,1,0:T(8,128)S(1)}, f32[30,8,128]{2,1,0:T(8,128)S(1)}, u32[]{:S(2)}, u32[]{:S(2)}) collective-permute-start(f32[30,8,128]{2,1,0:T(8,128)S(1)} %shard_map.144.cross), channel_id=1, source_target_pairs={{0,16},{8,24},{16,0},{24,8},{1,17},{9,25},{17,1},{25,9},{2,18},{10... | collective-permute-start | bytes 368648 | tf_op jit(solution)/shard_map/ppermute | solution.py:738
  15.5 5.5 %collective-permute-start.4 = (f32[48,8,128]{2,1,0:T(8,128)S(1)}, f32[48,8,128]{2,1,0:T(8,128)S(1)}, u32[]{:S(2)}, u32[]{:S(2)}) collective-permute-start(f32[48,8,128]{2,1,0:T(8,128)S(1)} %get-tuple-element.40.own.refs_0_), channel_id=1, source_target_pairs={{0,8},{8,0},{16,24},{24,16},{1,9},{9,1},{17,25},{25,17},{2,10},{10... | collective-permute-start | bytes 589832 | tf_op jit(solution)/shard_map/ppermute | solution.py:738
  15.6 8.0 %collective-permute-start.7 = (f32[2,8,2,8,128]{4,3,2,1,0:T(8,128)S(1)}, f32[2,8,2,8,128]{4,3,2,1,0:T(8,128)S(1)}, u32[]{:S(2)}, u32[]{:S(2)}) collective-permute-start(f32[2,8,2,8,128]{4,3,2,1,0:T(8,128)S(1)} %get-tuple-element.46), channel_id=1, source_target_pairs={{0,1},{1,0},{2,3},{3,2},{4,5},{5,4},{6,7},{7,6},{8,9},{9,8},{10,11... | collective-permute-start | bytes 393224 | tf_op jit(solution)/shard_map/ppermute | solution.py:735
  17.4 8.3 %collective-permute-start.6 = (f32[2,8,2,8,128]{4,3,2,1,0:T(8,128)S(1)}, f32[2,8,2,8,128]{4,3,2,1,0:T(8,128)S(1)}, u32[]{:S(2)}, u32[]{:S(2)}) collective-permute-start(f32[2,8,2,8,128]{4,3,2,1,0:T(8,128)S(1)} %get-tuple-element.42), channel_id=1, source_target_pairs={{0,7},{1,2},{2,1},{3,4},{4,3},{5,6},{6,5},{7,0},{8,15},{9,10},{10,... | collective-permute-start | bytes 393224 | tf_op jit(solution)/shard_map/ppermute | solution.py:732
  21.0 4.7 %collective-permute-start.5 = (f32[24,8,128]{2,1,0:T(8,128)S(1)}, f32[24,8,128]{2,1,0:T(8,128)S(1)}, u32[]{:S(2)}, u32[]{:S(2)}) collective-permute-start(f32[24,8,128]{2,1,0:T(8,128)S(1)} %shard_map.148.refs_2_), channel_id=1, source_target_pairs={{0,16},{8,24},{16,0},{24,8},{1,17},{9,25},{17,1},{25,9},{2,18},{10... | collective-permute-start | bytes 294920 | tf_op jit(solution)/shard_map/ppermute | solution.py:738
